TPU v7x, 32 devices: a whole 2x2x4 slice. The times are simulated.
32 devices in a mesh: row: 8 (over y, x, core), col: 4 (over z).
Axes of the slice: x: 2, y: 2, z: 4, core: 2. Of those that a mesh axis runs over, the one named last changes fastest.
Arguments:
- panel: float32 [6144, 256], P('row', 'col'), may hold values from -6 to 6
- trailing: float32 [6144, 12032], P('row', 'col'), may hold values from -6 to 6
Outputs:
- projections: float32 [12032, 256], P('col')
- remainder: float32 [6144, 12032], P('row', 'col')
All inputs are finite; a program needn't handle non-finite values.
Results may differ from a plain program's by a relative error of at most 0.000075.
Values sent between devices are 32-bit elements; how exact they have to be, the bound alone decides.
No kernel may reach another device: no remote copies, remote signals or barrier semaphores. Data moves between devices by JAX's collectives and lax.ppermute only.
A program may use at most 64 MiB of HBM per device.

v0:
```python
import jax
import jax.numpy as jnp
from jax import lax
from jax.sharding import PartitionSpec as P


def cross_rows(left, right):
    return lax.dot_general(
        left,
        right,
        (((0,), (0,)), ((), ())),
        precision=lax.Precision.HIGHEST,
        preferred_element_type=jnp.float32,
    )


def solve_right(lower_factor, terms):
    return jax.scipy.linalg.solve_triangular(lower_factor, terms.T, lower=True).T


def per_device(panel, trailing):
    panel_full = lax.all_gather(panel, "col", axis=1, tiled=True)
    panel_gram = lax.psum(cross_rows(panel_full, panel_full), "row")
    lower_factor = jnp.linalg.cholesky(panel_gram)
    orthonormal = solve_right(lower_factor, panel_full)
    cross_terms = lax.psum(cross_rows(trailing, panel_full), "row")
    projections = solve_right(lower_factor, cross_terms)
    update = lax.dot_general(
        orthonormal,
        projections,
        (((1,), (1,)), ((), ())),
        precision=lax.Precision.HIGHEST,
        preferred_element_type=jnp.float32,
    )
    remainder = trailing - update
    return (projections, remainder)


def solution(mesh):
    return jax.shard_map(
        per_device,
        mesh=mesh,
        in_specs=(P("row", "col"), P("row", "col")),
        out_specs=(P("col", None), P("row", "col")),
        check_vma=False,
    )
```

profile of v0, /device:TPU:0, one launch (start us, length us, event | category | flops | bytes accessed | tf_op | source)
XLA Modules:
  0.0 201.4 jit_solution(8789012491266461795)
XLA Ops:
  7.2 0.0 all-reduce.4.cloned.1.call-start
  7.2 21.5 %all_gather.3 = f32[768,256]{0,1:T(8,128)S(1)} all-gather(f32[768,64]{0,1:T(8,128)} %param.2), channel_id=1, replica_groups=mesh['row'=8,'col'=4] {'col'}, dimensions={1}, use_global_device_ids=true | all-gather | bytes 983040 | tf_op jit(solution)/shard_map/all_gather | solution.py:22
  28.7 1.5 fusion.18
  30.2 11.2 %fusion.19 = f32[256,3008]{0,1:T(8,128)} fusion(f32[768,256]{0,1:T(8,128)S(1)} %all_gather.3, f32[768,3008]{0,1:T(8,128)} %param.3), kind=kOutput, calls=%fused_computation.41 | convolution fusion | flops 7096762368 | bytes 13107200 | tf_op jit(solution)/shard_map/dot_general | solution.py:8
  41.4 0.0 all-reduce.4.cloned.1.call-update
  41.5 71.4 %all-reduce.4.cloned.1.call-done = (f32[256,3008]{0,1:T(8,128)}, f32[256,256]{0,1:T(8,128)}) async-done(((f32[256,3008]{0,1:T(8,128)}, f32[256,256]{0,1:T(8,128)}), (f32[256,3008]{0,1:T(8,128)}, f32[256,256]{0,1:T(8,128)})) %all-reduce.4.cloned.1.call-update) | async-done | bytes 3342352 | tf_op jit(solution)/shard_map/psum | solution.py:26
  112.9 1.1 copy.5
  114.0 1.0 fusion.8
  115.0 11.7 %cholesky.50 = f32[128,128]{1,0:T(8,128)S(1)} custom-call(f32[128,128]{1,0:T(8,128)S(1)} %cholesky.118), custom_call_target="Cholesky" | custom-call | tf_op jit(solution)/shard_map/jit(cholesky)/cholesky | solution.py:24
  126.8 9.8 %custom-call.18 = f32[1,128,128]{1,2,0:T(8,128)S(1)} custom-call(f32[1,128,128]{2,1,0:T(8,128)S(1)} %get-tuple-element.25), custom_call_target="InvertDiagBlocksLowerTriangular" | custom-call | tf_op jit(solution)/shard_map/jit(cholesky)/cholesky | solution.py:24
  136.6 0.2 constant_dynamic-update-slice_fusion.1
  136.8 0.3 convolution_subtract_fusion.3
  137.1 11.7 %cholesky.105 = f32[128,128]{1,0:T(8,128)S(1)} custom-call(f32[128,128]{1,0:T(8,128)S(1)} %convolution_subtract_fusion.3), custom_call_target="Cholesky" | custom-call | tf_op jit(solution)/shard_map/jit(cholesky)/cholesky | solution.py:24
  148.8 0.6 compare_reduce_fusion
  150.8 0.0 slice-start
  150.8 0.1 triangular_solve.72
  150.9 4.0 %while.1 = (s32[]{:T(128)}, f32[256,256]{1,0:T(8,128)S(1)}, s32[2,2]{1,0:T(2,128)S(1)}, f32[2,128,128]{2,1,0:T(8,128)S(1)}, s32[]{:T(128)}) while((s32[]{:T(128)}, f32[256,256]{1,0:T(8,128)S(1)}, s32[2,2]{1,0:T(2,128)S(1)}, f32[2,128,128]{2,1,0:T(8,128)S(1)}, s32[]{:T(128)}) %tuple.27), condition=%wide.while_cond, body=%wide.while_body.sunk | while | flops 2 | bytes 131181 | solution.py:18
  150.9 0.6 fusion.31
  151.5 1.4 bitcast_dynamic-update-slice_fusion.2
  152.9 0.6 fusion.31
  153.5 1.4 bitcast_dynamic-update-slice_fusion.2
  154.9 19.9 %custom-call.19 = f32[2,128,128]{1,2,0:T(8,128)S(1)} custom-call(f32[2,128,128]{2,1,0:T(8,128)S(1)} %get-tuple-element.9), custom_call_target="InvertDiagBlocksLowerTriangular" | custom-call | tf_op jit(solution)/shard_map/jit(_solve_triangular)/triangular_solve | solution.py:18
  174.8 0.0 copy-start
  174.8 0.5 fusion.6
  175.3 0.5 convolution_subtract_fusion.2
  175.8 0.5 fusion.12
  176.3 0.0 slice-start.1
  176.4 2.9 %fusion.1 = f32[128,3008]{0,1:T(8,128)S(1)} fusion(f32[256,3008]{0,1:T(8,128)} %get-tuple-element.18, f32[2,128,128]{1,2,0:T(8,128)S(1)} %custom-call.19), kind=kOutput, calls=%fused_computation.6 | convolution fusion | flops 591396864 | bytes 3145728 | tf_op jit(solution)/shard_map/jit(_solve_triangular)/triangular_solve | solution.py:18
  179.3 0.0 copy-done
  179.3 1.4 convolution_subtract_fusion.1
  180.7 0.0 slice-start.2
  180.7 1.4 fusion.13
  182.2 1.8 fusion
  184.0 0.0 slice-done
  184.0 0.0 slice-done.1
  184.0 0.0 slice-done.2
  184.0 10.5 %convolution_subtract_fusion = f32[768,3008]{0,1:T(8,128)} fusion(f32[768,3008]{0,1:T(8,128)S(1)} %bitcast.43, f32[128,3008]{0,1:T(8,128)S(1)} %fusion.13, f32[128,3008]{0,1:T(8,128)S(1)} %fusion.1, f32[128,768]{1,0:T(8,128)S(1)} %fusion.12, f32[128,768]{1,0:T(8,128)S(1)} %fusion.6), kind=kOutput, calls=%fused_computation.2 | convolution fusion | flops 7100039168 | bytes 22347776 | tf_op jit(solution)/shard_map/dot_general | solution.py:28
  (10 shorter events, 0.1 us)
Async XLA Ops:
  7.2 105.8 %all-reduce.4.cloned.1.call-start = ((), (), s32[]{:S(2)}) async-start(), calls=%async_computation | async-start | bytes 6684672 | tf_op jit(solution)/shard_map/psum | solution.py:26
  150.8 33.2 %slice-start = ((s8[9240576]{0:T(1024)(128)(4,1)}), s8[851968]{0:T(1024)(128)(4,1)S(1)}, s32[]{:S(2)}) async-start(s8[9240576]{0:T(1024)(128)(4,1)} %bitcast.42), calls=%async_computation.1 | async-start | bytes 1703936
  174.8 4.5 %copy-start = (f32[256,3008]{0,1:T(8,128)S(1)}, f32[256,3008]{0,1:T(8,128)}, u32[]{:S(2)}) copy-start(f32[256,3008]{0,1:T(8,128)} %get-tuple-element.18) | copy-start | bytes 9240580
  176.3 7.7 %slice-start.1 = ((s8[9240576]{0:T(1024)(128)(4,1)}), s8[4194304]{0:T(1024)(128)(4,1)S(1)}, s32[]{:S(2)}) async-start(s8[9240576]{0:T(1024)(128)(4,1)} %bitcast.42), calls=%async_computation.2 | async-start | bytes 8388608
  180.7 3.3 %slice-start.2 = ((s8[9240576]{0:T(1024)(128)(4,1)}), s8[4194304]{0:T(1024)(128)(4,1)S(1)}, s32[]{:S(2)}) async-start(s8[9240576]{0:T(1024)(128)(4,1)} %bitcast.42), calls=%async_computation.3 | async-start | bytes 8388608
Sparse Core Ops, SparseCore 0:
  41.6 71.2 all-reduce.3
where the time goes:
time: 202 us; the launch traced here: 201 us
  waiting for transfers between devices  71.5 us (35%)
  other arithmetic  56.7 us (28%)
  matrix products  31 us (15%)
  blocking collectives  21.5 us (11%)
  between operations  15.5 us (8%)
  local copies, waits for them, and re-layouts  5.15 us (3%)
    psum x1, waiting for transfers between devices, per_device(): cross_terms = lax.psum(cross_rows(trailing, panel_full), 'row')  71.4 us
    another operation x6, other arithmetic, per_device(): lower_factor = jnp.linalg.cholesky(panel_gram)  34 us
    all_gather x1, blocking collectives, per_device(): panel_full = lax.all_gather(panel, 'col', axis=1, tiled=True)  21.5 us
    another operation x3, other arithmetic, solve_right(): jax.scipy.linalg.solve_triangular(lower_factor, terms.T, lower=True)  19.9 us
    dot_general x2, matrix products, cross_rows(): lax.dot_general(left, right, (((0,), (0,)), ((), ())), precision=lax.Prec...  12.7 us
    dot_general x1, matrix products, per_device(): lax.dot_general(orthonormal, projections, (((1,), (1,)), ((), ())), preci...  10.5 us
    another operation x6, matrix products, solve_right(): jax.scipy.linalg.solve_triangular(lower_factor, terms.T, lower=True)  7.25 us
  transfers between devices with their start and end apart: 1, of which 1 were waited for; matrix products, arithmetic and copies ran while one was open for 0% of the time, Pallas kernels for 0%

commit v1 on v0

v1 whole, which is shorter than its diff:
```python
import functools

import jax
import jax.numpy as jnp
from jax import lax
from jax.experimental import pallas as pl
from jax.experimental.pallas import tpu as pltpu
from jax.sharding import PartitionSpec as P

F32, BF16 = jnp.float32, jnp.bfloat16
HIGHEST = lax.Precision.HIGHEST
NT, NN, TN = ((1,), (1,)), ((1,), (0,)), ((0,), (0,))
LANES, NB = 128, 64
VMEM_LIMIT = 40 * 2**20


def dot(a, b, dims, precision=None):
    return lax.dot_general(a, b, (dims, ((), ())), precision=precision, preferred_element_type=F32)


def split(x):
    hi = x.astype(BF16)
    return hi, (x - hi.astype(F32)).astype(BF16)


def params():
    return pltpu.CompilerParams(vmem_limit_bytes=VMEM_LIMIT)


def cost(flops, bytes_accessed):
    return pl.CostEstimate(flops=flops, bytes_accessed=bytes_accessed, transcendentals=0)


def block_rows(m):
    for b in (752, 376):
        if m % b == 0:
            return b
    return m


def cross_kernel(p_ref, t_ref, c_ref):
    n = p_ref.shape[0]
    p_hi, p_lo = split(p_ref[...])
    t_hi, t_lo = split(t_ref[...])
    both = dot(t_hi, jnp.concatenate([p_hi, p_lo], axis=0), NT)
    c_ref[...] = both[:, :n] + both[:, n:] + dot(t_lo, p_hi, NT)


def cross(p_t, t_t):
    n, k = p_t.shape
    m = t_t.shape[0]
    b = block_rows(m)
    return pl.pallas_call(
        cross_kernel,
        grid=(m // b,),
        in_specs=[pl.BlockSpec((n, k), lambda i: (0, 0)), pl.BlockSpec((b, k), lambda i: (i, 0))],
        out_specs=pl.BlockSpec((b, n), lambda i: (i, 0)),
        out_shape=jax.ShapeDtypeStruct((m, n), F32),
        compiler_params=params(),
        cost_estimate=cost(6 * n * k * m, 4 * (k * m + n * m + n * k)),
        name="cross",
    )(p_t, t_t)


def gram_kernel(p_ref, g_ref):
    p = p_ref[...]
    g_ref[...] = dot(p, p, NT, HIGHEST)


def gram(p_t):
    n, k = p_t.shape
    return pl.pallas_call(
        gram_kernel,
        out_shape=jax.ShapeDtypeStruct((n, n), F32),
        in_specs=[pl.BlockSpec(memory_space=pltpu.VMEM)],
        out_specs=pl.BlockSpec(memory_space=pltpu.VMEM),
        compiler_params=params(),
        cost_estimate=cost(12 * n * n * k, 4 * (n * k + n * n)),
        name="gram",
    )(p_t)


def tile(x):
    return jnp.broadcast_to(x, (8, LANES))


def eliminate(rows):
    sub = lax.broadcasted_iota(jnp.int32, (8, LANES), 0)
    n = len(rows)
    scaled = []
    for g in range(n):
        cols = [[tile(rows[i][:, 8 * g + c : 8 * g + c + 1]) for i in range(g, n)] for c in range(8)]
        own = rows[g]
        pivots = jnp.ones((8, LANES), F32)
        factors, lines = [], []
        for c in range(8):
            pivot = tile(cols[c][0][c : c + 1, :])
            inv = 1.0 / pivot
            f = [x * inv for x in cols[c]]
            f[0] = jnp.where(sub > c, f[0], 0.0)
            pivots = jnp.where(sub == c, pivot, pivots)
            for later in range(c + 1, 8):
                e = tile(cols[later][0][c : c + 1, :])
                cols[later] = [x - y * e for x, y in zip(cols[later], f)]
            line = tile(own[c : c + 1, :])
            own = own - f[0] * line
            factors.append(f)
            lines.append(line)
        for i in range(g + 1, n):
            for c in range(8):
                rows[i] = rows[i] - factors[c][i - g] * lines[c]
        scaled.append(own * lax.rsqrt(pivots))
    return scaled


def factor_kernel(g_ref, p_ref, lh_ref, ll_ref, qh_ref, ql_ref, work, linv):
    n = g_ref.shape[0]
    work[:, :n] = g_ref[...]
    i0 = lax.broadcasted_iota(jnp.int32, (n, n), 0)
    i1 = lax.broadcasted_iota(jnp.int32, (n, n), 1)
    eye = (i0 == i1).astype(F32)
    work[:, n:] = eye
    for s in range(0, n, NB):
        augmented = jnp.concatenate([work[s : s + NB, s : s + NB], eye[:NB, :NB]], axis=1)
        rows = eliminate([augmented[8 * i : 8 * i + 8] for i in range(NB // 8)])
        inv = jnp.concatenate(rows, axis=0)[:, NB:]
        r = dot(inv, work[s : s + NB, :], NN, HIGHEST)
        linv[s : s + NB, :] = r[:, n:]
        if s + NB < n:
            work[s + NB :, :] -= dot(r[:, s + NB : n], r, TN, HIGHEST)
    lh_ref[...], ll_ref[...] = split(linv[...])
    qh_ref[...], ql_ref[...] = split(dot(linv[...], p_ref[...], NN, HIGHEST))


def factor(g, p_t):
    n, k = p_t.shape
    vm = pl.BlockSpec(memory_space=pltpu.VMEM)
    return pl.pallas_call(
        factor_kernel,
        out_shape=[jax.ShapeDtypeStruct((n, n), BF16)] * 2 + [jax.ShapeDtypeStruct((n, k), BF16)] * 2,
        in_specs=[vm] * 2,
        out_specs=[vm] * 4,
        scratch_shapes=[pltpu.VMEM((n, 2 * n), F32), pltpu.VMEM((n, n), F32)],
        compiler_params=params(),
        cost_estimate=cost(10**10, 10**6),
        name="factor",
    )(g, p_t)


def update_kernel(first_ref, lh_ref, ll_ref, qh_ref, ql_ref, ca_ref, cb_ref, t_ref, p_ref, r_ref):
    a, b = ca_ref[...], cb_ref[...]
    swap = first_ref[0] != 0
    c_hi, c_lo = split(jnp.concatenate([jnp.where(swap, b, a), jnp.where(swap, a, b)], axis=1))
    lh, ll, qh, ql = lh_ref[...], ll_ref[...], qh_ref[...], ql_ref[...]
    p = dot(c_hi, lh, NT) + dot(c_lo, lh, NT) + dot(c_hi, ll, NT)
    p_ref[...] = p
    p_hi, p_lo = split(p)
    r_ref[...] = t_ref[...] - (dot(p_hi, qh, NN) + dot(p_lo, qh, NN) + dot(p_hi, ql, NN))


def update(first, lh, ll, qh, ql, ca, cb, t_t):
    n, k = qh.shape
    m = t_t.shape[0]
    b = block_rows(m)
    whole = lambda shape: pl.BlockSpec(shape, lambda i: (0, 0))
    part = lambda width: pl.BlockSpec((b, width), lambda i: (i, 0))
    return pl.pallas_call(
        update_kernel,
        grid=(m // b,),
        in_specs=[pl.BlockSpec(memory_space=pltpu.SMEM), whole((n, n)), whole((n, n)), whole((n, k)), whole((n, k)),
                  part(n // 2), part(n // 2), part(k)],
        out_specs=[part(n), part(k)],
        out_shape=[jax.ShapeDtypeStruct((m, n), F32), jax.ShapeDtypeStruct((m, k), F32)],
        compiler_params=params(),
        cost_estimate=cost(6 * n * (n + k) * m, 4 * m * (2 * k + 2 * n)),
        name="update",
    )(first, lh, ll, qh, ql, ca, cb, t_t)


class Rows:
    def __init__(self, count):
        self.count = count
        self.me = lax.axis_index("row")
        bits = list(range(1, count.bit_length() - 1))
        self.stages = [(0, 0)] + list(zip(bits, bits[::-1]))

    def swap(self, x, stage):
        by_core = self.stages[stage]
        return lax.ppermute(x, "row", [(r, r ^ (1 << by_core[r & 1])) for r in range(self.count)])

    def side(self, stage):
        b0, b1 = self.stages[stage]
        return jnp.where(self.me & 1 == 0, (self.me >> b0) & 1, (self.me >> b1) & 1)

    def halve(self, x, stage):
        h = x.shape[0] // 2
        s = self.side(stage)
        got = self.swap(lax.dynamic_slice_in_dim(x, (1 - s) * h, h), stage)
        return lax.dynamic_slice_in_dim(x, s * h, h) + got

    def double(self, x, stage):
        got = self.swap(x, stage)
        return jnp.where(self.side(stage) == 0, jnp.concatenate([x, got]), jnp.concatenate([got, x]))

    def sum_large(self, x):
        for s in range(len(self.stages)):
            x = self.halve(x, s)
        for s in reversed(range(len(self.stages))):
            x = self.double(x, s)
        return x

    def sum_small(self, x):
        x = self.halve(x, 0)
        for s in range(1, len(self.stages)):
            x = x + self.swap(x, s)
        return self.double(x, 0)


def per_device(shape, panel, trailing):
    p_own, t_t = panel.T, trailing.T
    rows = Rows(shape["row"])
    z, nz = lax.axis_index("col"), shape["col"]
    w, k = p_own.shape
    n = w * nz
    if nz == 4:
        def z_send(x, pairs):
            return lax.ppermute(x, "col", pairs)

        pair = z_send(p_own, [(0, 1), (1, 0), (2, 3), (3, 2)])
        across = z_send(p_own, [(0, 3), (3, 0), (1, 2), (2, 1)])
        inner = z_send(pair, [(1, 2), (2, 1)])
        outer = z_send(across, [(1, 0), (2, 3)])
        far = jnp.where((z == 1) | (z == 2), inner, outer)
        odd = z & 1 == 1
        near = jnp.where(odd, jnp.concatenate([pair, p_own]), jnp.concatenate([p_own, pair]))
        rest = jnp.where(odd, jnp.concatenate([across, far]), jnp.concatenate([far, across]))
        first = z >> 1
        p_full = jnp.where(first == 0, jnp.concatenate([near, rest]), jnp.concatenate([rest, near]))
    else:
        p_full = lax.all_gather(p_own, "col", axis=0, tiled=True)
        near, rest = p_full[: n // 2], p_full[n // 2 :]
        first = jnp.int32(0)
    c_near = rows.sum_large(cross(near, t_t))
    g = rows.sum_small(gram(p_full))
    c_rest = rows.sum_large(cross(rest, t_t))
    lh, ll, qh, ql = factor(g, p_full)
    projections, r_t = update(first.reshape(1), lh, ll, qh, ql, c_near, c_rest, t_t)
    return projections, r_t.T


def solution(mesh):
    return jax.shard_map(
        functools.partial(per_device, dict(mesh.shape)),
        mesh=mesh,
        in_specs=(P("row", "col"), P("row", "col")),
        out_specs=(P("col", None), P("row", "col")),
        check_vma=False,
    )
```

time: 202 us -> 95.1 us (0.47)
  other arithmetic: 56.7 us -> 2.14 us
  waiting for transfers between devices: 71.5 us -> 37.4 us
  matrix products: 31 us -> 0 us
  Pallas kernels: 0 us -> 27.3 us
  blocking collectives: 21.5 us -> 0 us
  starting transfers between devices: 0.04 us -> 20.3 us
  between operations: 15.5 us -> 0.99 us
    psum x1 -> x0, waiting for transfers between devices: 71.4 us -> none  [per_device(): cross_terms = lax.psum(cross_rows(trailing, panel_full), 'row')]
    another operation x9 -> x0, other arithmetic: 53.9 us -> none  [the longest x6 34 us: per_device(): lower_factor = jnp.linalg.cholesky(panel_gram)]
    ppermute x0 -> x20, waiting for transfers between devices: none -> 37.4 us  [the longest x16 25.6 us: swap(): lax.ppermute(x, 'row', [(r, r ^ 1 << by_core[r & 1]) for r in range(self....]
    pallas_call x0 -> x5, Pallas kernels: none -> 27.3 us  [the longest x1 10.5 us: factor(): pl.pallas_call(factor_kernel, out_shape=[jax.ShapeDtypeStruct((n, n), BF1...]
    dot_general x3 -> x0, matrix products: 23.3 us -> none  [the longest x2 12.7 us: cross_rows(): lax.dot_general(left, right, (((0,), (0,)), ((), ())), precision=lax.Prec...]
    all_gather x1 -> x0, blocking collectives: 21.5 us -> none  [per_device(): panel_full = lax.all_gather(panel, 'col', axis=1, tiled=True)]
    ppermute x0 -> x20, starting transfers between devices: none -> 20.3 us  [the longest x16 12.8 us: swap(): lax.ppermute(x, 'row', [(r, r ^ 1 << by_core[r & 1]) for r in range(self....]
    another operation x8 -> x0, matrix products: 7.73 us -> none  [the longest x6 7.25 us: solve_right(): jax.scipy.linalg.solve_triangular(lower_factor, terms.T, lower=True)]
  transfers between devices with their start and end apart: 1 -> 20, of which waited for: 1 -> 9; matrix products, arithmetic and copies ran while one was open for 0% -> 4% of each run, Pallas kernels for 0% -> 19%
where the time goes in v1:
time: 95.1 us; the launch traced here: 93.5 us
  waiting for transfers between devices  37.4 us (39%)
  Pallas kernels  27.3 us (29%)
  starting transfers between devices  20.3 us (21%)
  local copies, waits for them, and re-layouts  5.37 us (6%)
  other arithmetic  2.14 us (2%)
  between operations  0.99 us (1%)
    ppermute x16, waiting for transfers between devices, swap(): lax.ppermute(x, 'row', [(r, r ^ 1 << by_core[r & 1]) for r in range(self....  25.6 us
    ppermute x16, starting transfers between devices, swap(): lax.ppermute(x, 'row', [(r, r ^ 1 << by_core[r & 1]) for r in range(self....  12.8 us
    ppermute x4, waiting for transfers between devices, z_send(): return lax.ppermute(x, 'col', pairs)  11.8 us
    pallas_call x1, Pallas kernels, factor(): pl.pallas_call(factor_kernel, out_shape=[jax.ShapeDtypeStruct((n, n), BF1...  10.5 us
    pallas_call x1, Pallas kernels, update(): pl.pallas_call(update_kernel, grid=(m // b,), in_specs=[pl.BlockSpec(memo...  9.33 us
    ppermute x4, starting transfers between devices, z_send(): return lax.ppermute(x, 'col', pairs)  7.52 us
    pallas_call x2, Pallas kernels, cross(): pl.pallas_call(cross_kernel, grid=(m // b,), in_specs=[pl.BlockSpec((n, k...  6.62 us
    unnamed x10, local copies, waits for them, and re-layouts  3.64 us
  transfers between devices with their start and end apart: 20, of which 9 were waited for; matrix products, arithmetic and copies ran while one was open for 4% of the time, Pallas kernels for 19%

profile of v1, /device:TPU:0, one launch (start us, length us, event | category | flops | bytes accessed | tf_op | source)
XLA Modules:
  0.0 93.5 jit_solution(16373486617500933807)
XLA Ops:
  0.6 3.1 %collective-permute-start = (f32[64,768]{1,0:T(8,128)}, f32[64,768]{1,0:T(8,128)S(1)}, u32[]{:S(2)}, u32[]{:S(2)}) collective-permute-start(f32[64,768]{1,0:T(8,128)} %bitcast.9), channel_id=1, source_target_pairs={{0,1},{1,0},{2,3},{3,2},{4,5},{5,4},{6,7},{7,6},{8,9},{9,8},{10,11... | collective-permute-start | bytes 589832 | tf_op jit(solution)/shard_map/ppermute | solution.py:227
  3.7 2.5 %collective-permute-start.1 = (f32[64,768]{1,0:T(8,128)}, f32[64,768]{1,0:T(8,128)S(1)}, u32[]{:S(2)}, u32[]{:S(2)}) collective-permute-start(f32[64,768]{1,0:T(8,128)} %bitcast.10), channel_id=1, source_target_pairs={{0,3},{3,0},{1,2},{2,1},{4,7},{7,4},{5,6},{6,5},{8,11},{11,8},{9,1... | collective-permute-start | bytes 589832 | tf_op jit(solution)/shard_map/ppermute | solution.py:227
  6.2 3.1 %collective-permute-done = f32[64,768]{1,0:T(8,128)S(1)} collective-permute-done((f32[64,768]{1,0:T(8,128)}, f32[64,768]{1,0:T(8,128)S(1)}, u32[]{:S(2)}, u32[]{:S(2)}) %collective-permute-start) | collective-permute-done | bytes 196640 | tf_op jit(solution)/shard_map/ppermute | solution.py:227
  9.3 0.7 collective-permute-start.2
  10.0 1.1 %maximum_select_fusion.5.p_ref = f32[128,768]{1,0:T(8,128)S(1)} fusion(f32[64,768]{1,0:T(8,128)} %bitcast.11, f32[64,768]{1,0:T(8,128)S(1)} %collective-permute-done, pred[]{:T(512)S(6)} %eq.18), kind=kLoop, calls=%fused_computation.7 | loop fusion | flops 294912 | bytes 786433 | tf_op jit(solution)/shard_map/jit(_where)/select_n | solution.py:235
  11.1 0.0 copy-start
  11.1 3.6 %copy-done = f32[768,3008]{0,1:T(8,128)S(1)} copy-done((f32[768,3008]{0,1:T(8,128)S(1)}, f32[768,3008]{0,1:T(8,128)}, u32[]{:S(2)}) %copy-start) | copy-done | bytes 9240600
  14.7 3.2 %cross.2 = f32[3008,128]{1,0:T(8,128)S(1)} custom-call(f32[128,768]{1,0:T(8,128)S(1)} %maximum_select_fusion.5.p_ref, f32[3008,768]{1,0:T(8,128)S(1)} %bitcast.4), custom_call_target="tpu_custom_call" | custom-call | flops 1774190592 | bytes 11173888 | tf_op jit(solution)/shard_map/cross/pallas_call | solution.py:53
  17.9 0.0 collective-permute-done.1
  17.9 1.3 %collective-permute-start.3 = (f32[64,768]{1,0:T(8,128)S(1)}, f32[64,768]{1,0:T(8,128)S(1)}, u32[]{:S(2)}, u32[]{:S(2)}) collective-permute-start(f32[64,768]{1,0:T(8,128)S(1)} %collective-permute-done.1), channel_id=1, source_target_pairs={{1,0},{2,3},{5,4},{6,7},{9,8},{10,11},{13,12},{14,15},{17,16},{18,... | collective-permute-start | bytes 589832 | tf_op jit(solution)/shard_map/ppermute | solution.py:227
  19.2 0.1 constant_dynamic-slice_fusion.5
  19.3 0.1 collective-permute-start.8
  19.4 8.7 %collective-permute-done.3 = f32[64,768]{1,0:T(8,128)S(1)} collective-permute-done((f32[64,768]{1,0:T(8,128)S(1)}, f32[64,768]{1,0:T(8,128)S(1)}, u32[]{:S(2)}, u32[]{:S(2)}) %collective-permute-start.3) | collective-permute-done | bytes 196640 | tf_op jit(solution)/shard_map/ppermute | solution.py:227
  28.0 0.0 collective-permute-done.2
  28.1 0.1 maximum_select_fusion.2.p_ref
  28.2 0.8 gram.1
  29.1 0.1 collective-permute-start.4
  29.1 0.0 copy-done.1
  29.1 3.4 %cross.3 = f32[3008,128]{1,0:T(8,128)S(1)} custom-call(f32[128,768]{1,0:T(8,128)S(1)} %maximum_select_fusion.6.p_ref, f32[3008,768]{1,0:T(8,128)S(1)} %bitcast.5), custom_call_target="tpu_custom_call" | custom-call | flops 1774190592 | bytes 11173888 | tf_op jit(solution)/shard_map/cross/pallas_call | solution.py:53
  32.6 0.1 constant_dynamic-slice_fusion.2
  32.6 0.4 collective-permute-start.14
  33.0 0.0 collective-permute-done.4
  33.0 1.6 %collective-permute-start.5 = (f32[128,256]{1,0:T(8,128)S(1)}, f32[128,256]{1,0:T(8,128)S(1)}, u32[]{:S(2)}, u32[]{:S(2)}) collective-permute-start(f32[128,256]{1,0:T(8,128)S(1)} %dynamic-slice_add_fusion.6), channel_id=1, source_target_pairs={{0,8},{4,20},{8,0},{12,28},{16,24},{20,4},{24,16},{28,12},{1,9},{5... | collective-permute-start | bytes 393224 | tf_op jit(solution)/shard_map/ppermute | solution.py:189
  34.6 0.0 collective-permute-done.8
  34.6 0.1 dynamic-slice_add_fusion.1
  34.6 0.8 constant_dynamic-slice_fusion.4
  35.4 0.5 collective-permute-start.9
  36.0 0.0 collective-permute-done.14
  36.0 0.1 dynamic-slice_add_fusion
  36.0 0.8 constant_dynamic-slice_fusion.1
  36.8 1.5 %collective-permute-start.15 = (f32[752,128]{1,0:T(8,128)}, f32[752,128]{1,0:T(8,128)S(1)}, u32[]{:S(2)}, u32[]{:S(2)}) collective-permute-start(f32[752,128]{1,0:T(8,128)} %constant_dynamic-slice_fusion.1), channel_id=1, source_target_pairs={{0,8},{4,20},{8,0},{12,28},{16,24},{20,4},{24,16},{28,12},{1,9},{5... | collective-permute-start | bytes 1155080 | tf_op jit(solution)/shard_map/ppermute | solution.py:189
  38.3 0.0 collective-permute-done.5
  38.3 1.6 %collective-permute-start.6 = (f32[128,256]{1,0:T(8,128)S(1)}, f32[128,256]{1,0:T(8,128)S(1)}, u32[]{:S(2)}, u32[]{:S(2)}) collective-permute-start(f32[128,256]{1,0:T(8,128)S(1)} %add.60), channel_id=1, source_target_pairs={{0,16},{4,12},{8,24},{12,4},{16,0},{20,28},{24,8},{28,20},{1,17},{... | collective-permute-start | bytes 393224 | tf_op jit(solution)/shard_map/ppermute | solution.py:189
  39.9 4.8 %collective-permute-done.9 = f32[752,128]{1,0:T(8,128)S(1)} collective-permute-done((f32[752,128]{1,0:T(8,128)}, f32[752,128]{1,0:T(8,128)S(1)}, u32[]{:S(2)}, u32[]{:S(2)}) %collective-permute-start.9) | collective-permute-done | bytes 385056 | tf_op jit(solution)/shard_map/ppermute | solution.py:189
  44.8 2.0 %collective-permute-start.10 = (f32[376,128]{1,0:T(8,128)S(1)}, f32[376,128]{1,0:T(8,128)S(1)}, u32[]{:S(2)}, u32[]{:S(2)}) collective-permute-start(f32[376,128]{1,0:T(8,128)S(1)} %constant_dynamic-slice_fusion.3), channel_id=1, source_target_pairs={{0,16},{4,12},{8,24},{12,4},{16,0},{20,28},{24,8},{28,20},{1,17},{... | collective-permute-start | bytes 577544 | tf_op jit(solution)/shard_map/ppermute | solution.py:189
  46.8 4.2 %collective-permute-done.15 = f32[752,128]{1,0:T(8,128)S(1)} collective-permute-done((f32[752,128]{1,0:T(8,128)}, f32[752,128]{1,0:T(8,128)S(1)}, u32[]{:S(2)}, u32[]{:S(2)}) %collective-permute-start.15) | collective-permute-done | bytes 385056 | tf_op jit(solution)/shard_map/ppermute | solution.py:189
  51.1 2.5 %collective-permute-start.16 = (f32[376,128]{1,0:T(8,128)S(1)}, f32[376,128]{1,0:T(8,128)S(1)}, u32[]{:S(2)}, u32[]{:S(2)}) collective-permute-start(f32[376,128]{1,0:T(8,128)S(1)} %constant_dynamic-slice_fusion), channel_id=1, source_target_pairs={{0,16},{4,12},{8,24},{12,4},{16,0},{20,28},{24,8},{28,20},{1,17},{... | collective-permute-start | bytes 577544 | tf_op jit(solution)/shard_map/ppermute | solution.py:189
  53.6 0.0 collective-permute-done.10
  53.7 0.1 collective-permute-start.11
  53.7 3.5 %collective-permute-done.16 = f32[376,128]{1,0:T(8,128)S(1)} collective-permute-done((f32[376,128]{1,0:T(8,128)S(1)}, f32[376,128]{1,0:T(8,128)S(1)}, u32[]{:S(2)}, u32[]{:S(2)}) %collective-permute-start.16) | collective-permute-done | bytes 192544 | tf_op jit(solution)/shard_map/ppermute | solution.py:189
  57.3 2.2 %collective-permute-start.17 = (f32[376,128]{1,0:T(8,128)S(1)}, f32[376,128]{1,0:T(8,128)S(1)}, u32[]{:S(2)}, u32[]{:S(2)}) collective-permute-start(f32[376,128]{1,0:T(8,128)S(1)} %dynamic-slice_add_fusion.4), channel_id=1, source_target_pairs={{0,16},{4,12},{8,24},{12,4},{16,0},{20,28},{24,8},{28,20},{1,17},{... | collective-permute-start | bytes 577544 | tf_op jit(solution)/shard_map/ppermute | solution.py:189
  59.5 1.7 %collective-permute-done.11 = f32[376,128]{1,0:T(8,128)S(1)} collective-permute-done((f32[376,128]{1,0:T(8,128)S(1)}, f32[376,128]{1,0:T(8,128)S(1)}, u32[]{:S(2)}, u32[]{:S(2)}) %collective-permute-start.11) | collective-permute-done | bytes 192544 | tf_op jit(solution)/shard_map/ppermute | solution.py:189
  61.2 0.1 collective-permute-start.12
  61.2 0.0 collective-permute-done.6
  61.3 0.1 collective-permute-start.7
  61.4 3.9 %collective-permute-done.17 = f32[376,128]{1,0:T(8,128)S(1)} collective-permute-done((f32[376,128]{1,0:T(8,128)S(1)}, f32[376,128]{1,0:T(8,128)S(1)}, u32[]{:S(2)}, u32[]{:S(2)}) %collective-permute-start.17) | collective-permute-done | bytes 192544 | tf_op jit(solution)/shard_map/ppermute | solution.py:189
  65.3 0.1 collective-permute-start.18
  65.4 0.0 collective-permute-done.7
  65.4 3.5 %collective-permute-done.12 = f32[752,128]{1,0:T(8,128)S(1)} collective-permute-done((f32[752,128]{1,0:T(8,128)S(1)}, f32[752,128]{1,0:T(8,128)S(1)}, u32[]{:S(2)}, u32[]{:S(2)}) %collective-permute-start.12) | collective-permute-done | bytes 385056 | tf_op jit(solution)/shard_map/ppermute | solution.py:189
  68.9 0.1 maximum_select_fusion.3
  69.0 0.1 collective-permute-start.13
  69.1 4.0 %collective-permute-done.18 = f32[752,128]{1,0:T(8,128)S(1)} collective-permute-done((f32[752,128]{1,0:T(8,128)S(1)}, f32[752,128]{1,0:T(8,128)S(1)}, u32[]{:S(2)}, u32[]{:S(2)}) %collective-permute-start.18) | collective-permute-done | bytes 385056 | tf_op jit(solution)/shard_map/ppermute | solution.py:189
  73.1 0.1 maximum_select_fusion.4
  73.2 0.0 slice-start.1
  73.2 0.0 slice-start.2
  73.2 0.1 collective-permute-start.19
  73.3 10.5 %factor.1 = (bf16[256,256]{1,0:T(8,128)(2,1)S(1)}, bf16[256,256]{1,0:T(8,128)(2,1)S(1)}, bf16[256,768]{1,0:T(8,128)(2,1)S(1)}, bf16[256,768]{1,0:T(8,128)(2,1)S(1)}) custom-call(f32[256,256]{1,0:T(8,128)S(1)} %maximum_select_fusion.9.g_ref, f32[256,768]{1,0:T(8,128)S(1)} %maximum_select_fusion.2.p_ref), custom_call_target="tpu_custom_call" | custom-call | flops 10000000000 | bytes 1000000 | tf_op jit(solution)/shard_map/factor/pallas_call | solution.py:138
  83.8 0.0 collective-permute-done.13
  83.8 0.2 maximum_select_fusion.ca_ref
  84.0 0.0 collective-permute-done.19
  84.0 0.2 maximum_select_fusion.1.cb_ref
  84.1 0.0 slice-done
  84.1 0.0 slice-done.1
  84.2 9.3 %update.1 = (f32[3008,256]{1,0:T(8,128)}, f32[3008,768]{1,0:T(8,128)}) custom-call(s32[1]{0:T(128)} %bitcast.first_ref, bf16[256,256]{1,0:T(8,128)(2,1)S(1)} %get-tuple-element.8.lh_ref, bf16[256,256]{1,0:T(8,128)(2,1)S(1)} %get-tuple-element.9.ll_ref, bf16[256,768]{1,0:T(8,128)(2,1)S(1)} %get-tuple-element.10.qh_ref, ...), custom_call_target="tpu_custom_call" | custom-call | flops 4731174912 | bytes 24641536 | tf_op jit(solution)/shard_map/update/pallas_call | solution.py:167
  (19 shorter events, 0.4 us)
Async XLA Ops:
  0.6 8.7 %collective-permute-start = (f32[64,768]{1,0:T(8,128)}, f32[64,768]{1,0:T(8,128)S(1)}, u32[]{:S(2)}, u32[]{:S(2)}) collective-permute-start(f32[64,768]{1,0:T(8,128)} %bitcast.9), channel_id=1, source_target_pairs={{0,1},{1,0},{2,3},{3,2},{4,5},{5,4},{6,7},{7,6},{8,9},{9,8},{10,11... | collective-permute-start | bytes 589832 | tf_op jit(solution)/shard_map/ppermute | solution.py:227
  3.7 14.2 %collective-permute-start.1 = (f32[64,768]{1,0:T(8,128)}, f32[64,768]{1,0:T(8,128)S(1)}, u32[]{:S(2)}, u32[]{:S(2)}) collective-permute-start(f32[64,768]{1,0:T(8,128)} %bitcast.10), channel_id=1, source_target_pairs={{0,3},{3,0},{1,2},{2,1},{4,7},{7,4},{5,6},{6,5},{8,11},{11,8},{9,1... | collective-permute-start | bytes 589832 | tf_op jit(solution)/shard_map/ppermute | solution.py:227
  9.3 18.7 %collective-permute-start.2 = (f32[64,768]{1,0:T(8,128)S(1)}, f32[64,768]{1,0:T(8,128)S(1)}, u32[]{:S(2)}, u32[]{:S(2)}) collective-permute-start(f32[64,768]{1,0:T(8,128)S(1)} %collective-permute-done), channel_id=1, source_target_pairs={{1,2},{2,1},{5,6},{6,5},{9,10},{10,9},{13,14},{14,13},{17,18},{18,... | collective-permute-start | bytes 589832 | tf_op jit(solution)/shard_map/ppermute | solution.py:227
  11.1 3.6 %copy-start = (f32[768,3008]{0,1:T(8,128)S(1)}, f32[768,3008]{0,1:T(8,128)}, u32[]{:S(2)}) copy-start(f32[768,3008]{0,1:T(8,128)} %param.3) | copy-start | bytes 27721732
  14.7 14.4 %copy-start.1 = (f32[768,3008]{0,1:T(8,128)S(1)}, f32[768,3008]{0,1:T(8,128)}, u32[]{:S(2)}) copy-start(f32[768,3008]{0,1:T(8,128)} %param.3) | copy-start | bytes 27721732
  17.9 10.1 %collective-permute-start.3 = (f32[64,768]{1,0:T(8,128)S(1)}, f32[64,768]{1,0:T(8,128)S(1)}, u32[]{:S(2)}, u32[]{:S(2)}) collective-permute-start(f32[64,768]{1,0:T(8,128)S(1)} %collective-permute-done.1), channel_id=1, source_target_pairs={{1,0},{2,3},{5,4},{6,7},{9,8},{10,11},{13,12},{14,15},{17,16},{18,... | collective-permute-start | bytes 589832 | tf_op jit(solution)/shard_map/ppermute | solution.py:227
  19.3 15.3 %collective-permute-start.8 = (f32[1504,128]{1,0:T(8,128)S(1)}, f32[1504,128]{1,0:T(8,128)S(1)}, u32[]{:S(2)}, u32[]{:S(2)}) collective-permute-start(f32[1504,128]{1,0:T(8,128)S(1)} %constant_dynamic-slice_fusion.5), channel_id=1, source_target_pairs={{0,4},{4,0},{8,12},{12,8},{16,20},{20,16},{24,28},{28,24},{1,5},{5... | collective-permute-start | bytes 2310152 | tf_op jit(solution)/shard_map/ppermute | solution.py:189
  29.1 3.9 %collective-permute-start.4 = (f32[128,256]{1,0:T(8,128)S(1)}, f32[128,256]{1,0:T(8,128)S(1)}, u32[]{:S(2)}, u32[]{:S(2)}) collective-permute-start(f32[128,256]{1,0:T(8,128)S(1)} %constant_dynamic-slice_fusion.6), channel_id=1, source_target_pairs={{0,4},{4,0},{8,12},{12,8},{16,20},{20,16},{24,28},{28,24},{1,5},{5... | collective-permute-start | bytes 393224 | tf_op jit(solution)/shard_map/ppermute | solution.py:189
  32.6 3.3 %collective-permute-start.14 = (f32[1504,128]{1,0:T(8,128)S(1)}, f32[1504,128]{1,0:T(8,128)S(1)}, u32[]{:S(2)}, u32[]{:S(2)}) collective-permute-start(f32[1504,128]{1,0:T(8,128)S(1)} %constant_dynamic-slice_fusion.2), channel_id=1, source_target_pairs={{0,4},{4,0},{8,12},{12,8},{16,20},{20,16},{24,28},{28,24},{1,5},{5... | collective-permute-start | bytes 2310152 | tf_op jit(solution)/shard_map/ppermute | solution.py:189
  33.0 5.3 %collective-permute-start.5 = (f32[128,256]{1,0:T(8,128)S(1)}, f32[128,256]{1,0:T(8,128)S(1)}, u32[]{:S(2)}, u32[]{:S(2)}) collective-permute-start(f32[128,256]{1,0:T(8,128)S(1)} %dynamic-slice_add_fusion.6), channel_id=1, source_target_pairs={{0,8},{4,20},{8,0},{12,28},{16,24},{20,4},{24,16},{28,12},{1,9},{5... | collective-permute-start | bytes 393224 | tf_op jit(solution)/shard_map/ppermute | solution.py:189
  35.4 9.3 %collective-permute-start.9 = (f32[752,128]{1,0:T(8,128)}, f32[752,128]{1,0:T(8,128)S(1)}, u32[]{:S(2)}, u32[]{:S(2)}) collective-permute-start(f32[752,128]{1,0:T(8,128)} %constant_dynamic-slice_fusion.4), channel_id=1, source_target_pairs={{0,8},{4,20},{8,0},{12,28},{16,24},{20,4},{24,16},{28,12},{1,9},{5... | collective-permute-start | bytes 1155080 | tf_op jit(solution)/shard_map/ppermute | solution.py:189
  36.8 14.2 %collective-permute-start.15 = (f32[752,128]{1,0:T(8,128)}, f32[752,128]{1,0:T(8,128)S(1)}, u32[]{:S(2)}, u32[]{:S(2)}) collective-permute-start(f32[752,128]{1,0:T(8,128)} %constant_dynamic-slice_fusion.1), channel_id=1, source_target_pairs={{0,8},{4,20},{8,0},{12,28},{16,24},{20,4},{24,16},{28,12},{1,9},{5... | collective-permute-start | bytes 1155080 | tf_op jit(solution)/shard_map/ppermute | solution.py:189
  38.3 22.9 %collective-permute-start.6 = (f32[128,256]{1,0:T(8,128)S(1)}, f32[128,256]{1,0:T(8,128)S(1)}, u32[]{:S(2)}, u32[]{:S(2)}) collective-permute-start(f32[128,256]{1,0:T(8,128)S(1)} %add.60), channel_id=1, source_target_pairs={{0,16},{4,12},{8,24},{12,4},{16,0},{20,28},{24,8},{28,20},{1,17},{... | collective-permute-start | bytes 393224 | tf_op jit(solution)/shard_map/ppermute | solution.py:189
  44.8 8.8 %collective-permute-start.10 = (f32[376,128]{1,0:T(8,128)S(1)}, f32[376,128]{1,0:T(8,128)S(1)}, u32[]{:S(2)}, u32[]{:S(2)}) collective-permute-start(f32[376,128]{1,0:T(8,128)S(1)} %constant_dynamic-slice_fusion.3), channel_id=1, source_target_pairs={{0,16},{4,12},{8,24},{12,4},{16,0},{20,28},{24,8},{28,20},{1,17},{... | collective-permute-start | bytes 577544 | tf_op jit(solution)/shard_map/ppermute | solution.py:189
  51.1 6.1 %collective-permute-start.16 = (f32[376,128]{1,0:T(8,128)S(1)}, f32[376,128]{1,0:T(8,128)S(1)}, u32[]{:S(2)}, u32[]{:S(2)}) collective-permute-start(f32[376,128]{1,0:T(8,128)S(1)} %constant_dynamic-slice_fusion), channel_id=1, source_target_pairs={{0,16},{4,12},{8,24},{12,4},{16,0},{20,28},{24,8},{28,20},{1,17},{... | collective-permute-start | bytes 577544 | tf_op jit(solution)/shard_map/ppermute | solution.py:189
  53.7 7.5 %collective-permute-start.11 = (f32[376,128]{1,0:T(8,128)S(1)}, f32[376,128]{1,0:T(8,128)S(1)}, u32[]{:S(2)}, u32[]{:S(2)}) collective-permute-start(f32[376,128]{1,0:T(8,128)S(1)} %dynamic-slice_add_fusion.5), channel_id=1, source_target_pairs={{0,16},{4,12},{8,24},{12,4},{16,0},{20,28},{24,8},{28,20},{1,17},{... | collective-permute-start | bytes 577544 | tf_op jit(solution)/shard_map/ppermute | solution.py:189
  57.3 8.0 %collective-permute-start.17 = (f32[376,128]{1,0:T(8,128)S(1)}, f32[376,128]{1,0:T(8,128)S(1)}, u32[]{:S(2)}, u32[]{:S(2)}) collective-permute-start(f32[376,128]{1,0:T(8,128)S(1)} %dynamic-slice_add_fusion.4), channel_id=1, source_target_pairs={{0,16},{4,12},{8,24},{12,4},{16,0},{20,28},{24,8},{28,20},{1,17},{... | collective-permute-start | bytes 577544 | tf_op jit(solution)/shard_map/ppermute | solution.py:189
  61.2 7.8 %collective-permute-start.12 = (f32[752,128]{1,0:T(8,128)S(1)}, f32[752,128]{1,0:T(8,128)S(1)}, u32[]{:S(2)}, u32[]{:S(2)}) collective-permute-start(f32[752,128]{1,0:T(8,128)S(1)} %maximum_select_fusion.7), channel_id=1, source_target_pairs={{0,8},{4,20},{8,0},{12,28},{16,24},{20,4},{24,16},{28,12},{1,9},{5... | collective-permute-start | bytes 1155080 | tf_op jit(solution)/shard_map/ppermute | solution.py:189
  61.3 4.1 %collective-permute-start.7 = (f32[128,256]{1,0:T(8,128)S(1)}, f32[128,256]{1,0:T(8,128)S(1)}, u32[]{:S(2)}, u32[]{:S(2)}) collective-permute-start(f32[128,256]{1,0:T(8,128)S(1)} %add.61), channel_id=1, source_target_pairs={{0,4},{4,0},{8,12},{12,8},{16,20},{20,16},{24,28},{28,24},{1,5},{5... | collective-permute-start | bytes 393224 | tf_op jit(solution)/shard_map/ppermute | solution.py:189
  65.3 7.8 %collective-permute-start.18 = (f32[752,128]{1,0:T(8,128)S(1)}, f32[752,128]{1,0:T(8,128)S(1)}, u32[]{:S(2)}, u32[]{:S(2)}) collective-permute-start(f32[752,128]{1,0:T(8,128)S(1)} %maximum_select_fusion.8), channel_id=1, source_target_pairs={{0,8},{4,20},{8,0},{12,28},{16,24},{20,4},{24,16},{28,12},{1,9},{5... | collective-permute-start | bytes 1155080 | tf_op jit(solution)/shard_map/ppermute | solution.py:189
  69.0 14.8 %collective-permute-start.13 = (f32[1504,128]{1,0:T(8,128)S(1)}, f32[1504,128]{1,0:T(8,128)S(1)}, u32[]{:S(2)}, u32[]{:S(2)}) collective-permute-start(f32[1504,128]{1,0:T(8,128)S(1)} %maximum_select_fusion.3), channel_id=1, source_target_pairs={{0,4},{4,0},{8,12},{12,8},{16,20},{20,16},{24,28},{28,24},{1,5},{5... | collective-permute-start | bytes 2310152 | tf_op jit(solution)/shard_map/ppermute | solution.py:189
  73.1 11.1 %slice-start = ((s8[9240576]{0:T(1024)(128)(4,1)}), s8[4194304]{0:T(1024)(128)(4,1)S(1)}, s32[]{:S(2)}) async-start(s8[9240576]{0:T(1024)(128)(4,1)} %bitcast.6), calls=%async_computation | async-start | bytes 8388608
  73.2 11.0 %slice-start.1 = ((s8[9240576]{0:T(1024)(128)(4,1)}), s8[4194304]{0:T(1024)(128)(4,1)S(1)}, s32[]{:S(2)}) async-start(s8[9240576]{0:T(1024)(128)(4,1)} %bitcast.6), calls=%async_computation.1 | async-start | bytes 8388608
  73.2 11.0 %slice-start.2 = ((s8[9240576]{0:T(1024)(128)(4,1)}), s8[851968]{0:T(1024)(128)(4,1)S(1)}, s32[]{:S(2)}) async-start(s8[9240576]{0:T(1024)(128)(4,1)} %bitcast.6), calls=%async_computation.2 | async-start | bytes 1703936
  73.2 10.8 %collective-permute-start.19 = (f32[1504,128]{1,0:T(8,128)S(1)}, f32[1504,128]{1,0:T(8,128)S(1)}, u32[]{:S(2)}, u32[]{:S(2)}) collective-permute-start(f32[1504,128]{1,0:T(8,128)S(1)} %maximum_select_fusion.4), channel_id=1, source_target_pairs={{0,4},{4,0},{8,12},{12,8},{16,20},{20,16},{24,28},{28,24},{1,5},{5... | collective-permute-start | bytes 2310152 | tf_op jit(solution)/shard_map/ppermute | solution.py:189

commit v2 on v0

v2 whole, which is shorter than its diff:
```python
import functools

import jax
import jax.numpy as jnp
from jax import lax
from jax.experimental import pallas as pl
from jax.experimental.pallas import tpu as pltpu
from jax.sharding import PartitionSpec as P

F32, BF16 = jnp.float32, jnp.bfloat16
HIGHEST = lax.Precision.HIGHEST
NT, NN, TN = ((1,), (1,)), ((1,), (0,)), ((0,), (0,))
LANES, NB = 128, 64
VMEM_LIMIT = 12 * 2**20


def dot(a, b, dims, precision=None):
    return lax.dot_general(a, b, (dims, ((), ())), precision=precision, preferred_element_type=F32)


def split(x):
    hi = x.astype(BF16)
    return hi, (x - hi.astype(F32)).astype(BF16)


def params():
    return pltpu.CompilerParams(vmem_limit_bytes=VMEM_LIMIT)


def cost():
    return None


VM = pl.BlockSpec(memory_space=pltpu.VMEM)
HBM = pl.BlockSpec(memory_space=pltpu.HBM)
SMEM = pl.BlockSpec(memory_space=pltpu.SMEM)


def block_rows(m):
    for b in (752, 376):
        if m % b == 0:
            return b
    return m


Z, ODD, FIRST, OTHER, SIDE = 0, 1, 2, 3, 4


def touch_kernel(at_ref, p_ref, t_ref, o_ref, p_out, zero_ref):
    for i in range(at_ref.shape[0]):
        o_ref[i] = at_ref[i]
    p_out[...] = p_ref[...]
    zero_ref[...] = jnp.zeros_like(zero_ref)


def touch(at, p_t, t):
    return pl.pallas_call(
        touch_kernel,
        out_shape=[jax.ShapeDtypeStruct(s, d) for s, d in ((at.shape, jnp.int32), (p_t.shape, F32), (p_t.shape, F32))],
        in_specs=[SMEM, VM, VM],
        out_specs=[SMEM, VM, VM],
        compiler_params=params(),
        cost_estimate=cost(),
        name="touch",
    )(at, p_t, t)


def cross_kernel(at_ref, pa_ref, pb_ref, t_ref, *c_refs, mine):
    n = 2 * pa_ref.shape[0]
    m = c_refs[0].shape[0]
    b = block_rows(m)
    pa, pb = pa_ref[...], pb_ref[...]
    swap = at_ref[ODD] != 0
    p_hi, p_lo = split(jnp.concatenate([jnp.where(swap, pb, pa), jnp.where(swap, pa, pb)], axis=0))
    both = jnp.concatenate([p_hi, p_lo], axis=0)
    for c_ref, own in zip(c_refs, mine):
        half = at_ref[SIDE] if own else 1 - at_ref[SIDE]
        base = pl.multiple_of(half * m, 8)
        for i in range(m // b):
            t_hi, t_lo = split(t_ref[pl.ds(base + i * b, b), :])
            c = dot(t_hi, both, NT)
            c_ref[i * b : (i + 1) * b, :] = c[:, :n] + c[:, n:] + dot(t_lo, p_hi, NT)


def cross(at, mine, pa, pb, t):
    return pl.pallas_call(
        functools.partial(cross_kernel, mine=mine),
        out_shape=[jax.ShapeDtypeStruct((t.shape[0] // 2, 2 * pa.shape[0]), F32)] * len(mine),
        in_specs=[SMEM, VM, VM, VM],
        out_specs=[VM] * len(mine),
        compiler_params=params(),
        cost_estimate=cost(),
        name="cross",
    )(at, pa, pb, t)


def gram_kernel(at_ref, own, pair, far, across, p_full, g_ref):
    w = own.shape[0]
    z = at_ref[Z]
    for flip, block in enumerate((own, pair, far, across)):
        p_full[pl.ds(pl.multiple_of((z ^ flip) * w, 8), w), :] = block[...]
    p = p_full[...]
    g_ref[...] = dot(p, p, NT, HIGHEST)


def gram4(at, *blocks):
    w, k = blocks[0].shape
    return pl.pallas_call(
        gram_kernel,
        out_shape=[jax.ShapeDtypeStruct((4 * w, k), F32), jax.ShapeDtypeStruct((4 * w, 4 * w), F32)],
        in_specs=[SMEM] + [VM] * 4,
        out_specs=[VM] * 2,
        compiler_params=params(),
        cost_estimate=cost(),
        name="gram",
    )(at, *blocks)


def plain_gram_kernel(p_ref, g_ref):
    p = p_ref[...]
    g_ref[...] = dot(p, p, NT, HIGHEST)


def plain_gram(p_t):
    n = p_t.shape[0]
    return pl.pallas_call(
        plain_gram_kernel,
        out_shape=jax.ShapeDtypeStruct((n, n), F32),
        in_specs=[VM],
        out_specs=VM,
        compiler_params=params(),
        cost_estimate=cost(),
        name="gram",
    )(p_t)


def tile(x):
    return jnp.broadcast_to(x, (8, LANES))


def eliminate(rows):
    sub = lax.broadcasted_iota(jnp.int32, (8, LANES), 0)
    n = len(rows)
    scaled = []
    for g in range(n):
        cols = [[tile(rows[i][:, 8 * g + c : 8 * g + c + 1]) for i in range(g, n)] for c in range(8)]
        own = rows[g]
        pivots = jnp.ones((8, LANES), F32)
        factors, lines = [], []
        for c in range(8):
            pivot = tile(cols[c][0][c : c + 1, :])
            inv = 1.0 / pivot
            f = [x * inv for x in cols[c]]
            f[0] = jnp.where(sub > c, f[0], 0.0)
            pivots = jnp.where(sub == c, pivot, pivots)
            for later in range(c + 1, 8):
                e = tile(cols[later][0][c : c + 1, :])
                cols[later] = [x - y * e for x, y in zip(cols[later], f)]
            line = tile(own[c : c + 1, :])
            own = own - f[0] * line
            factors.append(f)
            lines.append(line)
        for i in range(g + 1, n):
            for c in range(8):
                rows[i] = rows[i] - factors[c][i - g] * lines[c]
        scaled.append(own * lax.rsqrt(pivots))
    return scaled


def factor_kernel(s_ref, *rest, first, last):
    left = s_ref.shape[0]
    if first:
        x_ref, *rest = rest
        j0 = lax.broadcasted_iota(jnp.int32, (left, left), 0)
        j1 = lax.broadcasted_iota(jnp.int32, (left, left), 1)
        right = (j0 == j1).astype(F32)
    else:
        r_ref, x_ref, *rest = rest
        right = r_ref[...]
    i0 = lax.broadcasted_iota(jnp.int32, (NB, NB), 0)
    i1 = lax.broadcasted_iota(jnp.int32, (NB, NB), 1)
    eye = (i0 == i1).astype(F32)
    augmented = jnp.concatenate([s_ref[:NB, :NB], eye], axis=1)
    rows = eliminate([augmented[8 * i : 8 * i + 8] for i in range(NB // 8)])
    inv = jnp.concatenate(rows, axis=0)[:, NB:]
    x = dot(inv, right[:NB, :], NN, HIGHEST)
    x_ref[...] = x
    if not last:
        s_out, r_out = rest
        u = dot(inv, s_ref[:NB, NB:], NN, HIGHEST)
        s_out[...] = s_ref[NB:, NB:] - dot(u, u, TN, HIGHEST)
        r_out[...] = right[NB:, :] - dot(u, x, TN, HIGHEST)


def factor_step(s, r=None):
    left = s.shape[0]
    n = left if r is None else r.shape[1]
    last = left == NB
    outs = [jax.ShapeDtypeStruct((NB, n), F32)]
    if not last:
        outs += [jax.ShapeDtypeStruct((left - NB, left - NB), F32), jax.ShapeDtypeStruct((left - NB, n), F32)]
    return pl.pallas_call(
        functools.partial(factor_kernel, first=r is None, last=last),
        out_shape=outs,
        in_specs=[VM] * (1 if r is None else 2),
        out_specs=[VM] * len(outs),
        compiler_params=params(),
        cost_estimate=cost(),
        name="factor",
    )(s, *(() if r is None else (r,)))


def finish_kernel(x0, x1, x2, x3, p_ref, lh_ref, ll_ref, qh_ref, ql_ref):
    linv = jnp.concatenate([x0[...], x1[...], x2[...], x3[...]], axis=0)
    lh_ref[...], ll_ref[...] = split(linv)
    qh_ref[...], ql_ref[...] = split(dot(linv, p_ref[...], NN, HIGHEST))


def finish(xs, p_t):
    n, k = p_t.shape
    return pl.pallas_call(
        finish_kernel,
        out_shape=[jax.ShapeDtypeStruct((n, n), BF16)] * 2 + [jax.ShapeDtypeStruct((n, k), BF16)] * 2,
        in_specs=[VM] * 5,
        out_specs=[VM] * 4,
        compiler_params=params(),
        cost_estimate=cost(),
        name="finish",
    )(*xs, p_t)


def update_kernel(at_ref, lh_ref, ll_ref, qh_ref, ql_ref, *refs, places, into):
    c_refs, t_ref = refs[: len(places)], refs[len(places)]
    p_out, r_out, p_buf, r_buf, sems = refs[len(places) + 1 + into :]
    b = p_buf.shape[1]
    half = t_ref.shape[0] // 2
    lh, ll, qh, ql = lh_ref[...], ll_ref[...], qh_ref[...], ql_ref[...]
    pending = []
    for c_ref, core in zip(c_refs, places):
        start = pl.multiple_of((at_ref[SIDE] ^ core) * half, 8)
        for i in range(c_ref.shape[0] // b):
            s = len(pending) % 2
            there = pl.ds(start + i * b, b)
            c_hi, c_lo = split(c_ref[i * b : (i + 1) * b, :])
            p = dot(c_hi, lh, NT) + dot(c_lo, lh, NT) + dot(c_hi, ll, NT)
            p_hi, p_lo = split(p)
            r = t_ref[there, :] - (dot(p_hi, qh, NN) + dot(p_lo, qh, NN) + dot(p_hi, ql, NN))
            if len(pending) >= 2:
                for c in pending[-2]:
                    c.wait()
            p_buf[s] = p
            r_buf[s] = r
            copies = [
                pltpu.make_async_copy(p_buf.at[s], p_out.at[there], sems.at[0, s]),
                pltpu.make_async_copy(r_buf.at[s], r_out.at[there], sems.at[1, s]),
            ]
            for c in copies:
                c.start()
            pending.append(copies)
    for copies in pending[-2:]:
        for c in copies:
            c.wait()


def update(at, parts, pieces, t, into=()):
    n, k = parts[2].shape
    m = t.shape[0]
    b = block_rows(next(iter(pieces.values())).shape[0])
    return pl.pallas_call(
        functools.partial(update_kernel, places=tuple(pieces), into=len(into)),
        out_shape=[jax.ShapeDtypeStruct((m, n), F32), jax.ShapeDtypeStruct((m, k), F32)],
        in_specs=[SMEM] + [VM] * (5 + len(pieces)) + [HBM] * len(into),
        out_specs=[HBM, HBM],
        scratch_shapes=[pltpu.VMEM((2, b, n), F32), pltpu.VMEM((2, b, k), F32), pltpu.SemaphoreType.DMA((2, 2))],
        input_output_aliases={6 + len(pieces) + i: i for i in range(len(into))},
        compiler_params=params(),
        cost_estimate=cost(),
        name="update",
    )(at, *parts, *pieces.values(), t, *into)


class Rows:
    def __init__(self, count):
        self.count = count
        bits = list(range(1, count.bit_length() - 1))
        self.stages = [(0, 0)] + list(zip(bits, bits[::-1]))

    def swap(self, x, stage):
        by_core = self.stages[stage]
        return lax.ppermute(x, "row", [(r, r ^ (1 << by_core[r & 1])) for r in range(self.count)])

    def place(self, nz):
        me, z = lax.axis_index("row"), lax.axis_index("col")

        def sides(r):
            return [jnp.where(r & 1 == 0, (r >> b0) & 1, (r >> b1) & 1) for b0, b1 in self.stages]

        own = sides(me)
        flags = [z, z & 1, z >> 1] if nz == 4 else [z, 0, 0]
        at = jnp.stack([jnp.asarray(x, jnp.int32) for x in flags + [sides(me ^ 1)[1]] + own])
        return at, [jnp.broadcast_to(s == 1, (1, LANES)) for s in [flags[2]] + own]


class Order:
    def __init__(self):
        self.last = None

    def gate(self, x):
        return x if self.last is None else lax.optimization_barrier((x, self.last))[0]

    def run(self, f, x, *args):
        out = f(self.gate(x), *args)
        self.last = out[0] if isinstance(out, (list, tuple)) else out
        return out


def pick(flag, x, y):
    flag = jnp.broadcast_to(flag[:, :1], x.shape)
    return jnp.where(flag, y, x), jnp.where(flag, x, y)


def per_device(shape, panel, trailing):
    rows = Rows(shape["row"])
    end = len(rows.stages) - 1
    nz = shape["col"]
    at, upper = rows.place(nz)
    p_first = panel.T
    panel, trailing, at, upper = lax.optimization_barrier((panel, trailing, at, upper))
    p_own, t = panel.T, trailing.T
    n = p_own.shape[0] * nz
    second, *upper = upper

    def halved(stage, x, *more):
        h = x.shape[0] // 2
        low, high = x[:h], x[h:]
        for y in more:
            low, high = low + y[:h], high + y[h:]
        return pick(upper[stage], low, high)

    def joined(stage, x, got):
        return jnp.concatenate(pick(upper[stage], x, got))

    o = Order()

    def send(x, stage):
        x = o.gate(x)
        o.last = x
        return rows.swap(x, stage)

    def add(x, y):
        return o.run(lambda x: x + y, x)

    def cut(stage, x, *more):
        return o.run(lambda x: halved(stage, x, *more), x)

    def put(stage, x, got):
        return o.run(lambda x: joined(stage, x, got), x)

    if nz == 4:
        def flipped(x, flip):
            return lax.ppermute(x, "col", [(z, z ^ flip) for z in range(nz)])

        pair, far = flipped(p_first, 1), flipped(p_own, 2)
        at, p_own, zero = touch(at, p_own, t)
        far = far + zero
        across = flipped(far, 1)
        o.last = far
        out_a, a = o.run(lambda x: cross(at, (False, True), x, pair, t), p_own)
        rest = (far, across)
    else:
        p_full = lax.all_gather(p_own, "col", axis=0, tiled=True)
        near, rest = [[p_full[i * (n // 4) : (i + 1) * (n // 4)] for i in h] for h in ((0, 1), (2, 3))]
        out_a, a = cross(at, (False, True), *near, t)
    if nz == 4:
        p_full, g = o.run(lambda x: gram4(at, x, pair, far, across), p_own)
        o.last = g
    else:
        g = o.run(plain_gram, p_full)
    g, out = cut(0, g)
    got_g = send(out, 0)
    got_a = send(out_a, 0)
    g = add(g, got_g)
    got_g = send(g, 1)
    a = add(a, got_a)
    got_a = send(a, 1)
    out_b, b = o.run(lambda x: cross(at, (False, True), x, rest[1], t), rest[0])
    for s in range(2, end + 1):
        g = add(g, got_g)
        got_g = send(g, s)
    got_b = send(out_b, 0)
    for s in range(2, end + 1):
        a = add(a, got_a)
        got_a = send(a, s)
    b = add(b, got_b)
    got_b = send(b, 1)
    g = add(g, got_g)
    g = put(0, g, send(g, 0))
    x0, g, r = o.run(factor_step, g)
    x1, g, r = o.run(factor_step, g, r)
    for s in range(2, end + 1):
        b = add(b, got_b)
        got_b = send(b, s)
    a = add(a, got_a)
    x2, g, r = o.run(factor_step, g, r)
    (x3,) = o.run(factor_step, g, r)
    parts = o.run(lambda x: finish((x0, x1, x2, x3), x), p_full)
    b = add(b, got_b)
    c = o.run(lambda x: jnp.concatenate(pick(second, a, x), axis=1), b)
    c_core = send(c, 0)
    outs = o.run(lambda x: update(at, parts, {0: x}, t), c)
    projections, r_t = o.run(lambda x: update(at, parts, {1: x}, t, outs), c_core)
    return projections, r_t.T


def solution(mesh):
    return jax.shard_map(
        functools.partial(per_device, dict(mesh.shape)),
        mesh=mesh,
        in_specs=(P("row", "col"), P("row", "col")),
        out_specs=(P("col", None), P("row", "col")),
        check_vma=False,
    )
```

time: 202 us -> 79.3 us (0.39)
  other arithmetic: 56.7 us -> 1.01 us
  waiting for transfers between devices: 71.5 us -> 24.9 us
  Pallas kernels: 0 us -> 31.6 us
  matrix products: 31 us -> 0 us
  blocking collectives: 21.5 us -> 0 us
  starting transfers between devices: 0.04 us -> 16 us
  between operations: 15.5 us -> 1.04 us
    psum x1 -> x0, waiting for transfers between devices: 71.4 us -> none  [per_device(): cross_terms = lax.psum(cross_rows(trailing, panel_full), 'row')]
    another operation x9 -> x0, other arithmetic: 53.9 us -> none  [the longest x6 34 us: per_device(): lower_factor = jnp.linalg.cholesky(panel_gram)]
    pallas_call x0 -> x11, Pallas kernels: none -> 31.6 us  [the longest x2 11.7 us: update(): pl.pallas_call(functools.partial(update_kernel, places=tuple(pieces), int...]
    ppermute x0 -> x14, waiting for transfers between devices: none -> 24.9 us  [the longest x11 20.7 us: swap(): lax.ppermute(x, 'row', [(r, r ^ 1 << by_core[r & 1]) for r in range(self....]
    dot_general x3 -> x0, matrix products: 23.3 us -> none  [the longest x2 12.7 us: cross_rows(): lax.dot_general(left, right, (((0,), (0,)), ((), ())), precision=lax.Prec...]
    all_gather x1 -> x0, blocking collectives: 21.5 us -> none  [per_device(): panel_full = lax.all_gather(panel, 'col', axis=1, tiled=True)]
    ppermute x0 -> x14, starting transfers between devices: none -> 16 us  [the longest x11 9.51 us: swap(): lax.ppermute(x, 'row', [(r, r ^ 1 << by_core[r & 1]) for r in range(self....]
    another operation x8 -> x0, matrix products: 7.73 us -> none  [the longest x6 7.25 us: solve_right(): jax.scipy.linalg.solve_triangular(lower_factor, terms.T, lower=True)]
  transfers between devices with their start and end apart: 1 -> 14, of which waited for: 1 -> 7; matrix products, arithmetic and copies ran while one was open for 0% -> 1% of each run, Pallas kernels for 0% -> 31%
where the time goes in v2:
time: 79.3 us; the launch traced here: 79.2 us
  Pallas kernels  31.6 us (40%)
  waiting for transfers between devices  24.9 us (31%)
  starting transfers between devices  16 us (20%)
  local copies, waits for them, and re-layouts  4.65 us (6%)
  between operations  1.04 us (1%)
  other arithmetic  1.01 us (1%)
    ppermute x11, waiting for transfers between devices, swap(): lax.ppermute(x, 'row', [(r, r ^ 1 << by_core[r & 1]) for r in range(self....  20.7 us
    pallas_call x2, Pallas kernels, update(): pl.pallas_call(functools.partial(update_kernel, places=tuple(pieces), int...  11.7 us
    pallas_call x4, Pallas kernels, factor_step(): pl.pallas_call(functools.partial(factor_kernel, first=r is None, last=las...  10.1 us
    ppermute x11, starting transfers between devices, swap(): lax.ppermute(x, 'row', [(r, r ^ 1 << by_core[r & 1]) for r in range(self....  9.51 us
    ppermute x3, starting transfers between devices, flipped(): return lax.ppermute(x, 'col', [(z, z ^ flip) for z in range(nz)])  6.46 us
    pallas_call x2, Pallas kernels, cross(): pl.pallas_call(functools.partial(cross_kernel, mine=mine), out_shape=[jax...  6.41 us
    unnamed x6, local copies, waits for them, and re-layouts  4.55 us
    ppermute x3, waiting for transfers between devices, flipped(): return lax.ppermute(x, 'col', [(z, z ^ flip) for z in range(nz)])  4.24 us
  transfers between devices with their start and end apart: 14, of which 7 were waited for; matrix products, arithmetic and copies ran while one was open for 1% of the time, Pallas kernels for 31%

profile of v2, /device:TPU:0, one launch (start us, length us, event | category | flops | bytes accessed | tf_op | source)
XLA Modules:
  0.0 79.2 jit_solution(3270920280169551821)
XLA Ops:
  0.7 0.1 stack.31.at_ref
  0.8 4.1 %collective-permute-start = (f32[64,768]{1,0:T(8,128)}, f32[64,768]{1,0:T(8,128)S(1)}, u32[]{:S(2)}, u32[]{:S(2)}) collective-permute-start(f32[64,768]{1,0:T(8,128)} %bitcast.20), channel_id=1, source_target_pairs={{0,2},{1,3},{2,0},{3,1},{4,6},{5,7},{6,4},{7,5},{8,10},{9,11},{10,... | collective-permute-start | bytes 589832 | tf_op jit(solution)/shard_map/ppermute | solution.py:361
  4.9 1.6 %collective-permute-start.1 = (f32[64,768]{1,0:T(8,128)}, f32[64,768]{1,0:T(8,128)S(1)}, u32[]{:S(2)}, u32[]{:S(2)}) collective-permute-start(f32[64,768]{1,0:T(8,128)} %bitcast.21), channel_id=1, source_target_pairs={{0,1},{1,0},{2,3},{3,2},{4,5},{5,4},{6,7},{7,6},{8,9},{9,8},{10,11... | collective-permute-start | bytes 589832 | tf_op jit(solution)/shard_map/ppermute | solution.py:361
  6.4 0.0 copy-start
  6.4 3.6 %copy-done = f32[768,3008]{0,1:T(8,128)S(1)} copy-done((f32[768,3008]{0,1:T(8,128)S(1)}, f32[768,3008]{0,1:T(8,128)}, u32[]{:S(2)}) %copy-start) | copy-done | bytes 9240600
  10.1 0.0 copy-start.2
  10.1 0.9 %copy-done.2 = f32[768,64]{0,1:T(8,128)S(1)} copy-done((f32[768,64]{0,1:T(8,128)S(1)}, f32[768,64]{0,1:T(8,128)}, u32[]{:S(2)}) %copy-start.2) | copy-done | bytes 196632
  11.0 0.0 copy-start.1
  11.0 1.1 %touch.1 = (s32[7]{0:T(128)S(1)}, f32[64,768]{1,0:T(8,128)S(1)}, f32[64,768]{1,0:T(8,128)S(1)}) custom-call(s32[7]{0:T(128)S(1)} %stack.31.at_ref, f32[64,768]{1,0:T(8,128)S(1)} %bitcast.22, f32[3008,768]{1,0:T(8,128)S(1)} %bitcast.15), custom_call_target="tpu_custom_call" | custom-call | tf_op jit(solution)/shard_map/touch/pallas_call | solution.py:57
  12.1 2.2 %collective-permute-done = f32[64,768]{1,0:T(8,128)S(1)} collective-permute-done((f32[64,768]{1,0:T(8,128)}, f32[64,768]{1,0:T(8,128)S(1)}, u32[]{:S(2)}, u32[]{:S(2)}) %collective-permute-start) | collective-permute-done | bytes 196640 | tf_op jit(solution)/shard_map/ppermute | solution.py:361
  14.3 0.8 collective-permute-start.2
  15.1 0.0 collective-permute-done.1.pb_ref.pair
  15.1 0.0 copy-done.1
  15.1 3.2 %cross.2 = (f32[1504,128]{1,0:T(8,128)S(1)}, f32[1504,128]{1,0:T(8,128)S(1)}) custom-call(s32[7]{0:T(128)S(1)} %get-tuple-element.66.at_ref, f32[64,768]{1,0:T(8,128)S(1)} %get-tuple-element.72.pa_ref.own, f32[64,768]{1,0:T(8,128)S(1)} %collective-permute-done.1.pb_ref.pair, f32[3008,768]{1,0:T(8,128)S(1)} %bitcast.16), custom_call_target="tpu_custom_call" | custom-call | tf_op jit(solution)/shard_map/cross/pallas_call | solution.py:86
  18.3 2.1 %collective-permute-done.2.across.pb_ref = f32[64,768]{1,0:T(8,128)S(1)} collective-permute-done((f32[64,768]{1,0:T(8,128)S(1)}, f32[64,768]{1,0:T(8,128)S(1)}, u32[]{:S(2)}, u32[]{:S(2)}) %collective-permute-start.2) | collective-permute-done | bytes 196640 | tf_op jit(solution)/shard_map/ppermute | solution.py:361
  20.4 1.4 %gram.1 = (f32[256,768]{1,0:T(8,128)S(1)}, f32[256,256]{1,0:T(8,128)S(1)}) custom-call(s32[7]{0:T(128)S(1)} %get-tuple-element.66.at_ref, f32[64,768]{1,0:T(8,128)S(1)} %get-tuple-element.72.pa_ref.own, f32[64,768]{1,0:T(8,128)S(1)} %collective-permute-done.1.pb_ref.pair, f32[64,768]{1,0:T(8,128)S(1)} %add.30.far.pa_ref, ...), custom_call_target="tpu_custom_call" | custom-call | tf_op jit(solution)/shard_map/gram/pallas_call | solution.py:108
  21.9 0.1 slice_select_fusion
  21.9 0.1 collective-permute-start.4
  22.0 0.5 collective-permute-start.3
  22.5 1.9 %collective-permute-done.3 = f32[128,256]{1,0:T(8,128)S(1)} collective-permute-done((f32[128,256]{1,0:T(8,128)S(1)}, f32[128,256]{1,0:T(8,128)S(1)}, u32[]{:S(2)}, u32[]{:S(2)}) %collective-permute-start.3) | collective-permute-done | bytes 131104 | tf_op jit(solution)/shard_map/ppermute | solution.py:290
  24.4 1.3 %collective-permute-start.5 = (f32[128,256]{1,0:T(8,128)S(1)}, f32[128,256]{1,0:T(8,128)S(1)}, u32[]{:S(2)}, u32[]{:S(2)}) collective-permute-start(f32[128,256]{1,0:T(8,128)S(1)} %add.31), channel_id=1, source_target_pairs={{0,8},{4,20},{8,0},{12,28},{16,24},{20,4},{24,16},{28,12},{1,9},{5... | collective-permute-start | bytes 393224 | tf_op jit(solution)/shard_map/ppermute | solution.py:290
  25.8 0.0 collective-permute-done.4
  25.8 0.1 add.32
  25.9 0.8 %collective-permute-start.6 = (f32[1504,128]{1,0:T(8,128)S(1)}, f32[1504,128]{1,0:T(8,128)S(1)}, u32[]{:S(2)}, u32[]{:S(2)}) collective-permute-start(f32[1504,128]{1,0:T(8,128)S(1)} %add.32), channel_id=1, source_target_pairs={{0,8},{4,20},{8,0},{12,28},{16,24},{20,4},{24,16},{28,12},{1,9},{5... | collective-permute-start | bytes 2310152 | tf_op jit(solution)/shard_map/ppermute | solution.py:290
  26.7 3.2 %cross.3 = (f32[1504,128]{1,0:T(8,128)S(1)}, f32[1504,128]{1,0:T(8,128)S(1)}) custom-call(s32[7]{0:T(128)S(1)} %get-tuple-element.66.at_ref, f32[64,768]{1,0:T(8,128)S(1)} %add.30.far.pa_ref, f32[64,768]{1,0:T(8,128)S(1)} %collective-permute-done.2.across.pb_ref, f32[3008,768]{1,0:T(8,128)S(1)} %bitcast.17), custom_call_target="tpu_custom_call" | custom-call | tf_op jit(solution)/shard_map/cross/pallas_call | solution.py:86
  29.9 0.0 collective-permute-done.5
  29.9 0.1 collective-permute-start.7
  30.0 7.7 %collective-permute-done.6 = f32[1504,128]{1,0:T(8,128)S(1)} collective-permute-done((f32[1504,128]{1,0:T(8,128)S(1)}, f32[1504,128]{1,0:T(8,128)S(1)}, u32[]{:S(2)}, u32[]{:S(2)}) %collective-permute-start.6) | collective-permute-done | bytes 770080 | tf_op jit(solution)/shard_map/ppermute | solution.py:290
  37.7 0.1 add.34
  37.8 0.0 collective-permute-done.7
  37.8 0.1 add.35
  37.9 1.3 %collective-permute-start.10 = (f32[1504,128]{1,0:T(8,128)S(1)}, f32[1504,128]{1,0:T(8,128)S(1)}, u32[]{:S(2)}, u32[]{:S(2)}) collective-permute-start(f32[1504,128]{1,0:T(8,128)S(1)} %add.35), channel_id=1, source_target_pairs={{0,8},{4,20},{8,0},{12,28},{16,24},{20,4},{24,16},{28,12},{1,9},{5... | collective-permute-start | bytes 2310152 | tf_op jit(solution)/shard_map/ppermute | solution.py:290
  39.2 1.5 %collective-permute-start.8 = (f32[128,256]{1,0:T(8,128)S(1)}, f32[128,256]{1,0:T(8,128)S(1)}, u32[]{:S(2)}, u32[]{:S(2)}) collective-permute-start(f32[128,256]{1,0:T(8,128)S(1)} %add.33), channel_id=1, source_target_pairs={{0,16},{4,12},{8,24},{12,4},{16,0},{20,28},{24,8},{28,20},{1,17},{... | collective-permute-start | bytes 393224 | tf_op jit(solution)/shard_map/ppermute | solution.py:290
  40.8 4.9 %collective-permute-done.8 = f32[128,256]{1,0:T(8,128)S(1)} collective-permute-done((f32[128,256]{1,0:T(8,128)S(1)}, f32[128,256]{1,0:T(8,128)S(1)}, u32[]{:S(2)}, u32[]{:S(2)}) %collective-permute-start.8) | collective-permute-done | bytes 131104 | tf_op jit(solution)/shard_map/ppermute | solution.py:290
  45.7 0.1 collective-permute-start.9
  45.8 1.6 %collective-permute-start.11 = (f32[1504,128]{1,0:T(8,128)S(1)}, f32[1504,128]{1,0:T(8,128)S(1)}, u32[]{:S(2)}, u32[]{:S(2)}) collective-permute-start(f32[1504,128]{1,0:T(8,128)S(1)} %add.34), channel_id=1, source_target_pairs={{0,16},{4,12},{8,24},{12,4},{16,0},{20,28},{24,8},{28,20},{1,17},{... | collective-permute-start | bytes 2310152 | tf_op jit(solution)/shard_map/ppermute | solution.py:290
  47.4 0.0 collective-permute-done.9
  47.4 0.1 broadcast_select_fusion.3
  47.5 2.8 %factor.4 = (f32[64,256]{1,0:T(8,128)S(1)}, f32[192,192]{1,0:T(8,128)S(1)}, f32[192,256]{1,0:T(8,128)S(1)}) custom-call(f32[256,256]{1,0:T(8,128)S(1)} %pad_maximum_fusion.1.s_ref), custom_call_target="tpu_custom_call" | custom-call | tf_op jit(solution)/shard_map/factor/pallas_call | solution.py:202
  50.2 2.6 %factor.5 = (f32[64,256]{1,0:T(8,128)S(1)}, f32[128,128]{1,0:T(8,128)S(1)}, f32[128,256]{1,0:T(8,128)S(1)}) custom-call(f32[192,192]{1,0:T(8,128)S(1)} %get-tuple-element.96.s_ref, f32[192,256]{1,0:T(8,128)S(1)} %get-tuple-element.97.rest_0_), custom_call_target="tpu_custom_call" | custom-call | tf_op jit(solution)/shard_map/factor/pallas_call | solution.py:202
  52.8 0.0 collective-permute-done.10
  52.8 0.1 add.37
  52.9 1.3 %collective-permute-start.12 = (f32[1504,128]{1,0:T(8,128)S(1)}, f32[1504,128]{1,0:T(8,128)S(1)}, u32[]{:S(2)}, u32[]{:S(2)}) collective-permute-start(f32[1504,128]{1,0:T(8,128)S(1)} %add.37), channel_id=1, source_target_pairs={{0,16},{4,12},{8,24},{12,4},{16,0},{20,28},{24,8},{28,20},{1,17},{... | collective-permute-start | bytes 2310152 | tf_op jit(solution)/shard_map/ppermute | solution.py:290
  54.3 3.5 %collective-permute-done.11 = f32[1504,128]{1,0:T(8,128)S(1)} collective-permute-done((f32[1504,128]{1,0:T(8,128)S(1)}, f32[1504,128]{1,0:T(8,128)S(1)}, u32[]{:S(2)}, u32[]{:S(2)}) %collective-permute-start.11) | collective-permute-done | bytes 770080 | tf_op jit(solution)/shard_map/ppermute | solution.py:290
  57.8 0.1 add.38
  57.8 2.7 %factor.6 = (f32[64,256]{1,0:T(8,128)S(1)}, f32[64,64]{1,0:T(8,128)S(1)}, f32[64,256]{1,0:T(8,128)S(1)}) custom-call(f32[128,128]{1,0:T(8,128)S(1)} %get-tuple-element.103.s_ref, f32[128,256]{1,0:T(8,128)S(1)} %get-tuple-element.104.rest_0_), custom_call_target="tpu_custom_call" | custom-call | tf_op jit(solution)/shard_map/factor/pallas_call | solution.py:202
  60.5 2.1 %factor.7.x3 = f32[64,256]{1,0:T(8,128)S(1)} custom-call(f32[64,64]{1,0:T(8,128)S(1)} %get-tuple-element.107.s_ref, f32[64,256]{1,0:T(8,128)S(1)} %get-tuple-element.108.rest_0_), custom_call_target="tpu_custom_call" | custom-call | tf_op jit(solution)/shard_map/factor/pallas_call | solution.py:202
  62.6 0.8 %finish.1 = (bf16[256,256]{1,0:T(8,128)(2,1)S(1)}, bf16[256,256]{1,0:T(8,128)(2,1)S(1)}, bf16[256,768]{1,0:T(8,128)(2,1)S(1)}, bf16[256,768]{1,0:T(8,128)(2,1)S(1)}) custom-call(f32[64,256]{1,0:T(8,128)S(1)} %get-tuple-element.94.x0, f32[64,256]{1,0:T(8,128)S(1)} %get-tuple-element.98.x1, f32[64,256]{1,0:T(8,128)S(1)} %get-tuple-element.105.x2, ...), custom_call_target="tpu_custom_call" | custom-call | tf_op jit(solution)/shard_map/finish/pallas_call | solution.py:221
  63.4 2.6 %collective-permute-done.12 = f32[1504,128]{1,0:T(8,128)S(1)} collective-permute-done((f32[1504,128]{1,0:T(8,128)S(1)}, f32[1504,128]{1,0:T(8,128)S(1)}, u32[]{:S(2)}, u32[]{:S(2)}) %collective-permute-start.12) | collective-permute-done | bytes 770080 | tf_op jit(solution)/shard_map/ppermute | solution.py:290
  66.0 0.1 add.39
  66.1 0.2 broadcast_select_fusion.1
  66.3 0.1 pad_maximum_fusion.refs_0_
  66.4 0.9 %collective-permute-start.13 = (f32[1504,256]{1,0:T(8,128)S(1)}, f32[1504,256]{1,0:T(8,128)S(1)}, u32[]{:S(2)}, u32[]{:S(2)}) collective-permute-start(f32[1504,256]{1,0:T(8,128)S(1)} %pad_maximum_fusion.refs_0_), channel_id=1, source_target_pairs={{0,4},{4,0},{8,12},{12,8},{16,20},{20,16},{24,28},{28,24},{1,5},{5... | collective-permute-start | bytes 4620296 | tf_op jit(solution)/shard_map/ppermute | solution.py:290
  67.3 5.8 %update.2 = (f32[3008,256]{1,0:T(8,128)}, f32[3008,768]{1,0:T(8,128)}) custom-call(s32[7]{0:T(128)S(1)} %get-tuple-element.66.at_ref, bf16[256,256]{1,0:T(8,128)(2,1)S(1)} %get-tuple-element.111.lh_ref, bf16[256,256]{1,0:T(8,128)(2,1)S(1)} %get-tuple-element.112.ll_ref, bf16[256,768]{1,0:T(8,128)(2,1)S(1)} %get-tuple-element.113.qh_ref, ...), custom_call_target="tpu_custom_call" | custom-call | tf_op jit(solution)/shard_map/update/pallas_call | solution.py:269
  73.2 0.0 collective-permute-done.13.refs_0_
  73.2 5.8 %update.3 = (f32[3008,256]{1,0:T(8,128)}, f32[3008,768]{1,0:T(8,128)}) custom-call(s32[7]{0:T(128)S(1)} %get-tuple-element.66.at_ref, bf16[256,256]{1,0:T(8,128)(2,1)S(1)} %get-tuple-element.111.lh_ref, bf16[256,256]{1,0:T(8,128)(2,1)S(1)} %get-tuple-element.112.ll_ref, ...), custom_call_target="tpu_custom_call", output_to_operand_aliasing={{0}: (7, {}), {1}: (8, {})} | custom-call | tf_op jit(solution)/shard_map/update/pallas_call | solution.py:269
  (7 shorter events, 0.1 us)
Async XLA Ops:
  0.8 13.5 %collective-permute-start = (f32[64,768]{1,0:T(8,128)}, f32[64,768]{1,0:T(8,128)S(1)}, u32[]{:S(2)}, u32[]{:S(2)}) collective-permute-start(f32[64,768]{1,0:T(8,128)} %bitcast.20), channel_id=1, source_target_pairs={{0,2},{1,3},{2,0},{3,1},{4,6},{5,7},{6,4},{7,5},{8,10},{9,11},{10,... | collective-permute-start | bytes 589832 | tf_op jit(solution)/shard_map/ppermute | solution.py:361
  4.9 10.2 %collective-permute-start.1 = (f32[64,768]{1,0:T(8,128)}, f32[64,768]{1,0:T(8,128)S(1)}, u32[]{:S(2)}, u32[]{:S(2)}) collective-permute-start(f32[64,768]{1,0:T(8,128)} %bitcast.21), channel_id=1, source_target_pairs={{0,1},{1,0},{2,3},{3,2},{4,5},{5,4},{6,7},{7,6},{8,9},{9,8},{10,11... | collective-permute-start | bytes 589832 | tf_op jit(solution)/shard_map/ppermute | solution.py:361
  6.4 3.6 %copy-start = (f32[768,3008]{0,1:T(8,128)S(1)}, f32[768,3008]{0,1:T(8,128)}, u32[]{:S(2)}) copy-start(f32[768,3008]{0,1:T(8,128)} %param.3) | copy-start | bytes 27721732
  10.1 0.9 %copy-start.2 = (f32[768,64]{0,1:T(8,128)S(1)}, f32[768,64]{0,1:T(8,128)}, u32[]{:S(2)}) copy-start(f32[768,64]{0,1:T(8,128)} %param.2) | copy-start | bytes 589828
  11.0 4.1 %copy-start.1 = (f32[768,3008]{0,1:T(8,128)S(1)}, f32[768,3008]{0,1:T(8,128)}, u32[]{:S(2)}) copy-start(f32[768,3008]{0,1:T(8,128)} %param.3) | copy-start | bytes 27721732
  14.3 6.1 %collective-permute-start.2 = (f32[64,768]{1,0:T(8,128)S(1)}, f32[64,768]{1,0:T(8,128)S(1)}, u32[]{:S(2)}, u32[]{:S(2)}) collective-permute-start(f32[64,768]{1,0:T(8,128)S(1)} %add.30.far.pa_ref), channel_id=1, source_target_pairs={{0,1},{1,0},{2,3},{3,2},{4,5},{5,4},{6,7},{7,6},{8,9},{9,8},{10,11... | collective-permute-start | bytes 589832 | tf_op jit(solution)/shard_map/ppermute | solution.py:361
  21.9 3.9 %collective-permute-start.4 = (f32[1504,128]{1,0:T(8,128)S(1)}, f32[1504,128]{1,0:T(8,128)S(1)}, u32[]{:S(2)}, u32[]{:S(2)}) collective-permute-start(f32[1504,128]{1,0:T(8,128)S(1)} %get-tuple-element.75), channel_id=1, source_target_pairs={{0,4},{4,0},{8,12},{12,8},{16,20},{20,16},{24,28},{28,24},{1,5},{5... | collective-permute-start | bytes 2310152 | tf_op jit(solution)/shard_map/ppermute | solution.py:290
  22.0 2.4 %collective-permute-start.3 = (f32[128,256]{1,0:T(8,128)S(1)}, f32[128,256]{1,0:T(8,128)S(1)}, u32[]{:S(2)}, u32[]{:S(2)}) collective-permute-start(f32[128,256]{1,0:T(8,128)S(1)} %get-tuple-element.74), channel_id=1, source_target_pairs={{0,4},{4,0},{8,12},{12,8},{16,20},{20,16},{24,28},{28,24},{1,5},{5... | collective-permute-start | bytes 393224 | tf_op jit(solution)/shard_map/ppermute | solution.py:290
  24.4 5.4 %collective-permute-start.5 = (f32[128,256]{1,0:T(8,128)S(1)}, f32[128,256]{1,0:T(8,128)S(1)}, u32[]{:S(2)}, u32[]{:S(2)}) collective-permute-start(f32[128,256]{1,0:T(8,128)S(1)} %add.31), channel_id=1, source_target_pairs={{0,8},{4,20},{8,0},{12,28},{16,24},{20,4},{24,16},{28,12},{1,9},{5... | collective-permute-start | bytes 393224 | tf_op jit(solution)/shard_map/ppermute | solution.py:290
  25.9 11.9 %collective-permute-start.6 = (f32[1504,128]{1,0:T(8,128)S(1)}, f32[1504,128]{1,0:T(8,128)S(1)}, u32[]{:S(2)}, u32[]{:S(2)}) collective-permute-start(f32[1504,128]{1,0:T(8,128)S(1)} %add.32), channel_id=1, source_target_pairs={{0,8},{4,20},{8,0},{12,28},{16,24},{20,4},{24,16},{28,12},{1,9},{5... | collective-permute-start | bytes 2310152 | tf_op jit(solution)/shard_map/ppermute | solution.py:290
  29.9 7.9 %collective-permute-start.7 = (f32[1504,128]{1,0:T(8,128)S(1)}, f32[1504,128]{1,0:T(8,128)S(1)}, u32[]{:S(2)}, u32[]{:S(2)}) collective-permute-start(f32[1504,128]{1,0:T(8,128)S(1)} %get-tuple-element.86), channel_id=1, source_target_pairs={{0,4},{4,0},{8,12},{12,8},{16,20},{20,16},{24,28},{28,24},{1,5},{5... | collective-permute-start | bytes 2310152 | tf_op jit(solution)/shard_map/ppermute | solution.py:290
  37.9 14.9 %collective-permute-start.10 = (f32[1504,128]{1,0:T(8,128)S(1)}, f32[1504,128]{1,0:T(8,128)S(1)}, u32[]{:S(2)}, u32[]{:S(2)}) collective-permute-start(f32[1504,128]{1,0:T(8,128)S(1)} %add.35), channel_id=1, source_target_pairs={{0,8},{4,20},{8,0},{12,28},{16,24},{20,4},{24,16},{28,12},{1,9},{5... | collective-permute-start | bytes 2310152 | tf_op jit(solution)/shard_map/ppermute | solution.py:290
  39.2 6.4 %collective-permute-start.8 = (f32[128,256]{1,0:T(8,128)S(1)}, f32[128,256]{1,0:T(8,128)S(1)}, u32[]{:S(2)}, u32[]{:S(2)}) collective-permute-start(f32[128,256]{1,0:T(8,128)S(1)} %add.33), channel_id=1, source_target_pairs={{0,16},{4,12},{8,24},{12,4},{16,0},{20,28},{24,8},{28,20},{1,17},{... | collective-permute-start | bytes 393224 | tf_op jit(solution)/shard_map/ppermute | solution.py:290
  45.7 1.7 %collective-permute-start.9 = (f32[128,256]{1,0:T(8,128)S(1)}, f32[128,256]{1,0:T(8,128)S(1)}, u32[]{:S(2)}, u32[]{:S(2)}) collective-permute-start(f32[128,256]{1,0:T(8,128)S(1)} %add.36), channel_id=1, source_target_pairs={{0,4},{4,0},{8,12},{12,8},{16,20},{20,16},{24,28},{28,24},{1,5},{5... | collective-permute-start | bytes 393224 | tf_op jit(solution)/shard_map/ppermute | solution.py:290
  45.8 12.0 %collective-permute-start.11 = (f32[1504,128]{1,0:T(8,128)S(1)}, f32[1504,128]{1,0:T(8,128)S(1)}, u32[]{:S(2)}, u32[]{:S(2)}) collective-permute-start(f32[1504,128]{1,0:T(8,128)S(1)} %add.34), channel_id=1, source_target_pairs={{0,16},{4,12},{8,24},{12,4},{16,0},{20,28},{24,8},{28,20},{1,17},{... | collective-permute-start | bytes 2310152 | tf_op jit(solution)/shard_map/ppermute | solution.py:290
  52.9 13.1 %collective-permute-start.12 = (f32[1504,128]{1,0:T(8,128)S(1)}, f32[1504,128]{1,0:T(8,128)S(1)}, u32[]{:S(2)}, u32[]{:S(2)}) collective-permute-start(f32[1504,128]{1,0:T(8,128)S(1)} %add.37), channel_id=1, source_target_pairs={{0,16},{4,12},{8,24},{12,4},{16,0},{20,28},{24,8},{28,20},{1,17},{... | collective-permute-start | bytes 2310152 | tf_op jit(solution)/shard_map/ppermute | solution.py:290
  66.4 6.7 %collective-permute-start.13 = (f32[1504,256]{1,0:T(8,128)S(1)}, f32[1504,256]{1,0:T(8,128)S(1)}, u32[]{:S(2)}, u32[]{:S(2)}) collective-permute-start(f32[1504,256]{1,0:T(8,128)S(1)} %pad_maximum_fusion.refs_0_), channel_id=1, source_target_pairs={{0,4},{4,0},{8,12},{12,8},{16,20},{20,16},{24,28},{28,24},{1,5},{5... | collective-permute-start | bytes 4620296 | tf_op jit(solution)/shard_map/ppermute | solution.py:290

commit v3 on v2

--- a/solution.py
+++ b/solution.py
@@ -11,7 +11,7 @@
 HIGHEST = lax.Precision.HIGHEST
 NT, NN, TN = ((1,), (1,)), ((1,), (0,)), ((0,), (0,))
 LANES, NB = 128, 64
-VMEM_LIMIT = 12 * 2**20
+VMEM_LIMIT = 16 * 2**20
 
 
 def dot(a, b, dims, precision=None):
@@ -229,54 +229,79 @@
     )(*xs, p_t)
 
 
-def update_kernel(at_ref, lh_ref, ll_ref, qh_ref, ql_ref, *refs, places, into):
-    c_refs, t_ref = refs[: len(places)], refs[len(places)]
-    p_out, r_out, p_buf, r_buf, sems = refs[len(places) + 1 + into :]
-    b = p_buf.shape[1]
-    half = t_ref.shape[0] // 2
+def quarter_start(at_ref, place, rows):
+    core, chip = place
+    side = at_ref[OTHER if core else SIDE + 1]
+    return pl.multiple_of((at_ref[SIDE] ^ core) * (rows // 2) + (side ^ chip) * (rows // 4), 8)
+
+
+def update_kernel(at_ref, lh_ref, ll_ref, qh_ref, ql_ref, *refs, places, carried, into, last):
+    c_refs, refs = refs[: len(places)], refs[len(places) :]
+    t_ref, refs = refs[0], refs[1:]
+    carry, refs = (refs[:2], refs[2:]) if carried else ((), refs)
+    outs = refs[into:]
+    rows = t_ref.shape[0]
+    copies = []
+    if last:
+        p_out, r_out, *outs = outs
+        sems = refs[-1]
+    if carried:
+        m = carry[0].shape[0] // len(carried)
+        for j, place in enumerate(carried):
+            here, there = pl.ds(j * m, m), pl.ds(quarter_start(at_ref, place, rows), m)
+            copies += [
+                pltpu.make_async_copy(carry[0].at[here], p_out.at[there], sems.at[0, j]),
+                pltpu.make_async_copy(carry[1].at[here], r_out.at[there], sems.at[1, j]),
+            ]
+        for c in copies:
+            c.start()
+    p_here, r_here = outs[:2]
     lh, ll, qh, ql = lh_ref[...], ll_ref[...], qh_ref[...], ql_ref[...]
-    pending = []
-    for c_ref, core in zip(c_refs, places):
-        start = pl.multiple_of((at_ref[SIDE] ^ core) * half, 8)
-        for i in range(c_ref.shape[0] // b):
-            s = len(pending) % 2
-            there = pl.ds(start + i * b, b)
+    m = c_refs[0].shape[0]
+    b = m // 2 if last and m % 16 == 0 else m
+    for j, (c_ref, place) in enumerate(zip(c_refs, places)):
+        start = quarter_start(at_ref, place, rows)
+        for i in range(m // b):
+            here, there = pl.ds(j * m + i * b, b), pl.ds(start + i * b, b)
             c_hi, c_lo = split(c_ref[i * b : (i + 1) * b, :])
             p = dot(c_hi, lh, NT) + dot(c_lo, lh, NT) + dot(c_hi, ll, NT)
+            p_here[here, :] = p
             p_hi, p_lo = split(p)
-            r = t_ref[there, :] - (dot(p_hi, qh, NN) + dot(p_lo, qh, NN) + dot(p_hi, ql, NN))
-            if len(pending) >= 2:
-                for c in pending[-2]:
-                    c.wait()
-            p_buf[s] = p
-            r_buf[s] = r
-            copies = [
-                pltpu.make_async_copy(p_buf.at[s], p_out.at[there], sems.at[0, s]),
-                pltpu.make_async_copy(r_buf.at[s], r_out.at[there], sems.at[1, s]),
-            ]
-            for c in copies:
-                c.start()
-            pending.append(copies)
-    for copies in pending[-2:]:
-        for c in copies:
-            c.wait()
-
-
-def update(at, parts, pieces, t, into=()):
+            r_here[here, :] = t_ref[there, :] - (dot(p_hi, qh, NN) + dot(p_lo, qh, NN) + dot(p_hi, ql, NN))
+            if last:
+                s = len(carried) + j * (m // b) + i
+                copies += [
+                    pltpu.make_async_copy(p_here.at[here], p_out.at[there], sems.at[0, s]),
+                    pltpu.make_async_copy(r_here.at[here], r_out.at[there], sems.at[1, s]),
+                ]
+                for c in copies[-2:]:
+                    c.start()
+    for c in copies:
+        c.wait()
+
+
+def update(at, parts, pieces, t, carried=(), carry=(), into=(), last=True):
     n, k = parts[2].shape
     m = t.shape[0]
-    b = block_rows(next(iter(pieces.values())).shape[0])
-    return pl.pallas_call(
-        functools.partial(update_kernel, places=tuple(pieces), into=len(into)),
-        out_shape=[jax.ShapeDtypeStruct((m, n), F32), jax.ShapeDtypeStruct((m, k), F32)],
-        in_specs=[SMEM] + [VM] * (5 + len(pieces)) + [HBM] * len(into),
-        out_specs=[HBM, HBM],
-        scratch_shapes=[pltpu.VMEM((2, b, n), F32), pltpu.VMEM((2, b, k), F32), pltpu.SemaphoreType.DMA((2, 2))],
-        input_output_aliases={6 + len(pieces) + i: i for i in range(len(into))},
+    h = sum(x.shape[0] for x in pieces.values())
+    own = [((h, n), F32), ((h, k), F32)]
+    if last:
+        out = [jax.ShapeDtypeStruct((m, n), F32), jax.ShapeDtypeStruct((m, k), F32)]
+        scratch = [pltpu.VMEM(*x) for x in own] + [pltpu.SemaphoreType.DMA((2, len(carried) + 2 * len(pieces)))]
+    else:
+        out, scratch = [jax.ShapeDtypeStruct(*x) for x in own], []
+    inputs = [at, *parts, *pieces.values(), t, *carry]
+    return pl.pallas_call(
+        functools.partial(update_kernel, places=tuple(pieces), carried=carried, into=len(into), last=last),
+        out_shape=out,
+        in_specs=[SMEM] + [VM] * (len(inputs) - 1) + [HBM] * len(into),
+        out_specs=[HBM if last else VM] * 2,
+        scratch_shapes=scratch,
+        input_output_aliases={len(inputs) + i: i for i in range(len(into))},
         compiler_params=params(),
         cost_estimate=cost(),
         name="update",
-    )(at, *parts, *pieces.values(), t, *into)
+    )(*inputs, *into)
 
 
 class Rows:
@@ -355,6 +380,9 @@
 
     def put(stage, x, got):
         return o.run(lambda x: joined(stage, x, got), x)
+
+    def columns(x, y):
+        return o.run(lambda y: jnp.concatenate(pick(second, x, y), axis=1), y)
 
     if nz == 4:
         def flipped(x, flip):
@@ -380,35 +408,49 @@
     got_g = send(out, 0)
     got_a = send(out_a, 0)
     g = add(g, got_g)
-    got_g = send(g, 1)
-    a = add(a, got_a)
-    got_a = send(a, 1)
+    got_g = send(g, end)
+    a, out_a = cut(1, a, got_a)
+    got_a = send(out_a, 1)
     out_b, b = o.run(lambda x: cross(at, (False, True), x, rest[1], t), rest[0])
-    for s in range(2, end + 1):
+    for s in range(end - 1, 0, -1):
         g = add(g, got_g)
         got_g = send(g, s)
-    got_b = send(out_b, 0)
-    for s in range(2, end + 1):
-        a = add(a, got_a)
-        got_a = send(a, s)
+    for s in range(2, end):
+        a, out_a = cut(s, a, got_a)
+        got_a = send(out_a, s)
+    a = add(a, got_a)
+    got_a = send(a, end)
+    b, out_b = cut(1, b, send(out_b, 0))
+    got_b = send(out_b, 1)
+    a = add(a, got_a)
+    for s in range(end - 1, 1, -1):
+        a = put(s, a, send(a, s))
+    for s in range(2, end):
+        b, out_b = cut(s, b, got_b)
+        got_b = send(out_b, s)
     b = add(b, got_b)
-    got_b = send(b, 1)
     g = add(g, got_g)
-    g = put(0, g, send(g, 0))
+    got_g = send(g, 0)
+    got_b = send(b, end)
+    a_chip = send(a, 1)
+    g = put(0, g, got_g)
     x0, g, r = o.run(factor_step, g)
     x1, g, r = o.run(factor_step, g, r)
-    for s in range(2, end + 1):
-        b = add(b, got_b)
-        got_b = send(b, s)
-    a = add(a, got_a)
     x2, g, r = o.run(factor_step, g, r)
     (x3,) = o.run(factor_step, g, r)
+    o.last = (x3, a_chip)
+    b = add(b, got_b)
+    for s in range(end - 1, 1, -1):
+        b = put(s, b, send(b, s))
+    b_chip = send(b, 1)
+    c = columns(a, b)
+    c_core = send(c, 0)
     parts = o.run(lambda x: finish((x0, x1, x2, x3), x), p_full)
-    b = add(b, got_b)
-    c = o.run(lambda x: jnp.concatenate(pick(second, a, x), axis=1), b)
-    c_core = send(c, 0)
-    outs = o.run(lambda x: update(at, parts, {0: x}, t), c)
-    projections, r_t = o.run(lambda x: update(at, parts, {1: x}, t, outs), c_core)
+    outs = o.run(lambda x: update(at, parts, {(0, 0): c, (1, 0): x}, t), c_core)
+    c_chip = columns(a_chip, b_chip)
+    c_both = send(c_chip, 0)
+    carry = o.run(lambda x: update(at, parts, {(0, 1): x}, t, last=False), c_chip)
+    projections, r_t = update(at, parts, {(1, 1): c_both}, t, ((0, 1),), carry, outs)
     return projections, r_t.T
 
 

time: 79.3 us -> 74.5 us (0.939)
  waiting for transfers between devices: 24.9 us -> 19.6 us
    ppermute x11 -> x14, waiting for transfers between devices: 20.7 us -> 15.4 us  [swap(): lax.ppermute(x, 'row', [(r, r ^ 1 << by_core[r & 1]) for r in range(self....]
    ppermute x11 -> x14, starting transfers between devices: 9.51 us -> 10.1 us  [swap(): lax.ppermute(x, 'row', [(r, r ^ 1 << by_core[r & 1]) for r in range(self....]
    pallas_call x2 -> x3, Pallas kernels: 11.7 us -> 11.4 us  [update(): pl.pallas_call(functools.partial(update_kernel, places=tuple(pieces), car...]
  transfers between devices with their start and end apart: 14 -> 17, of which waited for: 7 -> 11; matrix products, arithmetic and copies ran while one was open for 1% -> 0% of each run, Pallas kernels for 31% -> 35%
where the time goes in v3:
time: 74.5 us; the launch traced here: 74.2 us
  Pallas kernels  31.4 us (42%)
  waiting for transfers between devices  19.6 us (26%)
  starting transfers between devices  16.6 us (22%)
  local copies, waits for them, and re-layouts  4.66 us (6%)
  between operations  1.07 us (1%)
  other arithmetic  0.93 us (1%)
    ppermute x14, waiting for transfers between devices, swap(): lax.ppermute(x, 'row', [(r, r ^ 1 << by_core[r & 1]) for r in range(self....  15.4 us
    pallas_call x3, Pallas kernels, update(): pl.pallas_call(functools.partial(update_kernel, places=tuple(pieces), car...  11.4 us
    pallas_call x4, Pallas kernels, factor_step(): pl.pallas_call(functools.partial(factor_kernel, first=r is None, last=las...  10.2 us
    ppermute x14, starting transfers between devices, swap(): lax.ppermute(x, 'row', [(r, r ^ 1 << by_core[r & 1]) for r in range(self....  10.1 us
    ppermute x3, starting transfers between devices, flipped(): return lax.ppermute(x, 'col', [(z, z ^ flip) for z in range(nz)])  6.46 us
    pallas_call x2, Pallas kernels, cross(): pl.pallas_call(functools.partial(cross_kernel, mine=mine), out_shape=[jax...  6.42 us
    unnamed x6, local copies, waits for them, and re-layouts  4.55 us
    ppermute x3, waiting for transfers between devices, flipped(): return lax.ppermute(x, 'col', [(z, z ^ flip) for z in range(nz)])  4.24 us
  transfers between devices with their start and end apart: 17, of which 11 were waited for; matrix products, arithmetic and copies ran while one was open for 0% of the time, Pallas kernels for 35%

profile of v3, /device:TPU:0, one launch (start us, length us, event | category | flops | bytes accessed | tf_op | source)
XLA Modules:
  0.0 74.2 jit_solution(6049717819467960614)
XLA Ops:
  0.7 0.1 stack.31.at_ref
  0.8 4.1 %collective-permute-start = (f32[64,768]{1,0:T(8,128)}, f32[64,768]{1,0:T(8,128)S(1)}, u32[]{:S(2)}, u32[]{:S(2)}) collective-permute-start(f32[64,768]{1,0:T(8,128)} %bitcast.23), channel_id=1, source_target_pairs={{0,2},{1,3},{2,0},{3,1},{4,6},{5,7},{6,4},{7,5},{8,10},{9,11},{10,... | collective-permute-start | bytes 589832 | tf_op jit(solution)/shard_map/ppermute | solution.py:389
  4.9 1.6 %collective-permute-start.1 = (f32[64,768]{1,0:T(8,128)}, f32[64,768]{1,0:T(8,128)S(1)}, u32[]{:S(2)}, u32[]{:S(2)}) collective-permute-start(f32[64,768]{1,0:T(8,128)} %bitcast.24), channel_id=1, source_target_pairs={{0,1},{1,0},{2,3},{3,2},{4,5},{5,4},{6,7},{7,6},{8,9},{9,8},{10,11... | collective-permute-start | bytes 589832 | tf_op jit(solution)/shard_map/ppermute | solution.py:389
  6.5 0.0 copy-start
  6.5 3.6 %copy-done = f32[768,3008]{0,1:T(8,128)S(1)} copy-done((f32[768,3008]{0,1:T(8,128)S(1)}, f32[768,3008]{0,1:T(8,128)}, u32[]{:S(2)}) %copy-start) | copy-done | bytes 9240600
  10.1 0.0 copy-start.2
  10.1 0.9 %copy-done.2 = f32[768,64]{0,1:T(8,128)S(1)} copy-done((f32[768,64]{0,1:T(8,128)S(1)}, f32[768,64]{0,1:T(8,128)}, u32[]{:S(2)}) %copy-start.2) | copy-done | bytes 196632
  11.0 0.0 copy-start.1
  11.0 1.1 %touch.1 = (s32[7]{0:T(128)S(1)}, f32[64,768]{1,0:T(8,128)S(1)}, f32[64,768]{1,0:T(8,128)S(1)}) custom-call(s32[7]{0:T(128)S(1)} %stack.31.at_ref, f32[64,768]{1,0:T(8,128)S(1)} %bitcast.25, f32[3008,768]{1,0:T(8,128)S(1)} %bitcast.17), custom_call_target="tpu_custom_call" | custom-call | tf_op jit(solution)/shard_map/touch/pallas_call | solution.py:57
  12.2 2.2 %collective-permute-done = f32[64,768]{1,0:T(8,128)S(1)} collective-permute-done((f32[64,768]{1,0:T(8,128)}, f32[64,768]{1,0:T(8,128)S(1)}, u32[]{:S(2)}, u32[]{:S(2)}) %collective-permute-start) | collective-permute-done | bytes 196640 | tf_op jit(solution)/shard_map/ppermute | solution.py:389
  14.3 0.8 %collective-permute-start.2 = (f32[64,768]{1,0:T(8,128)S(1)}, f32[64,768]{1,0:T(8,128)S(1)}, u32[]{:S(2)}, u32[]{:S(2)}) collective-permute-start(f32[64,768]{1,0:T(8,128)S(1)} %add.36.far.pa_ref), channel_id=1, source_target_pairs={{0,1},{1,0},{2,3},{3,2},{4,5},{5,4},{6,7},{7,6},{8,9},{9,8},{10,11... | collective-permute-start | bytes 589832 | tf_op jit(solution)/shard_map/ppermute | solution.py:389
  15.1 0.0 collective-permute-done.1.pb_ref.pair
  15.1 0.0 copy-done.1
  15.1 3.2 %cross.2 = (f32[1504,128]{1,0:T(8,128)S(1)}, f32[1504,128]{1,0:T(8,128)S(1)}) custom-call(s32[7]{0:T(128)S(1)} %get-tuple-element.74.at_ref, f32[64,768]{1,0:T(8,128)S(1)} %get-tuple-element.80.pa_ref.own, f32[64,768]{1,0:T(8,128)S(1)} %collective-permute-done.1.pb_ref.pair, f32[3008,768]{1,0:T(8,128)S(1)} %bitcast.18), custom_call_target="tpu_custom_call" | custom-call | tf_op jit(solution)/shard_map/cross/pallas_call | solution.py:86
  18.4 2.1 %collective-permute-done.2.across.pb_ref = f32[64,768]{1,0:T(8,128)S(1)} collective-permute-done((f32[64,768]{1,0:T(8,128)S(1)}, f32[64,768]{1,0:T(8,128)S(1)}, u32[]{:S(2)}, u32[]{:S(2)}) %collective-permute-start.2) | collective-permute-done | bytes 196640 | tf_op jit(solution)/shard_map/ppermute | solution.py:389
  20.4 1.4 %gram.1 = (f32[256,768]{1,0:T(8,128)S(1)}, f32[256,256]{1,0:T(8,128)S(1)}) custom-call(s32[7]{0:T(128)S(1)} %get-tuple-element.74.at_ref, f32[64,768]{1,0:T(8,128)S(1)} %get-tuple-element.80.pa_ref.own, f32[64,768]{1,0:T(8,128)S(1)} %collective-permute-done.1.pb_ref.pair, f32[64,768]{1,0:T(8,128)S(1)} %add.36.far.pa_ref, ...), custom_call_target="tpu_custom_call" | custom-call | tf_op jit(solution)/shard_map/gram/pallas_call | solution.py:108
  21.9 0.1 slice_select_fusion
  21.9 0.1 collective-permute-start.4
  22.0 0.5 collective-permute-start.3
  22.5 1.9 %collective-permute-done.3 = f32[128,256]{1,0:T(8,128)S(1)} collective-permute-done((f32[128,256]{1,0:T(8,128)S(1)}, f32[128,256]{1,0:T(8,128)S(1)}, u32[]{:S(2)}, u32[]{:S(2)}) %collective-permute-start.3) | collective-permute-done | bytes 131104 | tf_op jit(solution)/shard_map/ppermute | solution.py:315
  24.5 0.0 collective-permute-done.4
  24.5 0.1 broadcast_select_fusion.6
  24.6 1.3 %collective-permute-start.6 = (f32[752,128]{1,0:T(8,128)S(1)}, f32[752,128]{1,0:T(8,128)S(1)}, u32[]{:S(2)}, u32[]{:S(2)}) collective-permute-start(f32[752,128]{1,0:T(8,128)S(1)} %get-tuple-element.89), channel_id=1, source_target_pairs={{0,8},{4,20},{8,0},{12,28},{16,24},{20,4},{24,16},{28,12},{1,9},{5... | collective-permute-start | bytes 1155080 | tf_op jit(solution)/shard_map/ppermute | solution.py:315
  25.9 1.5 %collective-permute-start.5 = (f32[128,256]{1,0:T(8,128)S(1)}, f32[128,256]{1,0:T(8,128)S(1)}, u32[]{:S(2)}, u32[]{:S(2)}) collective-permute-start(f32[128,256]{1,0:T(8,128)S(1)} %add.37), channel_id=1, source_target_pairs={{0,16},{4,12},{8,24},{12,4},{16,0},{20,28},{24,8},{28,20},{1,17},{... | collective-permute-start | bytes 393224 | tf_op jit(solution)/shard_map/ppermute | solution.py:315
  27.5 3.2 %cross.3 = (f32[1504,128]{1,0:T(8,128)S(1)}, f32[1504,128]{1,0:T(8,128)S(1)}) custom-call(s32[7]{0:T(128)S(1)} %get-tuple-element.74.at_ref, f32[64,768]{1,0:T(8,128)S(1)} %add.36.far.pa_ref, f32[64,768]{1,0:T(8,128)S(1)} %collective-permute-done.2.across.pb_ref, f32[3008,768]{1,0:T(8,128)S(1)} %bitcast.19), custom_call_target="tpu_custom_call" | custom-call | tf_op jit(solution)/shard_map/cross/pallas_call | solution.py:86
  30.7 1.7 %collective-permute-done.5 = f32[128,256]{1,0:T(8,128)S(1)} collective-permute-done((f32[128,256]{1,0:T(8,128)S(1)}, f32[128,256]{1,0:T(8,128)S(1)}, u32[]{:S(2)}, u32[]{:S(2)}) %collective-permute-start.5) | collective-permute-done | bytes 131104 | tf_op jit(solution)/shard_map/ppermute | solution.py:315
  32.4 1.4 %collective-permute-done.6 = f32[752,128]{1,0:T(8,128)S(1)} collective-permute-done((f32[752,128]{1,0:T(8,128)S(1)}, f32[752,128]{1,0:T(8,128)S(1)}, u32[]{:S(2)}, u32[]{:S(2)}) %collective-permute-start.6) | collective-permute-done | bytes 385056 | tf_op jit(solution)/shard_map/ppermute | solution.py:315
  33.8 0.1 add.41
  33.8 0.1 collective-permute-start.7
  33.9 1.0 %collective-permute-start.8 = (f32[752,128]{1,0:T(8,128)S(1)}, f32[752,128]{1,0:T(8,128)S(1)}, u32[]{:S(2)}, u32[]{:S(2)}) collective-permute-start(f32[752,128]{1,0:T(8,128)S(1)} %add.41), channel_id=1, source_target_pairs={{0,16},{4,12},{8,24},{12,4},{16,0},{20,28},{24,8},{28,20},{1,17},{... | collective-permute-start | bytes 1155080 | tf_op jit(solution)/shard_map/ppermute | solution.py:315
  34.9 1.3 %collective-permute-done.7 = f32[1504,128]{1,0:T(8,128)S(1)} collective-permute-done((f32[1504,128]{1,0:T(8,128)S(1)}, f32[1504,128]{1,0:T(8,128)S(1)}, u32[]{:S(2)}, u32[]{:S(2)}) %collective-permute-start.7) | collective-permute-done | bytes 770080 | tf_op jit(solution)/shard_map/ppermute | solution.py:315
  36.1 0.1 broadcast_select_fusion.4
  36.3 1.3 %collective-permute-start.9 = (f32[752,128]{1,0:T(8,128)S(1)}, f32[752,128]{1,0:T(8,128)S(1)}, u32[]{:S(2)}, u32[]{:S(2)}) collective-permute-start(f32[752,128]{1,0:T(8,128)S(1)} %get-tuple-element.99), channel_id=1, source_target_pairs={{0,8},{4,20},{8,0},{12,28},{16,24},{20,4},{24,16},{28,12},{1,9},{5... | collective-permute-start | bytes 1155080 | tf_op jit(solution)/shard_map/ppermute | solution.py:315
  37.6 0.8 %collective-permute-start.10 = (f32[128,256]{1,0:T(8,128)S(1)}, f32[128,256]{1,0:T(8,128)S(1)}, u32[]{:S(2)}, u32[]{:S(2)}) collective-permute-start(f32[128,256]{1,0:T(8,128)S(1)} %add.40), channel_id=1, source_target_pairs={{0,8},{4,20},{8,0},{12,28},{16,24},{20,4},{24,16},{28,12},{1,9},{5... | collective-permute-start | bytes 393224 | tf_op jit(solution)/shard_map/ppermute | solution.py:315
  38.4 5.8 %collective-permute-done.8 = f32[752,128]{1,0:T(8,128)S(1)} collective-permute-done((f32[752,128]{1,0:T(8,128)S(1)}, f32[752,128]{1,0:T(8,128)S(1)}, u32[]{:S(2)}, u32[]{:S(2)}) %collective-permute-start.8) | collective-permute-done | bytes 385056 | tf_op jit(solution)/shard_map/ppermute | solution.py:315
  44.2 1.0 %collective-permute-done.9 = f32[752,128]{1,0:T(8,128)S(1)} collective-permute-done((f32[752,128]{1,0:T(8,128)S(1)}, f32[752,128]{1,0:T(8,128)S(1)}, u32[]{:S(2)}, u32[]{:S(2)}) %collective-permute-start.9) | collective-permute-done | bytes 385056 | tf_op jit(solution)/shard_map/ppermute | solution.py:315
  45.2 0.1 add.45
  45.3 1.4 %collective-permute-done.10 = f32[128,256]{1,0:T(8,128)S(1)} collective-permute-done((f32[128,256]{1,0:T(8,128)S(1)}, f32[128,256]{1,0:T(8,128)S(1)}, u32[]{:S(2)}, u32[]{:S(2)}) %collective-permute-start.10) | collective-permute-done | bytes 131104 | tf_op jit(solution)/shard_map/ppermute | solution.py:315
  46.7 0.4 collective-permute-start.11
  47.1 1.3 %collective-permute-start.12 = (f32[752,128]{1,0:T(8,128)S(1)}, f32[752,128]{1,0:T(8,128)S(1)}, u32[]{:S(2)}, u32[]{:S(2)}) collective-permute-start(f32[752,128]{1,0:T(8,128)S(1)} %add.44), channel_id=1, source_target_pairs={{0,8},{4,20},{8,0},{12,28},{16,24},{20,4},{24,16},{28,12},{1,9},{5... | collective-permute-start | bytes 1155080 | tf_op jit(solution)/shard_map/ppermute | solution.py:315
  48.4 0.9 %collective-permute-start.13 = (f32[752,128]{1,0:T(8,128)S(1)}, f32[752,128]{1,0:T(8,128)S(1)}, u32[]{:S(2)}, u32[]{:S(2)}) collective-permute-start(f32[752,128]{1,0:T(8,128)S(1)} %add.45), channel_id=1, source_target_pairs={{0,16},{4,12},{8,24},{12,4},{16,0},{20,28},{24,8},{28,20},{1,17},{... | collective-permute-start | bytes 1155080 | tf_op jit(solution)/shard_map/ppermute | solution.py:315
  49.3 0.0 collective-permute-done.11
  49.3 0.1 broadcast_select_fusion.9
  49.4 2.8 %factor.4 = (f32[64,256]{1,0:T(8,128)S(1)}, f32[192,192]{1,0:T(8,128)S(1)}, f32[192,256]{1,0:T(8,128)S(1)}) custom-call(f32[256,256]{1,0:T(8,128)S(1)} %pad_maximum_fusion.2.s_ref), custom_call_target="tpu_custom_call" | custom-call | tf_op jit(solution)/shard_map/factor/pallas_call | solution.py:202
  52.1 2.6 %factor.5 = (f32[64,256]{1,0:T(8,128)S(1)}, f32[128,128]{1,0:T(8,128)S(1)}, f32[128,256]{1,0:T(8,128)S(1)}) custom-call(f32[192,192]{1,0:T(8,128)S(1)} %get-tuple-element.109.s_ref, f32[192,256]{1,0:T(8,128)S(1)} %get-tuple-element.110.rest_0_), custom_call_target="tpu_custom_call" | custom-call | tf_op jit(solution)/shard_map/factor/pallas_call | solution.py:202
  54.7 2.7 %factor.6 = (f32[64,256]{1,0:T(8,128)S(1)}, f32[64,64]{1,0:T(8,128)S(1)}, f32[64,256]{1,0:T(8,128)S(1)}) custom-call(f32[128,128]{1,0:T(8,128)S(1)} %get-tuple-element.113.s_ref, f32[128,256]{1,0:T(8,128)S(1)} %get-tuple-element.114.rest_0_), custom_call_target="tpu_custom_call" | custom-call | tf_op jit(solution)/shard_map/factor/pallas_call | solution.py:202
  57.5 2.1 %factor.7.x3 = f32[64,256]{1,0:T(8,128)S(1)} custom-call(f32[64,64]{1,0:T(8,128)S(1)} %get-tuple-element.117.s_ref, f32[64,256]{1,0:T(8,128)S(1)} %get-tuple-element.118.rest_0_), custom_call_target="tpu_custom_call" | custom-call | tf_op jit(solution)/shard_map/factor/pallas_call | solution.py:202
  59.6 0.0 collective-permute-done.12
  59.6 0.0 collective-permute-done.13
  59.6 0.1 add.47
  59.6 0.1 broadcast_select_fusion.3
  59.7 0.1 pad_maximum_fusion.refs_0_
  59.8 0.1 collective-permute-start.15
  59.9 0.8 %collective-permute-start.14 = (f32[752,128]{1,0:T(8,128)S(1)}, f32[752,128]{1,0:T(8,128)S(1)}, u32[]{:S(2)}, u32[]{:S(2)}) collective-permute-start(f32[752,128]{1,0:T(8,128)S(1)} %add.47), channel_id=1, source_target_pairs={{0,8},{4,20},{8,0},{12,28},{16,24},{20,4},{24,16},{28,12},{1,9},{5... | collective-permute-start | bytes 1155080 | tf_op jit(solution)/shard_map/ppermute | solution.py:315
  60.7 0.8 %finish.1 = (bf16[256,256]{1,0:T(8,128)(2,1)S(1)}, bf16[256,256]{1,0:T(8,128)(2,1)S(1)}, bf16[256,768]{1,0:T(8,128)(2,1)S(1)}, bf16[256,768]{1,0:T(8,128)(2,1)S(1)}) custom-call(f32[64,256]{1,0:T(8,128)S(1)} %get-tuple-element.107.x0, f32[64,256]{1,0:T(8,128)S(1)} %get-tuple-element.111.x1, f32[64,256]{1,0:T(8,128)S(1)} %get-tuple-element.115.x2, ...), custom_call_target="tpu_custom_call" | custom-call | tf_op jit(solution)/shard_map/finish/pallas_call | solution.py:221
  61.5 0.6 collective-permute-done.15.refs_1_
  62.1 5.2 %update.3 = (f32[3008,256]{1,0:T(8,128)}, f32[3008,768]{1,0:T(8,128)}) custom-call(s32[7]{0:T(128)S(1)} %get-tuple-element.74.at_ref, bf16[256,256]{1,0:T(8,128)(2,1)S(1)} %get-tuple-element.126.lh_ref, bf16[256,256]{1,0:T(8,128)(2,1)S(1)} %get-tuple-element.127.ll_ref, bf16[256,768]{1,0:T(8,128)(2,1)S(1)} %get-tuple-element.128.qh_ref, ...), custom_call_target="tpu_custom_call" | custom-call | tf_op jit(solution)/shard_map/update/pallas_call | solution.py:294
  67.3 0.3 collective-permute-done.14
  67.6 0.1 broadcast_select_fusion.1
  67.7 0.1 pad_maximum_fusion.1.refs_0_
  67.8 0.1 collective-permute-start.16
  67.9 2.5 %update.4 = (f32[752,256]{1,0:T(8,128)S(1)}, f32[752,768]{1,0:T(8,128)S(1)}) custom-call(s32[7]{0:T(128)S(1)} %get-tuple-element.74.at_ref, bf16[256,256]{1,0:T(8,128)(2,1)S(1)} %get-tuple-element.126.lh_ref, bf16[256,256]{1,0:T(8,128)(2,1)S(1)} %get-tuple-element.127.ll_ref, bf16[256,768]{1,0:T(8,128)(2,1)S(1)} %get-tuple-element.128.qh_ref, ...), custom_call_target="tpu_custom_call" | custom-call | tf_op jit(solution)/shard_map/update/pallas_call | solution.py:294
  70.4 0.0 collective-permute-done.16.refs_0_
  70.4 3.7 %update.5 = (f32[3008,256]{1,0:T(8,128)}, f32[3008,768]{1,0:T(8,128)}) custom-call(s32[7]{0:T(128)S(1)} %get-tuple-element.74.at_ref, bf16[256,256]{1,0:T(8,128)(2,1)S(1)} %get-tuple-element.126.lh_ref, bf16[256,256]{1,0:T(8,128)(2,1)S(1)} %get-tuple-element.127.ll_ref, ...), custom_call_target="tpu_custom_call", output_to_operand_aliasing={{0}: (9, {}), {1}: (10, {})} | custom-call | tf_op jit(solution)/shard_map/update/pallas_call | solution.py:294
  (9 shorter events, 0.2 us)
Async XLA Ops:
  0.8 13.5 %collective-permute-start = (f32[64,768]{1,0:T(8,128)}, f32[64,768]{1,0:T(8,128)S(1)}, u32[]{:S(2)}, u32[]{:S(2)}) collective-permute-start(f32[64,768]{1,0:T(8,128)} %bitcast.23), channel_id=1, source_target_pairs={{0,2},{1,3},{2,0},{3,1},{4,6},{5,7},{6,4},{7,5},{8,10},{9,11},{10,... | collective-permute-start | bytes 589832 | tf_op jit(solution)/shard_map/ppermute | solution.py:389
  4.9 10.2 %collective-permute-start.1 = (f32[64,768]{1,0:T(8,128)}, f32[64,768]{1,0:T(8,128)S(1)}, u32[]{:S(2)}, u32[]{:S(2)}) collective-permute-start(f32[64,768]{1,0:T(8,128)} %bitcast.24), channel_id=1, source_target_pairs={{0,1},{1,0},{2,3},{3,2},{4,5},{5,4},{6,7},{7,6},{8,9},{9,8},{10,11... | collective-permute-start | bytes 589832 | tf_op jit(solution)/shard_map/ppermute | solution.py:389
  6.5 3.6 %copy-start = (f32[768,3008]{0,1:T(8,128)S(1)}, f32[768,3008]{0,1:T(8,128)}, u32[]{:S(2)}) copy-start(f32[768,3008]{0,1:T(8,128)} %param.3) | copy-start | bytes 27721732
  10.1 0.9 %copy-start.2 = (f32[768,64]{0,1:T(8,128)S(1)}, f32[768,64]{0,1:T(8,128)}, u32[]{:S(2)}) copy-start(f32[768,64]{0,1:T(8,128)} %param.2) | copy-start | bytes 589828
  11.0 4.1 %copy-start.1 = (f32[768,3008]{0,1:T(8,128)S(1)}, f32[768,3008]{0,1:T(8,128)}, u32[]{:S(2)}) copy-start(f32[768,3008]{0,1:T(8,128)} %param.3) | copy-start | bytes 27721732
  14.3 6.1 %collective-permute-start.2 = (f32[64,768]{1,0:T(8,128)S(1)}, f32[64,768]{1,0:T(8,128)S(1)}, u32[]{:S(2)}, u32[]{:S(2)}) collective-permute-start(f32[64,768]{1,0:T(8,128)S(1)} %add.36.far.pa_ref), channel_id=1, source_target_pairs={{0,1},{1,0},{2,3},{3,2},{4,5},{5,4},{6,7},{7,6},{8,9},{9,8},{10,11... | collective-permute-start | bytes 589832 | tf_op jit(solution)/shard_map/ppermute | solution.py:389
  21.9 2.5 %collective-permute-start.4 = (f32[1504,128]{1,0:T(8,128)S(1)}, f32[1504,128]{1,0:T(8,128)S(1)}, u32[]{:S(2)}, u32[]{:S(2)}) collective-permute-start(f32[1504,128]{1,0:T(8,128)S(1)} %get-tuple-element.83), channel_id=1, source_target_pairs={{0,4},{4,0},{8,12},{12,8},{16,20},{20,16},{24,28},{28,24},{1,5},{5... | collective-permute-start | bytes 2310152 | tf_op jit(solution)/shard_map/ppermute | solution.py:315
  22.0 2.4 %collective-permute-start.3 = (f32[128,256]{1,0:T(8,128)S(1)}, f32[128,256]{1,0:T(8,128)S(1)}, u32[]{:S(2)}, u32[]{:S(2)}) collective-permute-start(f32[128,256]{1,0:T(8,128)S(1)} %get-tuple-element.82), channel_id=1, source_target_pairs={{0,4},{4,0},{8,12},{12,8},{16,20},{20,16},{24,28},{28,24},{1,5},{5... | collective-permute-start | bytes 393224 | tf_op jit(solution)/shard_map/ppermute | solution.py:315
  24.6 9.2 %collective-permute-start.6 = (f32[752,128]{1,0:T(8,128)S(1)}, f32[752,128]{1,0:T(8,128)S(1)}, u32[]{:S(2)}, u32[]{:S(2)}) collective-permute-start(f32[752,128]{1,0:T(8,128)S(1)} %get-tuple-element.89), channel_id=1, source_target_pairs={{0,8},{4,20},{8,0},{12,28},{16,24},{20,4},{24,16},{28,12},{1,9},{5... | collective-permute-start | bytes 1155080 | tf_op jit(solution)/shard_map/ppermute | solution.py:315
  25.9 6.4 %collective-permute-start.5 = (f32[128,256]{1,0:T(8,128)S(1)}, f32[128,256]{1,0:T(8,128)S(1)}, u32[]{:S(2)}, u32[]{:S(2)}) collective-permute-start(f32[128,256]{1,0:T(8,128)S(1)} %add.37), channel_id=1, source_target_pairs={{0,16},{4,12},{8,24},{12,4},{16,0},{20,28},{24,8},{28,20},{1,17},{... | collective-permute-start | bytes 393224 | tf_op jit(solution)/shard_map/ppermute | solution.py:315
  33.8 2.3 %collective-permute-start.7 = (f32[1504,128]{1,0:T(8,128)S(1)}, f32[1504,128]{1,0:T(8,128)S(1)}, u32[]{:S(2)}, u32[]{:S(2)}) collective-permute-start(f32[1504,128]{1,0:T(8,128)S(1)} %get-tuple-element.97), channel_id=1, source_target_pairs={{0,4},{4,0},{8,12},{12,8},{16,20},{20,16},{24,28},{28,24},{1,5},{5... | collective-permute-start | bytes 2310152 | tf_op jit(solution)/shard_map/ppermute | solution.py:315
  33.9 10.3 %collective-permute-start.8 = (f32[752,128]{1,0:T(8,128)S(1)}, f32[752,128]{1,0:T(8,128)S(1)}, u32[]{:S(2)}, u32[]{:S(2)}) collective-permute-start(f32[752,128]{1,0:T(8,128)S(1)} %add.41), channel_id=1, source_target_pairs={{0,16},{4,12},{8,24},{12,4},{16,0},{20,28},{24,8},{28,20},{1,17},{... | collective-permute-start | bytes 1155080 | tf_op jit(solution)/shard_map/ppermute | solution.py:315
  36.3 9.0 %collective-permute-start.9 = (f32[752,128]{1,0:T(8,128)S(1)}, f32[752,128]{1,0:T(8,128)S(1)}, u32[]{:S(2)}, u32[]{:S(2)}) collective-permute-start(f32[752,128]{1,0:T(8,128)S(1)} %get-tuple-element.99), channel_id=1, source_target_pairs={{0,8},{4,20},{8,0},{12,28},{16,24},{20,4},{24,16},{28,12},{1,9},{5... | collective-permute-start | bytes 1155080 | tf_op jit(solution)/shard_map/ppermute | solution.py:315
  37.6 9.0 %collective-permute-start.10 = (f32[128,256]{1,0:T(8,128)S(1)}, f32[128,256]{1,0:T(8,128)S(1)}, u32[]{:S(2)}, u32[]{:S(2)}) collective-permute-start(f32[128,256]{1,0:T(8,128)S(1)} %add.40), channel_id=1, source_target_pairs={{0,8},{4,20},{8,0},{12,28},{16,24},{20,4},{24,16},{28,12},{1,9},{5... | collective-permute-start | bytes 393224 | tf_op jit(solution)/shard_map/ppermute | solution.py:315
  46.7 2.6 %collective-permute-start.11 = (f32[128,256]{1,0:T(8,128)S(1)}, f32[128,256]{1,0:T(8,128)S(1)}, u32[]{:S(2)}, u32[]{:S(2)}) collective-permute-start(f32[128,256]{1,0:T(8,128)S(1)} %add.46), channel_id=1, source_target_pairs={{0,4},{4,0},{8,12},{12,8},{16,20},{20,16},{24,28},{28,24},{1,5},{5... | collective-permute-start | bytes 393224 | tf_op jit(solution)/shard_map/ppermute | solution.py:315
  47.1 12.5 %collective-permute-start.12 = (f32[752,128]{1,0:T(8,128)S(1)}, f32[752,128]{1,0:T(8,128)S(1)}, u32[]{:S(2)}, u32[]{:S(2)}) collective-permute-start(f32[752,128]{1,0:T(8,128)S(1)} %add.44), channel_id=1, source_target_pairs={{0,8},{4,20},{8,0},{12,28},{16,24},{20,4},{24,16},{28,12},{1,9},{5... | collective-permute-start | bytes 1155080 | tf_op jit(solution)/shard_map/ppermute | solution.py:315
  48.4 11.2 %collective-permute-start.13 = (f32[752,128]{1,0:T(8,128)S(1)}, f32[752,128]{1,0:T(8,128)S(1)}, u32[]{:S(2)}, u32[]{:S(2)}) collective-permute-start(f32[752,128]{1,0:T(8,128)S(1)} %add.45), channel_id=1, source_target_pairs={{0,16},{4,12},{8,24},{12,4},{16,0},{20,28},{24,8},{28,20},{1,17},{... | collective-permute-start | bytes 1155080 | tf_op jit(solution)/shard_map/ppermute | solution.py:315
  59.8 2.3 %collective-permute-start.15 = (f32[752,256]{1,0:T(8,128)S(1)}, f32[752,256]{1,0:T(8,128)S(1)}, u32[]{:S(2)}, u32[]{:S(2)}) collective-permute-start(f32[752,256]{1,0:T(8,128)S(1)} %pad_maximum_fusion.refs_0_), channel_id=1, source_target_pairs={{0,4},{4,0},{8,12},{12,8},{16,20},{20,16},{24,28},{28,24},{1,5},{5... | collective-permute-start | bytes 2310152 | tf_op jit(solution)/shard_map/ppermute | solution.py:315
  59.9 7.8 %collective-permute-start.14 = (f32[752,128]{1,0:T(8,128)S(1)}, f32[752,128]{1,0:T(8,128)S(1)}, u32[]{:S(2)}, u32[]{:S(2)}) collective-permute-start(f32[752,128]{1,0:T(8,128)S(1)} %add.47), channel_id=1, source_target_pairs={{0,8},{4,20},{8,0},{12,28},{16,24},{20,4},{24,16},{28,12},{1,9},{5... | collective-permute-start | bytes 1155080 | tf_op jit(solution)/shard_map/ppermute | solution.py:315
  67.8 2.6 %collective-permute-start.16 = (f32[752,256]{1,0:T(8,128)S(1)}, f32[752,256]{1,0:T(8,128)S(1)}, u32[]{:S(2)}, u32[]{:S(2)}) collective-permute-start(f32[752,256]{1,0:T(8,128)S(1)} %pad_maximum_fusion.1.refs_0_), channel_id=1, source_target_pairs={{0,4},{4,0},{8,12},{12,8},{16,20},{20,16},{24,28},{28,24},{1,5},{5... | collective-permute-start | bytes 2310152 | tf_op jit(solution)/shard_map/ppermute | solution.py:315

commit v4 on v3

--- a/solution.py
+++ b/solution.py
@@ -65,33 +65,68 @@
     )(at, p_t, t)
 
 
-def cross_kernel(at_ref, pa_ref, pb_ref, t_ref, *c_refs, mine):
+def cross_kernel(at_ref, pa_ref, pb_ref, t_ref, *c_refs, halves):
     n = 2 * pa_ref.shape[0]
-    m = c_refs[0].shape[0]
+    m = t_ref.shape[0] // 2
     b = block_rows(m)
     pa, pb = pa_ref[...], pb_ref[...]
     swap = at_ref[ODD] != 0
     p_hi, p_lo = split(jnp.concatenate([jnp.where(swap, pb, pa), jnp.where(swap, pa, pb)], axis=0))
     both = jnp.concatenate([p_hi, p_lo], axis=0)
-    for c_ref, own in zip(c_refs, mine):
+    refs = list(c_refs)
+    for own, pieces in halves:
         half = at_ref[SIDE] if own else 1 - at_ref[SIDE]
         base = pl.multiple_of(half * m, 8)
-        for i in range(m // b):
-            t_hi, t_lo = split(t_ref[pl.ds(base + i * b, b), :])
+        outs, refs = refs[:pieces], refs[pieces:]
+        piece = m // pieces
+        for i in range(0, m, b):
+            t_hi, t_lo = split(t_ref[pl.ds(base + i, b), :])
             c = dot(t_hi, both, NT)
-            c_ref[i * b : (i + 1) * b, :] = c[:, :n] + c[:, n:] + dot(t_lo, p_hi, NT)
-
-
-def cross(at, mine, pa, pb, t):
-    return pl.pallas_call(
-        functools.partial(cross_kernel, mine=mine),
-        out_shape=[jax.ShapeDtypeStruct((t.shape[0] // 2, 2 * pa.shape[0]), F32)] * len(mine),
+            c = c[:, :n] + c[:, n:] + dot(t_lo, p_hi, NT)
+            if pieces == 1:
+                outs[0][i : i + b, :] = c
+            else:
+                for j in range(0, b, piece):
+                    outs[(i + j) // piece][...] = c[j : j + piece]
+
+
+def cross(at, halves, pa, pb, t):
+    m, n = t.shape[0] // 2, 2 * pa.shape[0]
+    shapes = [(m // pieces, n) for _, pieces in halves for _ in range(pieces)]
+    return pl.pallas_call(
+        functools.partial(cross_kernel, halves=halves),
+        out_shape=[jax.ShapeDtypeStruct(s, F32) for s in shapes],
         in_specs=[SMEM, VM, VM, VM],
-        out_specs=[VM] * len(mine),
+        out_specs=[VM] * len(shapes),
         compiler_params=params(),
         cost_estimate=cost(),
         name="cross",
     )(at, pa, pb, t)
+
+
+def halve_kernel(at_ref, keep_ref, *refs):
+    *got_refs, keep_out, send_out = refs
+    m = got_refs[0].shape[0]
+    upper = at_ref[SIDE + 1] != 0
+    h = len(got_refs) // 2
+    for j in range(h):
+        low = keep_ref[j * m : (j + 1) * m, :] + got_refs[j][...]
+        high = keep_ref[(j + h) * m : (j + h + 1) * m, :] + got_refs[j + h][...]
+        keep_out[j * m : (j + 1) * m, :] = jnp.where(upper, high, low)
+        send_out[j * m : (j + 1) * m, :] = jnp.where(upper, low, high)
+
+
+def halve(at, keep, got):
+    m, n = keep.shape
+    return pl.pallas_call(
+        halve_kernel,
+        out_shape=[jax.ShapeDtypeStruct((m // 2, n), F32)] * 2,
+        in_specs=[SMEM] + [VM] * (1 + len(got)),
+        out_specs=[VM] * 2,
+        compiler_params=params(),
+        cost_estimate=cost(),
+        name="halve",
+    )(at, keep, *got)
 
 
 def gram_kernel(at_ref, own, pair, far, across, p_full, g_ref):
@@ -393,12 +428,20 @@
         far = far + zero
         across = flipped(far, 1)
         o.last = far
-        out_a, a = o.run(lambda x: cross(at, (False, True), x, pair, t), p_own)
+        *out_a, a = o.run(lambda x: cross(at, ((False, 4), (True, 1)), x, pair, t), p_own)
         rest = (far, across)
     else:
         p_full = lax.all_gather(p_own, "col", axis=0, tiled=True)
         near, rest = [[p_full[i * (n // 4) : (i + 1) * (n // 4)] for i in h] for h in ((0, 1), (2, 3))]
-        out_a, a = cross(at, (False, True), *near, t)
+        out_a, a = cross(at, ((False, 1), (True, 1)), *near, t)
+    if nz == 4:
+        got_a = [rows.swap(x, 0) for x in out_a]
+        o.last = (out_a[0], across)
+        a, out_a = o.run(lambda x: halve(at, x, got_a), a)
+        o.last = out_a
+    else:
+        a, out_a = cut(1, a, send(out_a, 0))
+    got_a = send(out_a, 1)
     if nz == 4:
         p_full, g = o.run(lambda x: gram4(at, x, pair, far, across), p_own)
         o.last = g
@@ -406,21 +449,20 @@
         g = o.run(plain_gram, p_full)
     g, out = cut(0, g)
     got_g = send(out, 0)
-    got_a = send(out_a, 0)
+    (out_b,) = o.run(lambda x: cross(at, ((False, 1),), x, rest[1], t), rest[0])
     g = add(g, got_g)
-    got_g = send(g, end)
-    a, out_a = cut(1, a, got_a)
-    got_a = send(out_a, 1)
-    out_b, b = o.run(lambda x: cross(at, (False, True), x, rest[1], t), rest[0])
-    for s in range(end - 1, 0, -1):
-        g = add(g, got_g)
-        got_g = send(g, s)
+    got_g = send(g, 1)
     for s in range(2, end):
         a, out_a = cut(s, a, got_a)
         got_a = send(out_a, s)
     a = add(a, got_a)
     got_a = send(a, end)
-    b, out_b = cut(1, b, send(out_b, 0))
+    got_b = send(out_b, 0)
+    (b,) = o.run(lambda x: cross(at, ((True, 1),), x, rest[1], t), rest[0])
+    for s in range(2, end + 1):
+        g = add(g, got_g)
+        got_g = send(g, s)
+    b, out_b = cut(1, b, got_b)
     got_b = send(out_b, 1)
     a = add(a, got_a)
     for s in range(end - 1, 1, -1):

time: 74.5 us -> 72 us (0.966)
  waiting for transfers between devices: 19.6 us -> 12.6 us
  starting transfers between devices: 16.6 us -> 19.9 us
  Pallas kernels: 31.4 us -> 32.8 us
    ppermute x14 -> x17, waiting for transfers between devices: 15.4 us -> 9.42 us  [swap(): lax.ppermute(x, 'row', [(r, r ^ 1 << by_core[r & 1]) for r in range(self....]
    ppermute x14 -> x17, starting transfers between devices: 10.1 us -> 13.4 us  [swap(): lax.ppermute(x, 'row', [(r, r ^ 1 << by_core[r & 1]) for r in range(self....]
    pallas_call x2 -> x4, Pallas kernels: 6.42 us -> 7.82 us  [the longest x3 7.17 us: cross(): pl.pallas_call(functools.partial(cross_kernel, halves=halves), out_shape=...]
    ppermute x3, waiting for transfers between devices: 4.24 us -> 3.16 us  [flipped(): return lax.ppermute(x, 'col', [(z, z ^ flip) for z in range(nz)])]
  transfers between devices with their start and end apart: 17 -> 20, of which waited for: 11 -> 9; matrix products, arithmetic and copies ran while one was open for 0% -> 1% of each run, Pallas kernels for 35% -> 40%
where the time goes in v4:
time: 72 us; the launch traced here: 71.8 us
  Pallas kernels  32.8 us (46%)
  starting transfers between devices  19.9 us (28%)
  waiting for transfers between devices  12.6 us (18%)
  local copies, waits for them, and re-layouts  4.66 us (6%)
  between operations  1.09 us (2%)
  other arithmetic  0.85 us (1%)
    ppermute x17, starting transfers between devices, swap(): lax.ppermute(x, 'row', [(r, r ^ 1 << by_core[r & 1]) for r in range(self....  13.4 us
    pallas_call x3, Pallas kernels, update(): pl.pallas_call(functools.partial(update_kernel, places=tuple(pieces), car...  11.4 us
    pallas_call x4, Pallas kernels, factor_step(): pl.pallas_call(functools.partial(factor_kernel, first=r is None, last=las...  10.2 us
    ppermute x17, waiting for transfers between devices, swap(): lax.ppermute(x, 'row', [(r, r ^ 1 << by_core[r & 1]) for r in range(self....  9.42 us
    pallas_call x3, Pallas kernels, cross(): pl.pallas_call(functools.partial(cross_kernel, halves=halves), out_shape=...  7.17 us
    ppermute x3, starting transfers between devices, flipped(): return lax.ppermute(x, 'col', [(z, z ^ flip) for z in range(nz)])  6.46 us
    unnamed x6, local copies, waits for them, and re-layouts  4.55 us
    ppermute x3, waiting for transfers between devices, flipped(): return lax.ppermute(x, 'col', [(z, z ^ flip) for z in range(nz)])  3.16 us
  transfers between devices with their start and end apart: 20, of which 9 were waited for; matrix products, arithmetic and copies ran while one was open for 1% of the time, Pallas kernels for 40%

profile of v4, /device:TPU:0, one launch (start us, length us, event | category | flops | bytes accessed | tf_op | source)
XLA Modules:
  0.0 71.8 jit_solution(7906093016754922019)
XLA Ops:
  0.7 0.1 stack.31.at_ref
  0.8 4.1 %collective-permute-start = (f32[64,768]{1,0:T(8,128)}, f32[64,768]{1,0:T(8,128)S(1)}, u32[]{:S(2)}, u32[]{:S(2)}) collective-permute-start(f32[64,768]{1,0:T(8,128)} %bitcast.24), channel_id=1, source_target_pairs={{0,2},{1,3},{2,0},{3,1},{4,6},{5,7},{6,4},{7,5},{8,10},{9,11},{10,... | collective-permute-start | bytes 589832 | tf_op jit(solution)/shard_map/ppermute | solution.py:424
  4.9 1.6 %collective-permute-start.1 = (f32[64,768]{1,0:T(8,128)}, f32[64,768]{1,0:T(8,128)S(1)}, u32[]{:S(2)}, u32[]{:S(2)}) collective-permute-start(f32[64,768]{1,0:T(8,128)} %bitcast.25), channel_id=1, source_target_pairs={{0,1},{1,0},{2,3},{3,2},{4,5},{5,4},{6,7},{7,6},{8,9},{9,8},{10,11... | collective-permute-start | bytes 589832 | tf_op jit(solution)/shard_map/ppermute | solution.py:424
  6.5 3.6 %copy-done = f32[768,3008]{0,1:T(8,128)S(1)} copy-done((f32[768,3008]{0,1:T(8,128)S(1)}, f32[768,3008]{0,1:T(8,128)}, u32[]{:S(2)}) %copy-start) | copy-done | bytes 9240600
  10.1 0.9 %copy-done.2 = f32[768,64]{0,1:T(8,128)S(1)} copy-done((f32[768,64]{0,1:T(8,128)S(1)}, f32[768,64]{0,1:T(8,128)}, u32[]{:S(2)}) %copy-start.2) | copy-done | bytes 196632
  11.0 1.1 %touch.1 = (s32[7]{0:T(128)S(1)}, f32[64,768]{1,0:T(8,128)S(1)}, f32[64,768]{1,0:T(8,128)S(1)}) custom-call(s32[7]{0:T(128)S(1)} %stack.31.at_ref, f32[64,768]{1,0:T(8,128)S(1)} %bitcast.26, f32[3008,768]{1,0:T(8,128)S(1)} %bitcast.17), custom_call_target="tpu_custom_call" | custom-call | tf_op jit(solution)/shard_map/touch/pallas_call | solution.py:57
  12.2 2.2 %collective-permute-done = f32[64,768]{1,0:T(8,128)S(1)} collective-permute-done((f32[64,768]{1,0:T(8,128)}, f32[64,768]{1,0:T(8,128)S(1)}, u32[]{:S(2)}, u32[]{:S(2)}) %collective-permute-start) | collective-permute-done | bytes 196640 | tf_op jit(solution)/shard_map/ppermute | solution.py:424
  14.3 0.8 %collective-permute-start.2 = (f32[64,768]{1,0:T(8,128)S(1)}, f32[64,768]{1,0:T(8,128)S(1)}, u32[]{:S(2)}, u32[]{:S(2)}) collective-permute-start(f32[64,768]{1,0:T(8,128)S(1)} %add.30.far.pa_ref), channel_id=1, source_target_pairs={{0,1},{1,0},{2,3},{3,2},{4,5},{5,4},{6,7},{7,6},{8,9},{9,8},{10,11... | collective-permute-start | bytes 589832 | tf_op jit(solution)/shard_map/ppermute | solution.py:424
  15.1 0.0 collective-permute-done.1.pb_ref.pair
  15.1 3.2 %cross.3 = (f32[376,128]{1,0:T(8,128)S(1)}, f32[376,128]{1,0:T(8,128)S(1)}, f32[376,128]{1,0:T(8,128)S(1)}, f32[376,128]{1,0:T(8,128)S(1)}, f32[1504,128]{1,0:T(8,128)S(1)}) custom-call(s32[7]{0:T(128)S(1)} %get-tuple-element.76.at_ref, f32[64,768]{1,0:T(8,128)S(1)} %get-tuple-element.88.pa_ref.own, f32[64,768]{1,0:T(8,128)S(1)} %collective-permute-done.1.pb_ref.pair, ...), custom_call_target="tpu_custom_call" | custom-call | tf_op jit(solution)/shard_map/cross/pallas_call | solution.py:96
  18.4 0.1 collective-permute-start.4
  18.4 0.5 collective-permute-start.5
  18.9 0.1 collective-permute-start.6
  19.0 0.4 collective-permute-start.3
  19.4 1.0 %collective-permute-done.2.across.pb_ref = f32[64,768]{1,0:T(8,128)S(1)} collective-permute-done((f32[64,768]{1,0:T(8,128)S(1)}, f32[64,768]{1,0:T(8,128)S(1)}, u32[]{:S(2)}, u32[]{:S(2)}) %collective-permute-start.2) | collective-permute-done | bytes 196640 | tf_op jit(solution)/shard_map/ppermute | solution.py:424
  20.4 0.0 collective-permute-done.4.refs_1_
  20.4 0.0 collective-permute-done.5.refs_2_
  20.4 0.0 collective-permute-done.6.refs_3_
  20.4 0.2 collective-permute-done.3.refs_0_
  20.7 0.7 halve.1
  21.3 1.6 %collective-permute-start.8 = (f32[752,128]{1,0:T(8,128)S(1)}, f32[752,128]{1,0:T(8,128)S(1)}, u32[]{:S(2)}, u32[]{:S(2)}) collective-permute-start(f32[752,128]{1,0:T(8,128)S(1)} %get-tuple-element.87), channel_id=1, source_target_pairs={{0,8},{4,20},{8,0},{12,28},{16,24},{20,4},{24,16},{28,12},{1,9},{5... | collective-permute-start | bytes 1155080 | tf_op jit(solution)/shard_map/ppermute | solution.py:350
  22.9 1.4 %gram.1 = (f32[256,768]{1,0:T(8,128)S(1)}, f32[256,256]{1,0:T(8,128)S(1)}) custom-call(s32[7]{0:T(128)S(1)} %get-tuple-element.76.at_ref, f32[64,768]{1,0:T(8,128)S(1)} %get-tuple-element.88.pa_ref.own, f32[64,768]{1,0:T(8,128)S(1)} %collective-permute-done.1.pb_ref.pair, f32[64,768]{1,0:T(8,128)S(1)} %add.30.far.pa_ref, ...), custom_call_target="tpu_custom_call" | custom-call | tf_op jit(solution)/shard_map/gram/pallas_call | solution.py:143
  24.3 0.1 slice_select_fusion
  24.4 0.1 collective-permute-start.7
  24.5 2.0 %cross.4 = f32[1504,128]{1,0:T(8,128)S(1)} custom-call(s32[7]{0:T(128)S(1)} %get-tuple-element.76.at_ref, f32[64,768]{1,0:T(8,128)S(1)} %add.30.far.pa_ref, f32[64,768]{1,0:T(8,128)S(1)} %collective-permute-done.2.across.pb_ref, f32[3008,768]{1,0:T(8,128)S(1)} %bitcast.19), custom_call_target="tpu_custom_call" | custom-call | tf_op jit(solution)/shard_map/cross/pallas_call | solution.py:96
  26.4 0.0 collective-permute-done.7
  26.5 2.6 %collective-permute-done.8 = f32[752,128]{1,0:T(8,128)S(1)} collective-permute-done((f32[752,128]{1,0:T(8,128)S(1)}, f32[752,128]{1,0:T(8,128)S(1)}, u32[]{:S(2)}, u32[]{:S(2)}) %collective-permute-start.8) | collective-permute-done | bytes 385056 | tf_op jit(solution)/shard_map/ppermute | solution.py:350
  29.1 0.1 add.32
  29.1 0.1 collective-permute-start.10
  29.2 1.6 %collective-permute-start.9 = (f32[128,256]{1,0:T(8,128)S(1)}, f32[128,256]{1,0:T(8,128)S(1)}, u32[]{:S(2)}, u32[]{:S(2)}) collective-permute-start(f32[128,256]{1,0:T(8,128)S(1)} %add.31), channel_id=1, source_target_pairs={{0,8},{4,20},{8,0},{12,28},{16,24},{20,4},{24,16},{28,12},{1,9},{5... | collective-permute-start | bytes 393224 | tf_op jit(solution)/shard_map/ppermute | solution.py:350
  30.8 1.5 %collective-permute-start.11 = (f32[752,128]{1,0:T(8,128)S(1)}, f32[752,128]{1,0:T(8,128)S(1)}, u32[]{:S(2)}, u32[]{:S(2)}) collective-permute-start(f32[752,128]{1,0:T(8,128)S(1)} %add.32), channel_id=1, source_target_pairs={{0,16},{4,12},{8,24},{12,4},{16,0},{20,28},{24,8},{28,20},{1,17},{... | collective-permute-start | bytes 1155080 | tf_op jit(solution)/shard_map/ppermute | solution.py:350
  32.3 2.0 %cross.5 = f32[1504,128]{1,0:T(8,128)S(1)} custom-call(s32[7]{0:T(128)S(1)} %get-tuple-element.76.at_ref, f32[64,768]{1,0:T(8,128)S(1)} %add.30.far.pa_ref, f32[64,768]{1,0:T(8,128)S(1)} %collective-permute-done.2.across.pb_ref, f32[3008,768]{1,0:T(8,128)S(1)} %bitcast.20), custom_call_target="tpu_custom_call" | custom-call | tf_op jit(solution)/shard_map/cross/pallas_call | solution.py:96
  34.3 0.7 %collective-permute-done.9 = f32[128,256]{1,0:T(8,128)S(1)} collective-permute-done((f32[128,256]{1,0:T(8,128)S(1)}, f32[128,256]{1,0:T(8,128)S(1)}, u32[]{:S(2)}, u32[]{:S(2)}) %collective-permute-start.9) | collective-permute-done | bytes 131104 | tf_op jit(solution)/shard_map/ppermute | solution.py:350
  35.0 0.0 collective-permute-done.10
  35.0 0.1 broadcast_select_fusion.4
  35.2 1.6 %collective-permute-start.12 = (f32[752,128]{1,0:T(8,128)S(1)}, f32[752,128]{1,0:T(8,128)S(1)}, u32[]{:S(2)}, u32[]{:S(2)}) collective-permute-start(f32[752,128]{1,0:T(8,128)S(1)} %get-tuple-element.103), channel_id=1, source_target_pairs={{0,8},{4,20},{8,0},{12,28},{16,24},{20,4},{24,16},{28,12},{1,9},{5... | collective-permute-start | bytes 1155080 | tf_op jit(solution)/shard_map/ppermute | solution.py:350
  36.8 2.2 %collective-permute-start.13 = (f32[128,256]{1,0:T(8,128)S(1)}, f32[128,256]{1,0:T(8,128)S(1)}, u32[]{:S(2)}, u32[]{:S(2)}) collective-permute-start(f32[128,256]{1,0:T(8,128)S(1)} %add.33), channel_id=1, source_target_pairs={{0,16},{4,12},{8,24},{12,4},{16,0},{20,28},{24,8},{28,20},{1,17},{... | collective-permute-start | bytes 393224 | tf_op jit(solution)/shard_map/ppermute | solution.py:350
  38.9 1.0 %collective-permute-done.11 = f32[752,128]{1,0:T(8,128)S(1)} collective-permute-done((f32[752,128]{1,0:T(8,128)S(1)}, f32[752,128]{1,0:T(8,128)S(1)}, u32[]{:S(2)}, u32[]{:S(2)}) %collective-permute-start.11) | collective-permute-done | bytes 385056 | tf_op jit(solution)/shard_map/ppermute | solution.py:350
  39.9 0.1 add.36
  40.0 4.0 %collective-permute-done.12 = f32[752,128]{1,0:T(8,128)S(1)} collective-permute-done((f32[752,128]{1,0:T(8,128)S(1)}, f32[752,128]{1,0:T(8,128)S(1)}, u32[]{:S(2)}, u32[]{:S(2)}) %collective-permute-start.12) | collective-permute-done | bytes 385056 | tf_op jit(solution)/shard_map/ppermute | solution.py:350
  44.0 0.2 collective-permute-start.14
  44.2 1.5 %collective-permute-start.15 = (f32[752,128]{1,0:T(8,128)S(1)}, f32[752,128]{1,0:T(8,128)S(1)}, u32[]{:S(2)}, u32[]{:S(2)}) collective-permute-start(f32[752,128]{1,0:T(8,128)S(1)} %add.36), channel_id=1, source_target_pairs={{0,8},{4,20},{8,0},{12,28},{16,24},{20,4},{24,16},{28,12},{1,9},{5... | collective-permute-start | bytes 1155080 | tf_op jit(solution)/shard_map/ppermute | solution.py:350
  45.6 1.2 %collective-permute-start.16 = (f32[752,128]{1,0:T(8,128)S(1)}, f32[752,128]{1,0:T(8,128)S(1)}, u32[]{:S(2)}, u32[]{:S(2)}) collective-permute-start(f32[752,128]{1,0:T(8,128)S(1)} %add.37), channel_id=1, source_target_pairs={{0,16},{4,12},{8,24},{12,4},{16,0},{20,28},{24,8},{28,20},{1,17},{... | collective-permute-start | bytes 1155080 | tf_op jit(solution)/shard_map/ppermute | solution.py:350
  46.8 0.0 collective-permute-done.14
  46.8 0.1 broadcast_select_fusion.7
  46.9 2.8 %factor.4 = (f32[64,256]{1,0:T(8,128)S(1)}, f32[192,192]{1,0:T(8,128)S(1)}, f32[192,256]{1,0:T(8,128)S(1)}) custom-call(f32[256,256]{1,0:T(8,128)S(1)} %pad_maximum_fusion.2.s_ref), custom_call_target="tpu_custom_call" | custom-call | tf_op jit(solution)/shard_map/factor/pallas_call | solution.py:237
  49.7 2.6 %factor.5 = (f32[64,256]{1,0:T(8,128)S(1)}, f32[128,128]{1,0:T(8,128)S(1)}, f32[128,256]{1,0:T(8,128)S(1)}) custom-call(f32[192,192]{1,0:T(8,128)S(1)} %get-tuple-element.113.s_ref, f32[192,256]{1,0:T(8,128)S(1)} %get-tuple-element.114.rest_0_), custom_call_target="tpu_custom_call" | custom-call | tf_op jit(solution)/shard_map/factor/pallas_call | solution.py:237
  52.3 2.7 %factor.6 = (f32[64,256]{1,0:T(8,128)S(1)}, f32[64,64]{1,0:T(8,128)S(1)}, f32[64,256]{1,0:T(8,128)S(1)}) custom-call(f32[128,128]{1,0:T(8,128)S(1)} %get-tuple-element.117.s_ref, f32[128,256]{1,0:T(8,128)S(1)} %get-tuple-element.118.rest_0_), custom_call_target="tpu_custom_call" | custom-call | tf_op jit(solution)/shard_map/factor/pallas_call | solution.py:237
  55.0 2.1 %factor.7.x3 = f32[64,256]{1,0:T(8,128)S(1)} custom-call(f32[64,64]{1,0:T(8,128)S(1)} %get-tuple-element.121.s_ref, f32[64,256]{1,0:T(8,128)S(1)} %get-tuple-element.122.rest_0_), custom_call_target="tpu_custom_call" | custom-call | tf_op jit(solution)/shard_map/factor/pallas_call | solution.py:237
  57.2 0.1 add.39
  57.2 0.1 broadcast_select_fusion.3
  57.3 0.1 pad_maximum_fusion.refs_0_
  57.4 0.1 collective-permute-start.18
  57.4 0.9 %collective-permute-start.17 = (f32[752,128]{1,0:T(8,128)S(1)}, f32[752,128]{1,0:T(8,128)S(1)}, u32[]{:S(2)}, u32[]{:S(2)}) collective-permute-start(f32[752,128]{1,0:T(8,128)S(1)} %add.39), channel_id=1, source_target_pairs={{0,8},{4,20},{8,0},{12,28},{16,24},{20,4},{24,16},{28,12},{1,9},{5... | collective-permute-start | bytes 1155080 | tf_op jit(solution)/shard_map/ppermute | solution.py:350
  58.3 0.8 %finish.1 = (bf16[256,256]{1,0:T(8,128)(2,1)S(1)}, bf16[256,256]{1,0:T(8,128)(2,1)S(1)}, bf16[256,768]{1,0:T(8,128)(2,1)S(1)}, bf16[256,768]{1,0:T(8,128)(2,1)S(1)}) custom-call(f32[64,256]{1,0:T(8,128)S(1)} %get-tuple-element.111.x0, f32[64,256]{1,0:T(8,128)S(1)} %get-tuple-element.115.x1, f32[64,256]{1,0:T(8,128)S(1)} %get-tuple-element.119.x2, ...), custom_call_target="tpu_custom_call" | custom-call | tf_op jit(solution)/shard_map/finish/pallas_call | solution.py:256
  59.1 0.6 collective-permute-done.18.refs_1_
  59.7 5.2 %update.3 = (f32[3008,256]{1,0:T(8,128)}, f32[3008,768]{1,0:T(8,128)}) custom-call(s32[7]{0:T(128)S(1)} %get-tuple-element.76.at_ref, bf16[256,256]{1,0:T(8,128)(2,1)S(1)} %get-tuple-element.130.lh_ref, bf16[256,256]{1,0:T(8,128)(2,1)S(1)} %get-tuple-element.131.ll_ref, bf16[256,768]{1,0:T(8,128)(2,1)S(1)} %get-tuple-element.132.qh_ref, ...), custom_call_target="tpu_custom_call" | custom-call | tf_op jit(solution)/shard_map/update/pallas_call | solution.py:329
  64.9 0.3 collective-permute-done.17
  65.2 0.1 broadcast_select_fusion.1
  65.3 0.1 pad_maximum_fusion.1.refs_0_
  65.3 0.1 collective-permute-start.19
  65.4 2.5 %update.4 = (f32[752,256]{1,0:T(8,128)S(1)}, f32[752,768]{1,0:T(8,128)S(1)}) custom-call(s32[7]{0:T(128)S(1)} %get-tuple-element.76.at_ref, bf16[256,256]{1,0:T(8,128)(2,1)S(1)} %get-tuple-element.130.lh_ref, bf16[256,256]{1,0:T(8,128)(2,1)S(1)} %get-tuple-element.131.ll_ref, bf16[256,768]{1,0:T(8,128)(2,1)S(1)} %get-tuple-element.132.qh_ref, ...), custom_call_target="tpu_custom_call" | custom-call | tf_op jit(solution)/shard_map/update/pallas_call | solution.py:329
  68.0 0.0 collective-permute-done.19.refs_0_
  68.0 3.7 %update.5 = (f32[3008,256]{1,0:T(8,128)}, f32[3008,768]{1,0:T(8,128)}) custom-call(s32[7]{0:T(128)S(1)} %get-tuple-element.76.at_ref, bf16[256,256]{1,0:T(8,128)(2,1)S(1)} %get-tuple-element.130.lh_ref, bf16[256,256]{1,0:T(8,128)(2,1)S(1)} %get-tuple-element.131.ll_ref, ...), custom_call_target="tpu_custom_call", output_to_operand_aliasing={{0}: (9, {}), {1}: (10, {})} | custom-call | tf_op jit(solution)/shard_map/update/pallas_call | solution.py:329
  (16 shorter events, 0.2 us)
Async XLA Ops:
  0.8 13.5 %collective-permute-start = (f32[64,768]{1,0:T(8,128)}, f32[64,768]{1,0:T(8,128)S(1)}, u32[]{:S(2)}, u32[]{:S(2)}) collective-permute-start(f32[64,768]{1,0:T(8,128)} %bitcast.24), channel_id=1, source_target_pairs={{0,2},{1,3},{2,0},{3,1},{4,6},{5,7},{6,4},{7,5},{8,10},{9,11},{10,... | collective-permute-start | bytes 589832 | tf_op jit(solution)/shard_map/ppermute | solution.py:424
  4.9 10.2 %collective-permute-start.1 = (f32[64,768]{1,0:T(8,128)}, f32[64,768]{1,0:T(8,128)S(1)}, u32[]{:S(2)}, u32[]{:S(2)}) collective-permute-start(f32[64,768]{1,0:T(8,128)} %bitcast.25), channel_id=1, source_target_pairs={{0,1},{1,0},{2,3},{3,2},{4,5},{5,4},{6,7},{7,6},{8,9},{9,8},{10,11... | collective-permute-start | bytes 589832 | tf_op jit(solution)/shard_map/ppermute | solution.py:424
  6.5 3.6 %copy-start = (f32[768,3008]{0,1:T(8,128)S(1)}, f32[768,3008]{0,1:T(8,128)}, u32[]{:S(2)}) copy-start(f32[768,3008]{0,1:T(8,128)} %param.3) | copy-start | bytes 27721732
  10.1 0.9 %copy-start.2 = (f32[768,64]{0,1:T(8,128)S(1)}, f32[768,64]{0,1:T(8,128)}, u32[]{:S(2)}) copy-start(f32[768,64]{0,1:T(8,128)} %param.2) | copy-start | bytes 589828
  11.0 4.1 %copy-start.1 = (f32[768,3008]{0,1:T(8,128)S(1)}, f32[768,3008]{0,1:T(8,128)}, u32[]{:S(2)}) copy-start(f32[768,3008]{0,1:T(8,128)} %param.3) | copy-start | bytes 27721732
  14.3 6.1 %collective-permute-start.2 = (f32[64,768]{1,0:T(8,128)S(1)}, f32[64,768]{1,0:T(8,128)S(1)}, u32[]{:S(2)}, u32[]{:S(2)}) collective-permute-start(f32[64,768]{1,0:T(8,128)S(1)} %add.30.far.pa_ref), channel_id=1, source_target_pairs={{0,1},{1,0},{2,3},{3,2},{4,5},{5,4},{6,7},{7,6},{8,9},{9,8},{10,11... | collective-permute-start | bytes 589832 | tf_op jit(solution)/shard_map/ppermute | solution.py:424
  18.4 2.1 %collective-permute-start.4 = (f32[376,128]{1,0:T(8,128)S(1)}, f32[376,128]{1,0:T(8,128)S(1)}, u32[]{:S(2)}, u32[]{:S(2)}) collective-permute-start(f32[376,128]{1,0:T(8,128)S(1)} %get-tuple-element.84), channel_id=1, source_target_pairs={{0,4},{4,0},{8,12},{12,8},{16,20},{20,16},{24,28},{28,24},{1,5},{5... | collective-permute-start | bytes 577544 | tf_op jit(solution)/shard_map/ppermute | solution.py:350
  18.4 2.0 %collective-permute-start.5 = (f32[376,128]{1,0:T(8,128)S(1)}, f32[376,128]{1,0:T(8,128)S(1)}, u32[]{:S(2)}, u32[]{:S(2)}) collective-permute-start(f32[376,128]{1,0:T(8,128)S(1)} %get-tuple-element.85), channel_id=1, source_target_pairs={{0,4},{4,0},{8,12},{12,8},{16,20},{20,16},{24,28},{28,24},{1,5},{5... | collective-permute-start | bytes 577544 | tf_op jit(solution)/shard_map/ppermute | solution.py:350
  18.9 1.5 %collective-permute-start.6 = (f32[376,128]{1,0:T(8,128)S(1)}, f32[376,128]{1,0:T(8,128)S(1)}, u32[]{:S(2)}, u32[]{:S(2)}) collective-permute-start(f32[376,128]{1,0:T(8,128)S(1)} %get-tuple-element.86), channel_id=1, source_target_pairs={{0,4},{4,0},{8,12},{12,8},{16,20},{20,16},{24,28},{28,24},{1,5},{5... | collective-permute-start | bytes 577544 | tf_op jit(solution)/shard_map/ppermute | solution.py:350
  19.0 1.7 %collective-permute-start.3 = (f32[376,128]{1,0:T(8,128)S(1)}, f32[376,128]{1,0:T(8,128)S(1)}, u32[]{:S(2)}, u32[]{:S(2)}) collective-permute-start(f32[376,128]{1,0:T(8,128)S(1)} %get-tuple-element.82), channel_id=1, source_target_pairs={{0,4},{4,0},{8,12},{12,8},{16,20},{20,16},{24,28},{28,24},{1,5},{5... | collective-permute-start | bytes 577544 | tf_op jit(solution)/shard_map/ppermute | solution.py:350
  21.3 7.8 %collective-permute-start.8 = (f32[752,128]{1,0:T(8,128)S(1)}, f32[752,128]{1,0:T(8,128)S(1)}, u32[]{:S(2)}, u32[]{:S(2)}) collective-permute-start(f32[752,128]{1,0:T(8,128)S(1)} %get-tuple-element.87), channel_id=1, source_target_pairs={{0,8},{4,20},{8,0},{12,28},{16,24},{20,4},{24,16},{28,12},{1,9},{5... | collective-permute-start | bytes 1155080 | tf_op jit(solution)/shard_map/ppermute | solution.py:350
  24.4 2.1 %collective-permute-start.7 = (f32[128,256]{1,0:T(8,128)S(1)}, f32[128,256]{1,0:T(8,128)S(1)}, u32[]{:S(2)}, u32[]{:S(2)}) collective-permute-start(f32[128,256]{1,0:T(8,128)S(1)} %get-tuple-element.90), channel_id=1, source_target_pairs={{0,4},{4,0},{8,12},{12,8},{16,20},{20,16},{24,28},{28,24},{1,5},{5... | collective-permute-start | bytes 393224 | tf_op jit(solution)/shard_map/ppermute | solution.py:350
  29.1 5.9 %collective-permute-start.10 = (f32[1504,128]{1,0:T(8,128)S(1)}, f32[1504,128]{1,0:T(8,128)S(1)}, u32[]{:S(2)}, u32[]{:S(2)}) collective-permute-start(f32[1504,128]{1,0:T(8,128)S(1)} %cross.4), channel_id=1, source_target_pairs={{0,4},{4,0},{8,12},{12,8},{16,20},{20,16},{24,28},{28,24},{1,5},{5... | collective-permute-start | bytes 2310152 | tf_op jit(solution)/shard_map/ppermute | solution.py:350
  29.2 5.8 %collective-permute-start.9 = (f32[128,256]{1,0:T(8,128)S(1)}, f32[128,256]{1,0:T(8,128)S(1)}, u32[]{:S(2)}, u32[]{:S(2)}) collective-permute-start(f32[128,256]{1,0:T(8,128)S(1)} %add.31), channel_id=1, source_target_pairs={{0,8},{4,20},{8,0},{12,28},{16,24},{20,4},{24,16},{28,12},{1,9},{5... | collective-permute-start | bytes 393224 | tf_op jit(solution)/shard_map/ppermute | solution.py:350
  30.8 9.1 %collective-permute-start.11 = (f32[752,128]{1,0:T(8,128)S(1)}, f32[752,128]{1,0:T(8,128)S(1)}, u32[]{:S(2)}, u32[]{:S(2)}) collective-permute-start(f32[752,128]{1,0:T(8,128)S(1)} %add.32), channel_id=1, source_target_pairs={{0,16},{4,12},{8,24},{12,4},{16,0},{20,28},{24,8},{28,20},{1,17},{... | collective-permute-start | bytes 1155080 | tf_op jit(solution)/shard_map/ppermute | solution.py:350
  35.2 8.7 %collective-permute-start.12 = (f32[752,128]{1,0:T(8,128)S(1)}, f32[752,128]{1,0:T(8,128)S(1)}, u32[]{:S(2)}, u32[]{:S(2)}) collective-permute-start(f32[752,128]{1,0:T(8,128)S(1)} %get-tuple-element.103), channel_id=1, source_target_pairs={{0,8},{4,20},{8,0},{12,28},{16,24},{20,4},{24,16},{28,12},{1,9},{5... | collective-permute-start | bytes 1155080 | tf_op jit(solution)/shard_map/ppermute | solution.py:350
  36.8 7.2 %collective-permute-start.13 = (f32[128,256]{1,0:T(8,128)S(1)}, f32[128,256]{1,0:T(8,128)S(1)}, u32[]{:S(2)}, u32[]{:S(2)}) collective-permute-start(f32[128,256]{1,0:T(8,128)S(1)} %add.33), channel_id=1, source_target_pairs={{0,16},{4,12},{8,24},{12,4},{16,0},{20,28},{24,8},{28,20},{1,17},{... | collective-permute-start | bytes 393224 | tf_op jit(solution)/shard_map/ppermute | solution.py:350
  44.0 2.8 %collective-permute-start.14 = (f32[128,256]{1,0:T(8,128)S(1)}, f32[128,256]{1,0:T(8,128)S(1)}, u32[]{:S(2)}, u32[]{:S(2)}) collective-permute-start(f32[128,256]{1,0:T(8,128)S(1)} %add.38), channel_id=1, source_target_pairs={{0,4},{4,0},{8,12},{12,8},{16,20},{20,16},{24,28},{28,24},{1,5},{5... | collective-permute-start | bytes 393224 | tf_op jit(solution)/shard_map/ppermute | solution.py:350
  44.2 13.0 %collective-permute-start.15 = (f32[752,128]{1,0:T(8,128)S(1)}, f32[752,128]{1,0:T(8,128)S(1)}, u32[]{:S(2)}, u32[]{:S(2)}) collective-permute-start(f32[752,128]{1,0:T(8,128)S(1)} %add.36), channel_id=1, source_target_pairs={{0,8},{4,20},{8,0},{12,28},{16,24},{20,4},{24,16},{28,12},{1,9},{5... | collective-permute-start | bytes 1155080 | tf_op jit(solution)/shard_map/ppermute | solution.py:350
  45.6 11.5 %collective-permute-start.16 = (f32[752,128]{1,0:T(8,128)S(1)}, f32[752,128]{1,0:T(8,128)S(1)}, u32[]{:S(2)}, u32[]{:S(2)}) collective-permute-start(f32[752,128]{1,0:T(8,128)S(1)} %add.37), channel_id=1, source_target_pairs={{0,16},{4,12},{8,24},{12,4},{16,0},{20,28},{24,8},{28,20},{1,17},{... | collective-permute-start | bytes 1155080 | tf_op jit(solution)/shard_map/ppermute | solution.py:350
  57.4 2.3 %collective-permute-start.18 = (f32[752,256]{1,0:T(8,128)S(1)}, f32[752,256]{1,0:T(8,128)S(1)}, u32[]{:S(2)}, u32[]{:S(2)}) collective-permute-start(f32[752,256]{1,0:T(8,128)S(1)} %pad_maximum_fusion.refs_0_), channel_id=1, source_target_pairs={{0,4},{4,0},{8,12},{12,8},{16,20},{20,16},{24,28},{28,24},{1,5},{5... | collective-permute-start | bytes 2310152 | tf_op jit(solution)/shard_map/ppermute | solution.py:350
  57.4 7.8 %collective-permute-start.17 = (f32[752,128]{1,0:T(8,128)S(1)}, f32[752,128]{1,0:T(8,128)S(1)}, u32[]{:S(2)}, u32[]{:S(2)}) collective-permute-start(f32[752,128]{1,0:T(8,128)S(1)} %add.39), channel_id=1, source_target_pairs={{0,8},{4,20},{8,0},{12,28},{16,24},{20,4},{24,16},{28,12},{1,9},{5... | collective-permute-start | bytes 1155080 | tf_op jit(solution)/shard_map/ppermute | solution.py:350
  65.3 2.6 %collective-permute-start.19 = (f32[752,256]{1,0:T(8,128)S(1)}, f32[752,256]{1,0:T(8,128)S(1)}, u32[]{:S(2)}, u32[]{:S(2)}) collective-permute-start(f32[752,256]{1,0:T(8,128)S(1)} %pad_maximum_fusion.1.refs_0_), channel_id=1, source_target_pairs={{0,4},{4,0},{8,12},{12,8},{16,20},{20,16},{24,28},{28,24},{1,5},{5... | collective-permute-start | bytes 2310152 | tf_op jit(solution)/shard_map/ppermute | solution.py:350

commit v5 on v4

--- a/solution.py
+++ b/solution.py
@@ -102,31 +102,6 @@
         cost_estimate=cost(),
         name="cross",
     )(at, pa, pb, t)
-
-
-def halve_kernel(at_ref, keep_ref, *refs):
-    *got_refs, keep_out, send_out = refs
-    m = got_refs[0].shape[0]
-    upper = at_ref[SIDE + 1] != 0
-    h = len(got_refs) // 2
-    for j in range(h):
-        low = keep_ref[j * m : (j + 1) * m, :] + got_refs[j][...]
-        high = keep_ref[(j + h) * m : (j + h + 1) * m, :] + got_refs[j + h][...]
-        keep_out[j * m : (j + 1) * m, :] = jnp.where(upper, high, low)
-        send_out[j * m : (j + 1) * m, :] = jnp.where(upper, low, high)
-
-
-def halve(at, keep, got):
-    m, n = keep.shape
-    return pl.pallas_call(
-        halve_kernel,
-        out_shape=[jax.ShapeDtypeStruct((m // 2, n), F32)] * 2,
-        in_specs=[SMEM] + [VM] * (1 + len(got)),
-        out_specs=[VM] * 2,
-        compiler_params=params(),
-        cost_estimate=cost(),
-        name="halve",
-    )(at, keep, *got)
 
 
 def gram_kernel(at_ref, own, pair, far, across, p_full, g_ref):
@@ -202,66 +177,64 @@
     return scaled
 
 
-def factor_kernel(s_ref, *rest, first, last):
-    left = s_ref.shape[0]
-    if first:
-        x_ref, *rest = rest
-        j0 = lax.broadcasted_iota(jnp.int32, (left, left), 0)
-        j1 = lax.broadcasted_iota(jnp.int32, (left, left), 1)
-        right = (j0 == j1).astype(F32)
-    else:
-        r_ref, x_ref, *rest = rest
-        right = r_ref[...]
+def factor_steps(s, right, steps):
     i0 = lax.broadcasted_iota(jnp.int32, (NB, NB), 0)
     i1 = lax.broadcasted_iota(jnp.int32, (NB, NB), 1)
     eye = (i0 == i1).astype(F32)
-    augmented = jnp.concatenate([s_ref[:NB, :NB], eye], axis=1)
-    rows = eliminate([augmented[8 * i : 8 * i + 8] for i in range(NB // 8)])
-    inv = jnp.concatenate(rows, axis=0)[:, NB:]
-    x = dot(inv, right[:NB, :], NN, HIGHEST)
-    x_ref[...] = x
-    if not last:
-        s_out, r_out = rest
-        u = dot(inv, s_ref[:NB, NB:], NN, HIGHEST)
-        s_out[...] = s_ref[NB:, NB:] - dot(u, u, TN, HIGHEST)
-        r_out[...] = right[NB:, :] - dot(u, x, TN, HIGHEST)
-
-
-def factor_step(s, r=None):
-    left = s.shape[0]
-    n = left if r is None else r.shape[1]
-    last = left == NB
-    outs = [jax.ShapeDtypeStruct((NB, n), F32)]
-    if not last:
-        outs += [jax.ShapeDtypeStruct((left - NB, left - NB), F32), jax.ShapeDtypeStruct((left - NB, n), F32)]
-    return pl.pallas_call(
-        functools.partial(factor_kernel, first=r is None, last=last),
-        out_shape=outs,
-        in_specs=[VM] * (1 if r is None else 2),
-        out_specs=[VM] * len(outs),
-        compiler_params=params(),
-        cost_estimate=cost(),
-        name="factor",
-    )(s, *(() if r is None else (r,)))
-
-
-def finish_kernel(x0, x1, x2, x3, p_ref, lh_ref, ll_ref, qh_ref, ql_ref):
-    linv = jnp.concatenate([x0[...], x1[...], x2[...], x3[...]], axis=0)
+    xs = []
+    for _ in range(steps):
+        augmented = jnp.concatenate([s[:NB, :NB], eye], axis=1)
+        rows = eliminate([augmented[8 * i : 8 * i + 8] for i in range(NB // 8)])
+        inv = jnp.concatenate(rows, axis=0)[:, NB:]
+        x = dot(inv, right[:NB, :], NN, HIGHEST)
+        xs.append(x)
+        if s.shape[0] > NB:
+            u = dot(inv, s[:NB, NB:], NN, HIGHEST)
+            s = s[NB:, NB:] - dot(u, u, TN, HIGHEST)
+            right = right[NB:, :] - dot(u, x, TN, HIGHEST)
+    return xs, s, right
+
+
+def begin_kernel(g_ref, x_ref, s_ref, r_ref):
+    n = g_ref.shape[0]
+    j0 = lax.broadcasted_iota(jnp.int32, (n, n), 0)
+    j1 = lax.broadcasted_iota(jnp.int32, (n, n), 1)
+    xs, s_ref[...], r_ref[...] = factor_steps(g_ref[...], (j0 == j1).astype(F32), x_ref.shape[0] // NB)
+    x_ref[...] = jnp.concatenate(xs, axis=0)
+
+
+def begin(g):
+    n = g.shape[0]
+    shapes = [(n - NB, n), (NB, NB), (NB, n)]
+    return pl.pallas_call(
+        begin_kernel,
+        out_shape=[jax.ShapeDtypeStruct(s, F32) for s in shapes],
+        in_specs=[VM],
+        out_specs=[VM] * 3,
+        compiler_params=params(),
+        cost_estimate=cost(),
+        name="begin",
+    )(g)
+
+
+def finish_kernel(x_ref, s_ref, r_ref, p_ref, lh_ref, ll_ref, qh_ref, ql_ref):
+    (x,), _, _ = factor_steps(s_ref[...], r_ref[...], 1)
+    linv = jnp.concatenate([x_ref[...], x], axis=0)
     lh_ref[...], ll_ref[...] = split(linv)
     qh_ref[...], ql_ref[...] = split(dot(linv, p_ref[...], NN, HIGHEST))
 
 
-def finish(xs, p_t):
+def finish(x, s, r, p_t):
     n, k = p_t.shape
     return pl.pallas_call(
         finish_kernel,
         out_shape=[jax.ShapeDtypeStruct((n, n), BF16)] * 2 + [jax.ShapeDtypeStruct((n, k), BF16)] * 2,
-        in_specs=[VM] * 5,
+        in_specs=[VM] * 4,
         out_specs=[VM] * 4,
         compiler_params=params(),
         cost_estimate=cost(),
         name="finish",
-    )(*xs, p_t)
+    )(x, s, r, p_t)
 
 
 def quarter_start(at_ref, place, rows):
@@ -293,18 +266,18 @@
     p_here, r_here = outs[:2]
     lh, ll, qh, ql = lh_ref[...], ll_ref[...], qh_ref[...], ql_ref[...]
     m = c_refs[0].shape[0]
-    b = m // 2 if last and m % 16 == 0 else m
+    cuts = [0, m // 2, m - m // 4 // 8 * 8, m] if last and m % 16 == 0 else [0, m]
     for j, (c_ref, place) in enumerate(zip(c_refs, places)):
         start = quarter_start(at_ref, place, rows)
-        for i in range(m // b):
-            here, there = pl.ds(j * m + i * b, b), pl.ds(start + i * b, b)
-            c_hi, c_lo = split(c_ref[i * b : (i + 1) * b, :])
+        for i, (low, high) in enumerate(zip(cuts, cuts[1:])):
+            here, there = pl.ds(j * m + low, high - low), pl.ds(start + low, high - low)
+            c_hi, c_lo = split(c_ref[low:high, :])
             p = dot(c_hi, lh, NT) + dot(c_lo, lh, NT) + dot(c_hi, ll, NT)
             p_here[here, :] = p
             p_hi, p_lo = split(p)
             r_here[here, :] = t_ref[there, :] - (dot(p_hi, qh, NN) + dot(p_lo, qh, NN) + dot(p_hi, ql, NN))
             if last:
-                s = len(carried) + j * (m // b) + i
+                s = len(carried) + j * (len(cuts) - 1) + i
                 copies += [
                     pltpu.make_async_copy(p_here.at[here], p_out.at[there], sems.at[0, s]),
                     pltpu.make_async_copy(r_here.at[here], r_out.at[there], sems.at[1, s]),
@@ -322,7 +295,7 @@
     own = [((h, n), F32), ((h, k), F32)]
     if last:
         out = [jax.ShapeDtypeStruct((m, n), F32), jax.ShapeDtypeStruct((m, k), F32)]
-        scratch = [pltpu.VMEM(*x) for x in own] + [pltpu.SemaphoreType.DMA((2, len(carried) + 2 * len(pieces)))]
+        scratch = [pltpu.VMEM(*x) for x in own] + [pltpu.SemaphoreType.DMA((2, len(carried) + 3 * len(pieces)))]
     else:
         out, scratch = [jax.ShapeDtypeStruct(*x) for x in own], []
     inputs = [at, *parts, *pieces.values(), t, *carry]
@@ -437,7 +410,13 @@
     if nz == 4:
         got_a = [rows.swap(x, 0) for x in out_a]
         o.last = (out_a[0], across)
-        a, out_a = o.run(lambda x: halve(at, x, got_a), a)
+        def cut_pieces(x):
+            q = got_a[0].shape[0]
+            x = [x[i * q : (i + 1) * q] + y for i, y in enumerate(got_a)]
+            pairs = [pick(upper[1], low, high) for low, high in zip(x[:2], x[2:])]
+            return [jnp.concatenate(z) for z in zip(*pairs)]
+
+        a, out_a = o.run(cut_pieces, a)
         o.last = out_a
     else:
         a, out_a = cut(1, a, send(out_a, 0))
@@ -476,18 +455,15 @@
     got_b = send(b, end)
     a_chip = send(a, 1)
     g = put(0, g, got_g)
-    x0, g, r = o.run(factor_step, g)
-    x1, g, r = o.run(factor_step, g, r)
-    x2, g, r = o.run(factor_step, g, r)
-    (x3,) = o.run(factor_step, g, r)
-    o.last = (x3, a_chip)
+    x, s_left, r_left = o.run(begin, g)
+    o.last = (x, a_chip)
     b = add(b, got_b)
     for s in range(end - 1, 1, -1):
         b = put(s, b, send(b, s))
     b_chip = send(b, 1)
     c = columns(a, b)
     c_core = send(c, 0)
-    parts = o.run(lambda x: finish((x0, x1, x2, x3), x), p_full)
+    parts = o.run(lambda p: finish(x, s_left, r_left, p), p_full)
     outs = o.run(lambda x: update(at, parts, {(0, 0): c, (1, 0): x}, t), c_core)
     c_chip = columns(a_chip, b_chip)
     c_both = send(c_chip, 0)

time: 72 us -> 71.8 us (level)
  Pallas kernels: 32.8 us -> 31.5 us
  starting transfers between devices: 19.9 us -> 20.8 us
    pallas_call x5 -> x1, Pallas kernels: 10.8 us -> 7.86 us  [begin(): pl.pallas_call(begin_kernel, out_shape=[jax.ShapeDtypeStruct(s, F32) for...]
    pallas_call x1, Pallas kernels: 0.82 us -> 2.88 us  [finish(): pl.pallas_call(finish_kernel, out_shape=[jax.ShapeDtypeStruct((n, n), BF1...]
    ppermute x17, starting transfers between devices: 13.4 us -> 14.3 us  [swap(): lax.ppermute(x, 'row', [(r, r ^ 1 << by_core[r & 1]) for r in range(self....]
  transfers between devices with their start and end apart: 20 -> 20, of which waited for: 9 -> 8; matrix products, arithmetic and copies ran while one was open for 1% -> 1% of each run, Pallas kernels for 40% -> 39%
where the time goes in v5:
time: 71.8 us; the launch traced here: 71.6 us
  Pallas kernels  31.5 us (44%)
  starting transfers between devices  20.8 us (29%)
  waiting for transfers between devices  12.5 us (17%)
  local copies, waits for them, and re-layouts  4.66 us (6%)
  between operations  1.08 us (2%)
  other arithmetic  1 us (1%)
    ppermute x17, starting transfers between devices, swap(): lax.ppermute(x, 'row', [(r, r ^ 1 << by_core[r & 1]) for r in range(self....  14.3 us
    pallas_call x3, Pallas kernels, update(): pl.pallas_call(functools.partial(update_kernel, places=tuple(pieces), car...  11.1 us
    ppermute x17, waiting for transfers between devices, swap(): lax.ppermute(x, 'row', [(r, r ^ 1 << by_core[r & 1]) for r in range(self....  9.35 us
    pallas_call x1, Pallas kernels, begin(): pl.pallas_call(begin_kernel, out_shape=[jax.ShapeDtypeStruct(s, F32) for...  7.86 us
    pallas_call x3, Pallas kernels, cross(): pl.pallas_call(functools.partial(cross_kernel, halves=halves), out_shape=...  7.17 us
    ppermute x3, starting transfers between devices, flipped(): return lax.ppermute(x, 'col', [(z, z ^ flip) for z in range(nz)])  6.46 us
    unnamed x6, local copies, waits for them, and re-layouts  4.55 us
    ppermute x3, waiting for transfers between devices, flipped(): return lax.ppermute(x, 'col', [(z, z ^ flip) for z in range(nz)])  3.16 us
  transfers between devices with their start and end apart: 20, of which 8 were waited for; matrix products, arithmetic and copies ran while one was open for 1% of the time, Pallas kernels for 39%

profile of v5, /device:TPU:0, one launch (start us, length us, event | category | flops | bytes accessed | tf_op | source)
XLA Modules:
  0.0 71.6 jit_solution(867843180697980782)
XLA Ops:
  0.7 0.1 stack.31.at_ref
  0.8 4.1 %collective-permute-start = (f32[64,768]{1,0:T(8,128)}, f32[64,768]{1,0:T(8,128)S(1)}, u32[]{:S(2)}, u32[]{:S(2)}) collective-permute-start(f32[64,768]{1,0:T(8,128)} %bitcast.24), channel_id=1, source_target_pairs={{0,2},{1,3},{2,0},{3,1},{4,6},{5,7},{6,4},{7,5},{8,10},{9,11},{10,... | collective-permute-start | bytes 589832 | tf_op jit(solution)/shard_map/ppermute | solution.py:397
  4.9 1.6 %collective-permute-start.1 = (f32[64,768]{1,0:T(8,128)}, f32[64,768]{1,0:T(8,128)S(1)}, u32[]{:S(2)}, u32[]{:S(2)}) collective-permute-start(f32[64,768]{1,0:T(8,128)} %bitcast.25), channel_id=1, source_target_pairs={{0,1},{1,0},{2,3},{3,2},{4,5},{5,4},{6,7},{7,6},{8,9},{9,8},{10,11... | collective-permute-start | bytes 589832 | tf_op jit(solution)/shard_map/ppermute | solution.py:397
  6.5 3.6 %copy-done = f32[768,3008]{0,1:T(8,128)S(1)} copy-done((f32[768,3008]{0,1:T(8,128)S(1)}, f32[768,3008]{0,1:T(8,128)}, u32[]{:S(2)}) %copy-start) | copy-done | bytes 9240600
  10.1 0.9 %copy-done.2 = f32[768,64]{0,1:T(8,128)S(1)} copy-done((f32[768,64]{0,1:T(8,128)S(1)}, f32[768,64]{0,1:T(8,128)}, u32[]{:S(2)}) %copy-start.2) | copy-done | bytes 196632
  11.0 1.1 %touch.1 = (s32[7]{0:T(128)S(1)}, f32[64,768]{1,0:T(8,128)S(1)}, f32[64,768]{1,0:T(8,128)S(1)}) custom-call(s32[7]{0:T(128)S(1)} %stack.31.at_ref, f32[64,768]{1,0:T(8,128)S(1)} %bitcast.26, f32[3008,768]{1,0:T(8,128)S(1)} %bitcast.17), custom_call_target="tpu_custom_call" | custom-call | tf_op jit(solution)/shard_map/touch/pallas_call | solution.py:57
  12.2 2.2 %collective-permute-done = f32[64,768]{1,0:T(8,128)S(1)} collective-permute-done((f32[64,768]{1,0:T(8,128)}, f32[64,768]{1,0:T(8,128)S(1)}, u32[]{:S(2)}, u32[]{:S(2)}) %collective-permute-start) | collective-permute-done | bytes 196640 | tf_op jit(solution)/shard_map/ppermute | solution.py:397
  14.3 0.8 %collective-permute-start.2 = (f32[64,768]{1,0:T(8,128)S(1)}, f32[64,768]{1,0:T(8,128)S(1)}, u32[]{:S(2)}, u32[]{:S(2)}) collective-permute-start(f32[64,768]{1,0:T(8,128)S(1)} %add.42.far.pa_ref), channel_id=1, source_target_pairs={{0,1},{1,0},{2,3},{3,2},{4,5},{5,4},{6,7},{7,6},{8,9},{9,8},{10,11... | collective-permute-start | bytes 589832 | tf_op jit(solution)/shard_map/ppermute | solution.py:397
  15.1 0.0 collective-permute-done.1.pb_ref.pair
  15.1 0.0 copy-done.1
  15.1 3.2 %cross.3 = (f32[376,128]{1,0:T(8,128)S(1)}, f32[376,128]{1,0:T(8,128)S(1)}, f32[376,128]{1,0:T(8,128)S(1)}, f32[376,128]{1,0:T(8,128)S(1)}, f32[1504,128]{1,0:T(8,128)S(1)}) custom-call(s32[7]{0:T(128)S(1)} %get-tuple-element.65.at_ref, f32[64,768]{1,0:T(8,128)S(1)} %get-tuple-element.77.pa_ref.own, f32[64,768]{1,0:T(8,128)S(1)} %collective-permute-done.1.pb_ref.pair, ...), custom_call_target="tpu_custom_call" | custom-call | tf_op jit(solution)/shard_map/cross/pallas_call | solution.py:96
  18.4 0.1 collective-permute-start.4
  18.4 0.5 collective-permute-start.5
  18.9 0.1 collective-permute-start.6
  19.0 0.4 collective-permute-start.3
  19.4 1.0 %collective-permute-done.2.across.pb_ref = f32[64,768]{1,0:T(8,128)S(1)} collective-permute-done((f32[64,768]{1,0:T(8,128)S(1)}, f32[64,768]{1,0:T(8,128)S(1)}, u32[]{:S(2)}, u32[]{:S(2)}) %collective-permute-start.2) | collective-permute-done | bytes 196640 | tf_op jit(solution)/shard_map/ppermute | solution.py:397
  20.4 0.0 collective-permute-done.4
  20.4 0.0 collective-permute-done.5
  20.4 0.0 collective-permute-done.6
  20.4 0.2 collective-permute-done.3
  20.7 0.1 broadcast_select_fusion.7
  20.9 1.6 %collective-permute-start.8 = (f32[752,128]{1,0:T(8,128)S(1)}, f32[752,128]{1,0:T(8,128)S(1)}, u32[]{:S(2)}, u32[]{:S(2)}) collective-permute-start(f32[752,128]{1,0:T(8,128)S(1)} %pad_maximum_fusion.2), channel_id=1, source_target_pairs={{0,8},{4,20},{8,0},{12,28},{16,24},{20,4},{24,16},{28,12},{1,9},{5... | collective-permute-start | bytes 1155080 | tf_op jit(solution)/shard_map/ppermute | solution.py:323
  22.4 1.4 %gram.1 = (f32[256,768]{1,0:T(8,128)S(1)}, f32[256,256]{1,0:T(8,128)S(1)}) custom-call(s32[7]{0:T(128)S(1)} %get-tuple-element.65.at_ref, f32[64,768]{1,0:T(8,128)S(1)} %get-tuple-element.77.pa_ref.own, f32[64,768]{1,0:T(8,128)S(1)} %collective-permute-done.1.pb_ref.pair, f32[64,768]{1,0:T(8,128)S(1)} %add.42.far.pa_ref, ...), custom_call_target="tpu_custom_call" | custom-call | tf_op jit(solution)/shard_map/gram/pallas_call | solution.py:118
  23.9 0.1 slice_select_fusion
  23.9 0.1 collective-permute-start.7
  24.0 2.0 %cross.4 = f32[1504,128]{1,0:T(8,128)S(1)} custom-call(s32[7]{0:T(128)S(1)} %get-tuple-element.65.at_ref, f32[64,768]{1,0:T(8,128)S(1)} %add.42.far.pa_ref, f32[64,768]{1,0:T(8,128)S(1)} %collective-permute-done.2.across.pb_ref, f32[3008,768]{1,0:T(8,128)S(1)} %bitcast.19), custom_call_target="tpu_custom_call" | custom-call | tf_op jit(solution)/shard_map/cross/pallas_call | solution.py:96
  26.0 0.0 collective-permute-done.7
  26.0 2.6 %collective-permute-done.8 = f32[752,128]{1,0:T(8,128)S(1)} collective-permute-done((f32[752,128]{1,0:T(8,128)S(1)}, f32[752,128]{1,0:T(8,128)S(1)}, u32[]{:S(2)}, u32[]{:S(2)}) %collective-permute-start.8) | collective-permute-done | bytes 385056 | tf_op jit(solution)/shard_map/ppermute | solution.py:323
  28.6 0.1 add.48
  28.7 0.1 collective-permute-start.10
  28.8 1.6 %collective-permute-start.9 = (f32[128,256]{1,0:T(8,128)S(1)}, f32[128,256]{1,0:T(8,128)S(1)}, u32[]{:S(2)}, u32[]{:S(2)}) collective-permute-start(f32[128,256]{1,0:T(8,128)S(1)} %add.47), channel_id=1, source_target_pairs={{0,8},{4,20},{8,0},{12,28},{16,24},{20,4},{24,16},{28,12},{1,9},{5... | collective-permute-start | bytes 393224 | tf_op jit(solution)/shard_map/ppermute | solution.py:323
  30.3 1.5 %collective-permute-start.11 = (f32[752,128]{1,0:T(8,128)S(1)}, f32[752,128]{1,0:T(8,128)S(1)}, u32[]{:S(2)}, u32[]{:S(2)}) collective-permute-start(f32[752,128]{1,0:T(8,128)S(1)} %add.48), channel_id=1, source_target_pairs={{0,16},{4,12},{8,24},{12,4},{16,0},{20,28},{24,8},{28,20},{1,17},{... | collective-permute-start | bytes 1155080 | tf_op jit(solution)/shard_map/ppermute | solution.py:323
  31.8 2.0 %cross.5 = f32[1504,128]{1,0:T(8,128)S(1)} custom-call(s32[7]{0:T(128)S(1)} %get-tuple-element.65.at_ref, f32[64,768]{1,0:T(8,128)S(1)} %add.42.far.pa_ref, f32[64,768]{1,0:T(8,128)S(1)} %collective-permute-done.2.across.pb_ref, f32[3008,768]{1,0:T(8,128)S(1)} %bitcast.20), custom_call_target="tpu_custom_call" | custom-call | tf_op jit(solution)/shard_map/cross/pallas_call | solution.py:96
  33.8 0.7 %collective-permute-done.9 = f32[128,256]{1,0:T(8,128)S(1)} collective-permute-done((f32[128,256]{1,0:T(8,128)S(1)}, f32[128,256]{1,0:T(8,128)S(1)}, u32[]{:S(2)}, u32[]{:S(2)}) %collective-permute-start.9) | collective-permute-done | bytes 131104 | tf_op jit(solution)/shard_map/ppermute | solution.py:323
  34.6 0.0 collective-permute-done.10
  34.6 0.1 broadcast_select_fusion.4
  34.7 1.6 %collective-permute-start.12 = (f32[752,128]{1,0:T(8,128)S(1)}, f32[752,128]{1,0:T(8,128)S(1)}, u32[]{:S(2)}, u32[]{:S(2)}) collective-permute-start(f32[752,128]{1,0:T(8,128)S(1)} %get-tuple-element.90), channel_id=1, source_target_pairs={{0,8},{4,20},{8,0},{12,28},{16,24},{20,4},{24,16},{28,12},{1,9},{5... | collective-permute-start | bytes 1155080 | tf_op jit(solution)/shard_map/ppermute | solution.py:323
  36.3 2.2 %collective-permute-start.13 = (f32[128,256]{1,0:T(8,128)S(1)}, f32[128,256]{1,0:T(8,128)S(1)}, u32[]{:S(2)}, u32[]{:S(2)}) collective-permute-start(f32[128,256]{1,0:T(8,128)S(1)} %add.49), channel_id=1, source_target_pairs={{0,16},{4,12},{8,24},{12,4},{16,0},{20,28},{24,8},{28,20},{1,17},{... | collective-permute-start | bytes 393224 | tf_op jit(solution)/shard_map/ppermute | solution.py:323
  38.4 1.0 %collective-permute-done.11 = f32[752,128]{1,0:T(8,128)S(1)} collective-permute-done((f32[752,128]{1,0:T(8,128)S(1)}, f32[752,128]{1,0:T(8,128)S(1)}, u32[]{:S(2)}, u32[]{:S(2)}) %collective-permute-start.11) | collective-permute-done | bytes 385056 | tf_op jit(solution)/shard_map/ppermute | solution.py:323
  39.5 4.0 %collective-permute-done.12 = f32[752,128]{1,0:T(8,128)S(1)} collective-permute-done((f32[752,128]{1,0:T(8,128)S(1)}, f32[752,128]{1,0:T(8,128)S(1)}, u32[]{:S(2)}, u32[]{:S(2)}) %collective-permute-start.12) | collective-permute-done | bytes 385056 | tf_op jit(solution)/shard_map/ppermute | solution.py:323
  43.4 0.1 add.53
  43.5 0.0 collective-permute-done.13
  43.5 0.2 collective-permute-start.14
  43.7 1.5 %collective-permute-start.15 = (f32[752,128]{1,0:T(8,128)S(1)}, f32[752,128]{1,0:T(8,128)S(1)}, u32[]{:S(2)}, u32[]{:S(2)}) collective-permute-start(f32[752,128]{1,0:T(8,128)S(1)} %add.52), channel_id=1, source_target_pairs={{0,8},{4,20},{8,0},{12,28},{16,24},{20,4},{24,16},{28,12},{1,9},{5... | collective-permute-start | bytes 1155080 | tf_op jit(solution)/shard_map/ppermute | solution.py:323
  45.2 1.2 %collective-permute-start.16 = (f32[752,128]{1,0:T(8,128)S(1)}, f32[752,128]{1,0:T(8,128)S(1)}, u32[]{:S(2)}, u32[]{:S(2)}) collective-permute-start(f32[752,128]{1,0:T(8,128)S(1)} %add.53), channel_id=1, source_target_pairs={{0,16},{4,12},{8,24},{12,4},{16,0},{20,28},{24,8},{28,20},{1,17},{... | collective-permute-start | bytes 1155080 | tf_op jit(solution)/shard_map/ppermute | solution.py:323
  46.4 0.0 collective-permute-done.14
  46.4 0.1 broadcast_select_fusion.11
  46.5 7.9 %begin.1 = (f32[192,256]{1,0:T(8,128)S(1)}, f32[64,64]{1,0:T(8,128)S(1)}, f32[64,256]{1,0:T(8,128)S(1)}) custom-call(f32[256,256]{1,0:T(8,128)S(1)} %pad_maximum_fusion.4.g_ref), custom_call_target="tpu_custom_call" | custom-call | tf_op jit(solution)/shard_map/begin/pallas_call | solution.py:209
  54.3 0.8 %collective-permute-done.15 = f32[752,128]{1,0:T(8,128)S(1)} collective-permute-done((f32[752,128]{1,0:T(8,128)S(1)}, f32[752,128]{1,0:T(8,128)S(1)}, u32[]{:S(2)}, u32[]{:S(2)}) %collective-permute-start.15) | collective-permute-done | bytes 385056 | tf_op jit(solution)/shard_map/ppermute | solution.py:323
  55.1 0.0 collective-permute-done.16
  55.2 0.1 broadcast_select_fusion.3
  55.3 0.1 pad_maximum_fusion.refs_0_
  55.3 0.3 collective-permute-start.18
  55.6 1.5 %collective-permute-start.17 = (f32[752,128]{1,0:T(8,128)S(1)}, f32[752,128]{1,0:T(8,128)S(1)}, u32[]{:S(2)}, u32[]{:S(2)}) collective-permute-start(f32[752,128]{1,0:T(8,128)S(1)} %add.55), channel_id=1, source_target_pairs={{0,8},{4,20},{8,0},{12,28},{16,24},{20,4},{24,16},{28,12},{1,9},{5... | collective-permute-start | bytes 1155080 | tf_op jit(solution)/shard_map/ppermute | solution.py:323
  57.1 2.9 %finish.1 = (bf16[256,256]{1,0:T(8,128)(2,1)S(1)}, bf16[256,256]{1,0:T(8,128)(2,1)S(1)}, bf16[256,768]{1,0:T(8,128)(2,1)S(1)}, bf16[256,768]{1,0:T(8,128)(2,1)S(1)}) custom-call(f32[192,256]{1,0:T(8,128)S(1)} %get-tuple-element.98.x_ref, f32[64,64]{1,0:T(8,128)S(1)} %get-tuple-element.99.s_ref, f32[64,256]{1,0:T(8,128)S(1)} %get-tuple-element.100.r_ref, ...), custom_call_target="tpu_custom_call" | custom-call | tf_op jit(solution)/shard_map/finish/pallas_call | solution.py:229
  60.0 0.0 collective-permute-done.18.refs_1_
  60.0 5.0 %update.3 = (f32[3008,256]{1,0:T(8,128)}, f32[3008,768]{1,0:T(8,128)}) custom-call(s32[7]{0:T(128)S(1)} %get-tuple-element.65.at_ref, bf16[256,256]{1,0:T(8,128)(2,1)S(1)} %get-tuple-element.108.lh_ref, bf16[256,256]{1,0:T(8,128)(2,1)S(1)} %get-tuple-element.109.ll_ref, bf16[256,768]{1,0:T(8,128)(2,1)S(1)} %get-tuple-element.110.qh_ref, ...), custom_call_target="tpu_custom_call" | custom-call | tf_op jit(solution)/shard_map/update/pallas_call | solution.py:302
  65.0 0.0 collective-permute-done.17
  65.0 0.1 broadcast_select_fusion.1
  65.1 0.1 pad_maximum_fusion.1.refs_0_
  65.2 0.2 collective-permute-start.19
  65.3 2.5 %update.4 = (f32[752,256]{1,0:T(8,128)S(1)}, f32[752,768]{1,0:T(8,128)S(1)}) custom-call(s32[7]{0:T(128)S(1)} %get-tuple-element.65.at_ref, bf16[256,256]{1,0:T(8,128)(2,1)S(1)} %get-tuple-element.108.lh_ref, bf16[256,256]{1,0:T(8,128)(2,1)S(1)} %get-tuple-element.109.ll_ref, bf16[256,768]{1,0:T(8,128)(2,1)S(1)} %get-tuple-element.110.qh_ref, ...), custom_call_target="tpu_custom_call" | custom-call | tf_op jit(solution)/shard_map/update/pallas_call | solution.py:302
  67.9 0.0 collective-permute-done.19.refs_0_
  67.9 3.5 %update.5 = (f32[3008,256]{1,0:T(8,128)}, f32[3008,768]{1,0:T(8,128)}) custom-call(s32[7]{0:T(128)S(1)} %get-tuple-element.65.at_ref, bf16[256,256]{1,0:T(8,128)(2,1)S(1)} %get-tuple-element.108.lh_ref, bf16[256,256]{1,0:T(8,128)(2,1)S(1)} %get-tuple-element.109.ll_ref, ...), custom_call_target="tpu_custom_call", output_to_operand_aliasing={{0}: (9, {}), {1}: (10, {})} | custom-call | tf_op jit(solution)/shard_map/update/pallas_call | solution.py:302
  (15 shorter events, 0.3 us)
Async XLA Ops:
  0.8 13.5 %collective-permute-start = (f32[64,768]{1,0:T(8,128)}, f32[64,768]{1,0:T(8,128)S(1)}, u32[]{:S(2)}, u32[]{:S(2)}) collective-permute-start(f32[64,768]{1,0:T(8,128)} %bitcast.24), channel_id=1, source_target_pairs={{0,2},{1,3},{2,0},{3,1},{4,6},{5,7},{6,4},{7,5},{8,10},{9,11},{10,... | collective-permute-start | bytes 589832 | tf_op jit(solution)/shard_map/ppermute | solution.py:397
  4.9 10.2 %collective-permute-start.1 = (f32[64,768]{1,0:T(8,128)}, f32[64,768]{1,0:T(8,128)S(1)}, u32[]{:S(2)}, u32[]{:S(2)}) collective-permute-start(f32[64,768]{1,0:T(8,128)} %bitcast.25), channel_id=1, source_target_pairs={{0,1},{1,0},{2,3},{3,2},{4,5},{5,4},{6,7},{7,6},{8,9},{9,8},{10,11... | collective-permute-start | bytes 589832 | tf_op jit(solution)/shard_map/ppermute | solution.py:397
  6.5 3.6 %copy-start = (f32[768,3008]{0,1:T(8,128)S(1)}, f32[768,3008]{0,1:T(8,128)}, u32[]{:S(2)}) copy-start(f32[768,3008]{0,1:T(8,128)} %param.3) | copy-start | bytes 27721732
  10.1 0.9 %copy-start.2 = (f32[768,64]{0,1:T(8,128)S(1)}, f32[768,64]{0,1:T(8,128)}, u32[]{:S(2)}) copy-start(f32[768,64]{0,1:T(8,128)} %param.2) | copy-start | bytes 589828
  11.0 4.1 %copy-start.1 = (f32[768,3008]{0,1:T(8,128)S(1)}, f32[768,3008]{0,1:T(8,128)}, u32[]{:S(2)}) copy-start(f32[768,3008]{0,1:T(8,128)} %param.3) | copy-start | bytes 27721732
  14.3 6.1 %collective-permute-start.2 = (f32[64,768]{1,0:T(8,128)S(1)}, f32[64,768]{1,0:T(8,128)S(1)}, u32[]{:S(2)}, u32[]{:S(2)}) collective-permute-start(f32[64,768]{1,0:T(8,128)S(1)} %add.42.far.pa_ref), channel_id=1, source_target_pairs={{0,1},{1,0},{2,3},{3,2},{4,5},{5,4},{6,7},{7,6},{8,9},{9,8},{10,11... | collective-permute-start | bytes 589832 | tf_op jit(solution)/shard_map/ppermute | solution.py:397
  18.4 2.1 %collective-permute-start.4 = (f32[376,128]{1,0:T(8,128)S(1)}, f32[376,128]{1,0:T(8,128)S(1)}, u32[]{:S(2)}, u32[]{:S(2)}) collective-permute-start(f32[376,128]{1,0:T(8,128)S(1)} %get-tuple-element.74), channel_id=1, source_target_pairs={{0,4},{4,0},{8,12},{12,8},{16,20},{20,16},{24,28},{28,24},{1,5},{5... | collective-permute-start | bytes 577544 | tf_op jit(solution)/shard_map/ppermute | solution.py:323
  18.4 2.0 %collective-permute-start.5 = (f32[376,128]{1,0:T(8,128)S(1)}, f32[376,128]{1,0:T(8,128)S(1)}, u32[]{:S(2)}, u32[]{:S(2)}) collective-permute-start(f32[376,128]{1,0:T(8,128)S(1)} %get-tuple-element.75), channel_id=1, source_target_pairs={{0,4},{4,0},{8,12},{12,8},{16,20},{20,16},{24,28},{28,24},{1,5},{5... | collective-permute-start | bytes 577544 | tf_op jit(solution)/shard_map/ppermute | solution.py:323
  18.9 1.5 %collective-permute-start.6 = (f32[376,128]{1,0:T(8,128)S(1)}, f32[376,128]{1,0:T(8,128)S(1)}, u32[]{:S(2)}, u32[]{:S(2)}) collective-permute-start(f32[376,128]{1,0:T(8,128)S(1)} %get-tuple-element.76), channel_id=1, source_target_pairs={{0,4},{4,0},{8,12},{12,8},{16,20},{20,16},{24,28},{28,24},{1,5},{5... | collective-permute-start | bytes 577544 | tf_op jit(solution)/shard_map/ppermute | solution.py:323
  19.0 1.7 %collective-permute-start.3 = (f32[376,128]{1,0:T(8,128)S(1)}, f32[376,128]{1,0:T(8,128)S(1)}, u32[]{:S(2)}, u32[]{:S(2)}) collective-permute-start(f32[376,128]{1,0:T(8,128)S(1)} %get-tuple-element.72), channel_id=1, source_target_pairs={{0,4},{4,0},{8,12},{12,8},{16,20},{20,16},{24,28},{28,24},{1,5},{5... | collective-permute-start | bytes 577544 | tf_op jit(solution)/shard_map/ppermute | solution.py:323
  20.9 7.8 %collective-permute-start.8 = (f32[752,128]{1,0:T(8,128)S(1)}, f32[752,128]{1,0:T(8,128)S(1)}, u32[]{:S(2)}, u32[]{:S(2)}) collective-permute-start(f32[752,128]{1,0:T(8,128)S(1)} %pad_maximum_fusion.2), channel_id=1, source_target_pairs={{0,8},{4,20},{8,0},{12,28},{16,24},{20,4},{24,16},{28,12},{1,9},{5... | collective-permute-start | bytes 1155080 | tf_op jit(solution)/shard_map/ppermute | solution.py:323
  23.9 2.1 %collective-permute-start.7 = (f32[128,256]{1,0:T(8,128)S(1)}, f32[128,256]{1,0:T(8,128)S(1)}, u32[]{:S(2)}, u32[]{:S(2)}) collective-permute-start(f32[128,256]{1,0:T(8,128)S(1)} %get-tuple-element.79), channel_id=1, source_target_pairs={{0,4},{4,0},{8,12},{12,8},{16,20},{20,16},{24,28},{28,24},{1,5},{5... | collective-permute-start | bytes 393224 | tf_op jit(solution)/shard_map/ppermute | solution.py:323
  28.7 5.9 %collective-permute-start.10 = (f32[1504,128]{1,0:T(8,128)S(1)}, f32[1504,128]{1,0:T(8,128)S(1)}, u32[]{:S(2)}, u32[]{:S(2)}) collective-permute-start(f32[1504,128]{1,0:T(8,128)S(1)} %cross.4), channel_id=1, source_target_pairs={{0,4},{4,0},{8,12},{12,8},{16,20},{20,16},{24,28},{28,24},{1,5},{5... | collective-permute-start | bytes 2310152 | tf_op jit(solution)/shard_map/ppermute | solution.py:323
  28.8 5.8 %collective-permute-start.9 = (f32[128,256]{1,0:T(8,128)S(1)}, f32[128,256]{1,0:T(8,128)S(1)}, u32[]{:S(2)}, u32[]{:S(2)}) collective-permute-start(f32[128,256]{1,0:T(8,128)S(1)} %add.47), channel_id=1, source_target_pairs={{0,8},{4,20},{8,0},{12,28},{16,24},{20,4},{24,16},{28,12},{1,9},{5... | collective-permute-start | bytes 393224 | tf_op jit(solution)/shard_map/ppermute | solution.py:323
  30.3 9.1 %collective-permute-start.11 = (f32[752,128]{1,0:T(8,128)S(1)}, f32[752,128]{1,0:T(8,128)S(1)}, u32[]{:S(2)}, u32[]{:S(2)}) collective-permute-start(f32[752,128]{1,0:T(8,128)S(1)} %add.48), channel_id=1, source_target_pairs={{0,16},{4,12},{8,24},{12,4},{16,0},{20,28},{24,8},{28,20},{1,17},{... | collective-permute-start | bytes 1155080 | tf_op jit(solution)/shard_map/ppermute | solution.py:323
  34.7 8.8 %collective-permute-start.12 = (f32[752,128]{1,0:T(8,128)S(1)}, f32[752,128]{1,0:T(8,128)S(1)}, u32[]{:S(2)}, u32[]{:S(2)}) collective-permute-start(f32[752,128]{1,0:T(8,128)S(1)} %get-tuple-element.90), channel_id=1, source_target_pairs={{0,8},{4,20},{8,0},{12,28},{16,24},{20,4},{24,16},{28,12},{1,9},{5... | collective-permute-start | bytes 1155080 | tf_op jit(solution)/shard_map/ppermute | solution.py:323
  36.3 7.2 %collective-permute-start.13 = (f32[128,256]{1,0:T(8,128)S(1)}, f32[128,256]{1,0:T(8,128)S(1)}, u32[]{:S(2)}, u32[]{:S(2)}) collective-permute-start(f32[128,256]{1,0:T(8,128)S(1)} %add.49), channel_id=1, source_target_pairs={{0,16},{4,12},{8,24},{12,4},{16,0},{20,28},{24,8},{28,20},{1,17},{... | collective-permute-start | bytes 393224 | tf_op jit(solution)/shard_map/ppermute | solution.py:323
  43.5 2.8 %collective-permute-start.14 = (f32[128,256]{1,0:T(8,128)S(1)}, f32[128,256]{1,0:T(8,128)S(1)}, u32[]{:S(2)}, u32[]{:S(2)}) collective-permute-start(f32[128,256]{1,0:T(8,128)S(1)} %add.54), channel_id=1, source_target_pairs={{0,4},{4,0},{8,12},{12,8},{16,20},{20,16},{24,28},{28,24},{1,5},{5... | collective-permute-start | bytes 393224 | tf_op jit(solution)/shard_map/ppermute | solution.py:323
  43.7 11.4 %collective-permute-start.15 = (f32[752,128]{1,0:T(8,128)S(1)}, f32[752,128]{1,0:T(8,128)S(1)}, u32[]{:S(2)}, u32[]{:S(2)}) collective-permute-start(f32[752,128]{1,0:T(8,128)S(1)} %add.52), channel_id=1, source_target_pairs={{0,8},{4,20},{8,0},{12,28},{16,24},{20,4},{24,16},{28,12},{1,9},{5... | collective-permute-start | bytes 1155080 | tf_op jit(solution)/shard_map/ppermute | solution.py:323
  45.2 10.0 %collective-permute-start.16 = (f32[752,128]{1,0:T(8,128)S(1)}, f32[752,128]{1,0:T(8,128)S(1)}, u32[]{:S(2)}, u32[]{:S(2)}) collective-permute-start(f32[752,128]{1,0:T(8,128)S(1)} %add.53), channel_id=1, source_target_pairs={{0,16},{4,12},{8,24},{12,4},{16,0},{20,28},{24,8},{28,20},{1,17},{... | collective-permute-start | bytes 1155080 | tf_op jit(solution)/shard_map/ppermute | solution.py:323
  55.3 4.6 %collective-permute-start.18 = (f32[752,256]{1,0:T(8,128)S(1)}, f32[752,256]{1,0:T(8,128)S(1)}, u32[]{:S(2)}, u32[]{:S(2)}) collective-permute-start(f32[752,256]{1,0:T(8,128)S(1)} %pad_maximum_fusion.refs_0_), channel_id=1, source_target_pairs={{0,4},{4,0},{8,12},{12,8},{16,20},{20,16},{24,28},{28,24},{1,5},{5... | collective-permute-start | bytes 2310152 | tf_op jit(solution)/shard_map/ppermute | solution.py:323
  55.6 9.4 %collective-permute-start.17 = (f32[752,128]{1,0:T(8,128)S(1)}, f32[752,128]{1,0:T(8,128)S(1)}, u32[]{:S(2)}, u32[]{:S(2)}) collective-permute-start(f32[752,128]{1,0:T(8,128)S(1)} %add.55), channel_id=1, source_target_pairs={{0,8},{4,20},{8,0},{12,28},{16,24},{20,4},{24,16},{28,12},{1,9},{5... | collective-permute-start | bytes 1155080 | tf_op jit(solution)/shard_map/ppermute | solution.py:323
  65.2 2.7 %collective-permute-start.19 = (f32[752,256]{1,0:T(8,128)S(1)}, f32[752,256]{1,0:T(8,128)S(1)}, u32[]{:S(2)}, u32[]{:S(2)}) collective-permute-start(f32[752,256]{1,0:T(8,128)S(1)} %pad_maximum_fusion.1.refs_0_), channel_id=1, source_target_pairs={{0,4},{4,0},{8,12},{12,8},{16,20},{20,16},{24,28},{28,24},{1,5},{5... | collective-permute-start | bytes 2310152 | tf_op jit(solution)/shard_map/ppermute | solution.py:323
